TPU v7x, 32 devices: a whole 2x2x4 slice. The times are simulated.
32 devices in a mesh: expert: 8 (over y, x, core), tensor: 4 (over z).
Axes of the slice: x: 2, y: 2, z: 4, core: 2. Of those that a mesh axis runs over, the one named last changes fastest.
Arguments:
- tokens: bfloat16 [8192, 2048], P('expert'), may hold values from -6 to 6
- cotangent: bfloat16 [8192, 2048], P('expert'), may hold values from -6 to 6
- seq_lengths: int32 [32], P('expert'), may hold values from 0 to 1024, as said below
- expert_ids: int32 [8192, 8], P('expert'), may hold values from 0 to 15, as said below
- slot_index: int32 [8192, 8], P('expert'), may hold values from -1 to 383, as said below
- w_query: bfloat16 [2048, 2048], P(None, 'tensor'), may hold values from -0.125 to 0.125
- w_key: bfloat16 [2048, 2048], P(None, 'tensor'), may hold values from -0.125 to 0.125
- w_value: bfloat16 [2048, 2048], P(None, 'tensor'), may hold values from -0.125 to 0.125
- w_output: bfloat16 [2048, 2048], P('tensor'), may hold values from -0.75 to 0.75
- query_gain: float32 [2048], P('tensor'), may hold values from 0.5 to 1.5
- key_gain: float32 [2048], P('tensor'), may hold values from 0.5 to 1.5
- attn_gain: float32 [2048], replicated, may hold values from 0.5 to 1.5
- moe_gain: float32 [2048], replicated, may hold values from 0.5 to 1.5
- router: bfloat16 [2048, 16], replicated, may hold values from -0.06591797 to 0.06591797
- w_gate: bfloat16 [16, 2048, 1024], P('expert', None, 'tensor'), may hold values from -0.125 to 0.125
- w_up: bfloat16 [16, 2048, 1024], P('expert', None, 'tensor'), may hold values from -0.125 to 0.125
- w_down: bfloat16 [16, 1024, 2048], P('expert', 'tensor'), may hold values from -12 to 12
Outputs:
- out: bfloat16 [8192, 2048], P('expert')
- grad_input: bfloat16 [8192, 2048], P('expert')
- grad_w_query: bfloat16 [2048, 2048], P('expert', 'tensor')
- grad_w_key: bfloat16 [2048, 2048], P('expert', 'tensor')
- grad_w_value: bfloat16 [2048, 2048], P('expert', 'tensor')
- grad_w_output: bfloat16 [2048, 2048], P('tensor', 'expert')
- grad_query_gain: bfloat16 [2048], P(('tensor', 'expert'))
- grad_key_gain: bfloat16 [2048], P(('tensor', 'expert'))
- grad_attn_gain: bfloat16 [2048], P('expert')
- grad_moe_gain: bfloat16 [2048], P('expert')
- grad_router: bfloat16 [2048, 16], P('expert')
- grad_w_gate: bfloat16 [16, 2048, 1024], P('expert', None, 'tensor')
- grad_w_up: bfloat16 [16, 2048, 1024], P('expert', None, 'tensor')
- grad_w_down: bfloat16 [16, 1024, 2048], P('expert', 'tensor')
Inputs may be any that keep to these rules, and one draw needn't show every extreme that they name: `seq_lengths`: each group's 4 lengths fill its first rows in order and sum to 512 or more; some group holds a single sequence of 1024 rows. `expert_ids`: the 8 experts of a token differ. `slot_index`: -1 marks a choice that is not carried (every choice of a padding row, and some others). The carried choices of one group that name one expert hold distinct slots. One expert receives 384 rows from every group.
All inputs are finite; a program needn't handle non-finite values.
Results may differ from a plain program's by a relative error of at most 0.03.
Values may be sent and summed in bfloat16 or wider, within the bound.
No kernel may reach another device: no remote copies, remote signals or barrier semaphores. Data moves between devices by JAX's collectives and lax.ppermute only.
A program may use at most 384 MiB of HBM per device.

v0:
```python
import jax
import jax.numpy as jnp
from jax import lax
from jax.sharding import PartitionSpec as P

HEAD_DIM = 128
TOP = 8


EPS = 1e-05
THETA = 10000.0
NEG = -1e30


def norm_rows(values, gain):
    inverse = lax.rsqrt(jnp.mean(values * values, axis=-1, keepdims=True) + EPS)
    return (values * inverse * gain, inverse)


def norm_back(values, inverse, gain, upstream):
    scaled = upstream * gain
    inner = jnp.mean(values * scaled, axis=-1, keepdims=True)
    grad_values = inverse * scaled - values * inverse * inverse * inverse * inner
    grad_gain = jnp.sum(upstream * values * inverse, axis=0)
    return (grad_values, grad_gain)


def layout(lengths, rows):
    ends = jnp.cumsum(lengths, axis=-1)
    starts = ends - lengths
    places = jnp.arange(rows, dtype=jnp.int32)
    inside = (
        (places[..., :, None] >= starts[..., None, :]) & (places[..., :, None] < ends[..., None, :])
    ).astype(jnp.int32)
    number = jnp.arange(lengths.shape[-1], dtype=jnp.int32)
    alive = jnp.sum(inside, axis=-1)
    segment = jnp.sum(inside * number, axis=-1) + (1 - alive) * (lengths.shape[-1] + places)
    position = jnp.sum(inside * (places[..., :, None] - starts[..., None, :]), axis=-1)
    return (segment, position)


def rope_angles(position, head_size):
    half = head_size // 2
    freq = THETA ** (-2.0 * jnp.arange(half, dtype=jnp.float32) / head_size)
    angle = position.astype(jnp.float32)[..., None] * freq
    return (jnp.cos(angle), jnp.sin(angle))


def rotate(values, cosine, sine):
    half = values.shape[-1] // 2
    first, second = (values[..., :half], values[..., half:])
    cos_here = cosine[..., None, :]
    sin_here = sine[..., None, :]
    return jnp.concatenate(
        [first * cos_here - second * sin_here, second * cos_here + first * sin_here], axis=-1
    )


def unrotate(grads, cosine, sine):
    half = grads.shape[-1] // 2
    first, second = (grads[..., :half], grads[..., half:])
    cos_here = cosine[..., None, :]
    sin_here = sine[..., None, :]
    return jnp.concatenate(
        [first * cos_here + second * sin_here, second * cos_here - first * sin_here], axis=-1
    )


def block_scores(query_block, keys, seg_block, segment, start):
    scores = jnp.einsum(
        "qhd,khd->hqk", query_block, keys, preferred_element_type=jnp.float32
    ) * HEAD_DIM ** (-0.5)
    rows_query = start + jnp.arange(query_block.shape[0], dtype=jnp.int32)
    rows_key = jnp.arange(keys.shape[0], dtype=jnp.int32)
    allowed = (seg_block[:, None] == segment[None, :]) & (rows_key[None, :] <= rows_query[:, None])
    return jnp.where(allowed[None], scores, NEG)


def attention_forward(queries, keys, values, segment, block):
    rows = queries.shape[0]

    def one_block(index):
        start = index * block
        query_block = lax.dynamic_slice_in_dim(queries, start, block, 0)
        seg_block = lax.dynamic_slice_in_dim(segment, start, block, 0)
        scores = block_scores(query_block, keys, seg_block, segment, start)
        top = jnp.max(scores, axis=-1, keepdims=True)
        raised = jnp.exp(scores - top)
        total = jnp.sum(raised, axis=-1, keepdims=True)
        weights = (raised / total).astype(jnp.bfloat16)
        context = jnp.einsum("hqk,khd->qhd", weights, values, preferred_element_type=jnp.float32)
        return (context, top, total)

    context, top, total = lax.map(one_block, jnp.arange(rows // block, dtype=jnp.int32))
    return (context.reshape(queries.shape), top, total)


def attention_backward(queries, keys, values, segment, block, top, total, grad_context):
    rows = queries.shape[0]
    scale = HEAD_DIM ** (-0.5)

    def one_block(carry, index):
        grad_keys, grad_values = carry
        start = index * block
        query_block = lax.dynamic_slice_in_dim(queries, start, block, 0)
        seg_block = lax.dynamic_slice_in_dim(segment, start, block, 0)
        grad_block = lax.dynamic_slice_in_dim(grad_context, start, block, 0)
        scores = block_scores(query_block, keys, seg_block, segment, start)
        weights_f = jnp.exp(scores - top[index]) / total[index]
        weights = weights_f.astype(jnp.bfloat16)
        grad_weights = jnp.einsum(
            "qhd,khd->hqk", grad_block, values, preferred_element_type=jnp.float32
        )
        inner = jnp.sum(weights_f * grad_weights, axis=-1, keepdims=True)
        grad_scores = (weights_f * (grad_weights - inner)).astype(jnp.bfloat16)
        grad_query = (
            jnp.einsum("hqk,khd->qhd", grad_scores, keys, preferred_element_type=jnp.float32)
            * scale
        )
        grad_keys = (
            grad_keys
            + jnp.einsum(
                "hqk,qhd->khd", grad_scores, query_block, preferred_element_type=jnp.float32
            )
            * scale
        )
        grad_values = grad_values + jnp.einsum(
            "hqk,qhd->khd", weights, grad_block, preferred_element_type=jnp.float32
        )
        return ((grad_keys, grad_values), grad_query)

    empty = jnp.zeros(keys.shape, jnp.float32)
    (grad_keys, grad_values), grad_query = lax.scan(
        one_block, (empty, empty), jnp.arange(rows // block, dtype=jnp.int32)
    )
    return (grad_query.reshape(queries.shape), grad_keys, grad_values)


def shards(
    tokens,
    cotangent,
    seq_lengths,
    expert_ids,
    slot_index,
    w_query,
    w_key,
    w_value,
    w_output,
    query_gain,
    key_gain,
    attn_gain,
    moe_gain,
    router,
    w_gate,
    w_up,
    w_down,
):
    rows, width = tokens.shape
    local = w_query.shape[1]
    heads_here = local // HEAD_DIM
    groups = lax.axis_size("expert")
    experts_here = w_gate.shape[0]
    experts_all = experts_here * groups
    capacity = max(2, 3 * rows * TOP // (4 * experts_all))
    block = min(512, rows)
    shape_heads = (rows, heads_here, HEAD_DIM)
    segment, position = layout(seq_lengths, rows)
    cosine, sine = rope_angles(position, HEAD_DIM)
    inputs = tokens.astype(jnp.float32)
    normed, inverse_in = norm_rows(inputs, attn_gain)
    attn_in = normed.astype(jnp.bfloat16)
    query_raw = jnp.dot(attn_in, w_query, preferred_element_type=jnp.float32)
    key_raw = jnp.dot(attn_in, w_key, preferred_element_type=jnp.float32)
    value_raw = jnp.dot(attn_in, w_value, preferred_element_type=jnp.float32)
    query_total, key_total = lax.psum(
        (jnp.sum(query_raw * query_raw, axis=-1), jnp.sum(key_raw * key_raw, axis=-1)), "tensor"
    )
    query_inverse = lax.rsqrt(query_total / width + EPS)[:, None]
    key_inverse = lax.rsqrt(key_total / width + EPS)[:, None]
    queries = rotate(
        (query_raw * query_inverse * query_gain).reshape(shape_heads), cosine, sine
    ).astype(jnp.bfloat16)
    keys = rotate((key_raw * key_inverse * key_gain).reshape(shape_heads), cosine, sine).astype(
        jnp.bfloat16
    )
    values = value_raw.reshape(shape_heads).astype(jnp.bfloat16)
    context, top, total = attention_forward(queries, keys, values, segment, block)
    context_low = context.reshape(rows, local).astype(jnp.bfloat16)
    attn = lax.psum(
        jnp.dot(context_low, w_output, preferred_element_type=jnp.float32).astype(jnp.bfloat16),
        "tensor",
    ).astype(jnp.float32)
    hidden_in = inputs + attn
    moe_in, inverse_moe = norm_rows(hidden_in, moe_gain)
    router_wide = router.astype(jnp.float32)
    shares = jax.nn.softmax(jnp.dot(moe_in, router_wide, precision=lax.Precision.HIGHEST), axis=-1)
    chosen = expert_ids[:, :, None] == jnp.arange(experts_all, dtype=jnp.int32)[None, None, :]
    gates = jnp.sum(jnp.where(chosen, shares[:, None, :], 0.0), axis=-1)
    kept = slot_index >= 0
    target_slot = jnp.where(
        kept, expert_ids * capacity + slot_index, experts_all * capacity
    ).reshape(-1)
    token_of = (
        jnp.full((experts_all * capacity,), -1, jnp.int32)
        .at[target_slot]
        .set(jnp.repeat(jnp.arange(rows, dtype=jnp.int32), TOP), mode="drop")
    )
    gate_of = (
        jnp.zeros((experts_all * capacity,), jnp.float32)
        .at[target_slot]
        .set(gates.reshape(-1), mode="drop")
    )
    filled = (token_of >= 0)[:, None]
    source_row = jnp.maximum(token_of, 0)
    moe_low = moe_in.astype(jnp.bfloat16)
    send_rows = jnp.where(filled, moe_low[source_row], jnp.zeros((), jnp.bfloat16)).reshape(
        groups, experts_here * capacity, width
    )
    arrived = lax.all_to_all(send_rows, "expert", split_axis=0, concat_axis=0, tiled=True)
    arrived = arrived.reshape(groups, experts_here, capacity, width)
    gate_pre = jnp.einsum("secd,edf->secf", arrived, w_gate, preferred_element_type=jnp.float32)
    up_pre = jnp.einsum("secd,edf->secf", arrived, w_up, preferred_element_type=jnp.float32)
    activated = jax.nn.silu(gate_pre)
    hidden = (activated * up_pre).astype(jnp.bfloat16)
    partial_value = jnp.einsum(
        "secf,efd->secd", hidden, w_down, preferred_element_type=jnp.float32
    ).astype(jnp.bfloat16)
    dy_rows = jnp.where(filled, cotangent[source_row], jnp.zeros((), jnp.bfloat16))
    returned = lax.all_to_all(partial_value, "expert", split_axis=0, concat_axis=0, tiled=True)
    returned = returned.reshape(experts_all * capacity, width).astype(jnp.float32)
    moe_part = jax.ops.segment_sum(returned * gate_of[:, None], source_row, num_segments=rows)
    moe = lax.psum(moe_part.astype(jnp.bfloat16), "tensor").astype(jnp.float32)
    row_dots = jnp.sum(dy_rows.astype(jnp.float32) * returned, axis=-1)
    out = (hidden_in + moe).astype(jnp.bfloat16)
    grad_gate = jnp.take(row_dots, target_slot, mode="fill", fill_value=0.0).reshape(rows, TOP)
    grad_shares = jnp.sum(jnp.where(chosen, grad_gate[:, :, None], 0.0), axis=1)
    grad_logits = shares * (grad_shares - jnp.sum(shares * grad_shares, axis=-1, keepdims=True))
    router_back = jnp.einsum("te,de->td", grad_logits, router_wide, precision=lax.Precision.HIGHEST)
    router_part = jnp.einsum("td,te->de", moe_in, grad_logits, precision=lax.Precision.HIGHEST)
    grad_rows = (
        (dy_rows.astype(jnp.float32) * gate_of[:, None])
        .astype(jnp.bfloat16)
        .reshape(groups, experts_here * capacity, width)
    )
    grad_arrived = lax.all_to_all(grad_rows, "expert", split_axis=0, concat_axis=0, tiled=True)
    grad_arrived = grad_arrived.reshape(groups, experts_here, capacity, width)
    grad_hidden = jnp.einsum(
        "secd,efd->secf", grad_arrived, w_down, preferred_element_type=jnp.float32
    )
    grad_w_down = jnp.einsum(
        "secf,secd->efd", hidden, grad_arrived, preferred_element_type=jnp.float32
    )
    sigma = jax.nn.sigmoid(gate_pre)
    grad_gate_pre = (grad_hidden * up_pre * sigma * (1.0 + gate_pre * (1.0 - sigma))).astype(
        jnp.bfloat16
    )
    grad_up_pre = (grad_hidden * activated).astype(jnp.bfloat16)
    grad_w_gate = jnp.einsum(
        "secd,secf->edf", arrived, grad_gate_pre, preferred_element_type=jnp.float32
    )
    grad_w_up = jnp.einsum(
        "secd,secf->edf", arrived, grad_up_pre, preferred_element_type=jnp.float32
    )
    grad_in_rows = jnp.einsum(
        "secf,edf->secd", grad_gate_pre, w_gate, preferred_element_type=jnp.float32
    )
    grad_in_rows = (
        grad_in_rows
        + jnp.einsum("secf,edf->secd", grad_up_pre, w_up, preferred_element_type=jnp.float32)
    ).astype(jnp.bfloat16)
    back_rows = lax.all_to_all(
        grad_in_rows.reshape(groups, experts_here * capacity, width),
        "expert",
        split_axis=0,
        concat_axis=0,
        tiled=True,
    )
    back_rows = back_rows.reshape(experts_all * capacity, width).astype(jnp.float32)
    moe_back = jax.ops.segment_sum(back_rows, source_row, num_segments=rows)
    grad_moe_in, grad_router_rows = (
        lax.psum((moe_back + router_back).astype(jnp.bfloat16), "tensor").astype(jnp.float32),
        lax.psum(router_part.astype(jnp.bfloat16), "tensor").astype(jnp.float32),
    )
    grad_norm_moe, grad_moe_gain = norm_back(hidden_in, inverse_moe, moe_gain, grad_moe_in)
    grad_hidden_in = cotangent.astype(jnp.float32) + grad_norm_moe
    grad_low = grad_hidden_in.astype(jnp.bfloat16)
    grad_w_output = jnp.einsum(
        "tf,td->fd", context_low, grad_low, preferred_element_type=jnp.float32
    )
    grad_context = (
        jnp.einsum("td,fd->tf", grad_low, w_output, preferred_element_type=jnp.float32)
        .astype(jnp.bfloat16)
        .reshape(shape_heads)
    )
    grad_queries, grad_keys, grad_values = attention_backward(
        queries, keys, values, segment, block, top, total, grad_context
    )
    grad_query_normed = unrotate(grad_queries, cosine, sine).reshape(rows, local)
    grad_key_normed = unrotate(grad_keys, cosine, sine).reshape(rows, local)
    query_scaled = grad_query_normed * query_gain
    key_scaled = grad_key_normed * key_gain
    query_inner, key_inner = lax.psum(
        (jnp.sum(query_raw * query_scaled, axis=-1), jnp.sum(key_raw * key_scaled, axis=-1)),
        "tensor",
    )
    grad_query_raw = (
        query_inverse * query_scaled
        - query_raw * query_inverse * query_inverse * query_inverse * (query_inner / width)[:, None]
    )
    grad_key_raw = (
        key_inverse * key_scaled
        - key_raw * key_inverse * key_inverse * key_inverse * (key_inner / width)[:, None]
    )
    grad_query_gain = jnp.sum(grad_query_normed * query_raw * query_inverse, axis=0)
    grad_key_gain = jnp.sum(grad_key_normed * key_raw * key_inverse, axis=0)
    query_low = grad_query_raw.astype(jnp.bfloat16)
    key_low = grad_key_raw.astype(jnp.bfloat16)
    value_low = grad_values.reshape(rows, local).astype(jnp.bfloat16)
    grad_w_query = jnp.einsum("td,tf->df", attn_in, query_low, preferred_element_type=jnp.float32)
    grad_w_key = jnp.einsum("td,tf->df", attn_in, key_low, preferred_element_type=jnp.float32)
    grad_w_value = jnp.einsum("td,tf->df", attn_in, value_low, preferred_element_type=jnp.float32)
    terms_in = jnp.einsum("tf,df->td", query_low, w_query, preferred_element_type=jnp.float32)
    terms_in = terms_in + jnp.einsum(
        "tf,df->td", key_low, w_key, preferred_element_type=jnp.float32
    )
    terms_in = terms_in + jnp.einsum(
        "tf,df->td", value_low, w_value, preferred_element_type=jnp.float32
    )
    grad_normed = lax.psum(terms_in.astype(jnp.bfloat16), "tensor").astype(jnp.float32)
    grad_norm_in, grad_attn_gain = norm_back(inputs, inverse_in, attn_gain, grad_normed)
    grad_input = (grad_hidden_in + grad_norm_in).astype(jnp.bfloat16)
    sums = (
        lax.psum_scatter(
            grad_w_query.astype(jnp.bfloat16), "expert", scatter_dimension=0, tiled=True
        ).astype(jnp.float32),
        lax.psum_scatter(
            grad_w_key.astype(jnp.bfloat16), "expert", scatter_dimension=0, tiled=True
        ).astype(jnp.float32),
        lax.psum_scatter(
            grad_w_value.astype(jnp.bfloat16), "expert", scatter_dimension=0, tiled=True
        ).astype(jnp.float32),
        lax.psum_scatter(
            grad_w_output.astype(jnp.bfloat16), "expert", scatter_dimension=1, tiled=True
        ).astype(jnp.float32),
        lax.psum_scatter(
            grad_query_gain.astype(jnp.bfloat16), "expert", scatter_dimension=0, tiled=True
        ).astype(jnp.float32),
        lax.psum_scatter(
            grad_key_gain.astype(jnp.bfloat16), "expert", scatter_dimension=0, tiled=True
        ).astype(jnp.float32),
        lax.psum_scatter(
            grad_attn_gain.astype(jnp.bfloat16), "expert", scatter_dimension=0, tiled=True
        ).astype(jnp.float32),
        lax.psum_scatter(
            grad_moe_gain.astype(jnp.bfloat16), "expert", scatter_dimension=0, tiled=True
        ).astype(jnp.float32),
        lax.psum_scatter(
            grad_router_rows.astype(jnp.bfloat16), "expert", scatter_dimension=0, tiled=True
        ).astype(jnp.float32),
    )
    lows = tuple((item.astype(jnp.bfloat16) for item in sums))
    return (
        out,
        grad_input,
        lows[0],
        lows[1],
        lows[2],
        lows[3],
        lows[4],
        lows[5],
        lows[6],
        lows[7],
        lows[8],
        grad_w_gate.astype(jnp.bfloat16),
        grad_w_up.astype(jnp.bfloat16),
        grad_w_down.astype(jnp.bfloat16),
    )


def solution(mesh):
    placed = (
        P("expert", None),
        P("expert", None),
        P("expert"),
        P("expert", None),
        P("expert", None),
        P(None, "tensor"),
        P(None, "tensor"),
        P(None, "tensor"),
        P("tensor", None),
        P("tensor"),
        P("tensor"),
        P(),
        P(),
        P(),
        P("expert", None, "tensor"),
        P("expert", None, "tensor"),
        P("expert", "tensor", None),
    )
    return jax.shard_map(
        shards,
        mesh=mesh,
        in_specs=placed,
        out_specs=(
            P("expert", None),
            P("expert", None),
            P("expert", "tensor"),
            P("expert", "tensor"),
            P("expert", "tensor"),
            P("tensor", "expert"),
            P(("tensor", "expert")),
            P(("tensor", "expert")),
            P("expert"),
            P("expert"),
            P("expert", None),
            P("expert", None, "tensor"),
            P("expert", None, "tensor"),
            P("expert", "tensor", None),
        ),
        check_vma=False,
    )
```

profile of v0, /device:TPU:20, one launch (start us, length us, event | category | flops | bytes accessed | tf_op | source)
XLA Modules:
  0.0 2541.0 jit_solution(791192991260033545)
XLA Ops:
  12.5 5.1 convolution_convert_fusion.5
  19.2 6.8 multiply_reduce_fusion.5
  26.1 4.0 multiply_reduce_fusion.6
  30.0 9.6 all-reduce.5
  60.8 5.0 subtract_convert_fusion.2
  68.9 23.7 while.29
  96.1 5.9 convolution_convert_fusion
  103.7 30.5 %scatter_custom_fusion = s32[6144]{0:T(1024)S(1)} fusion(s32[8192]{0:T(1024)S(1)} %bitcast.232, s32[8192]{0:T(1024)S(1)} %reshape.416, s32[]{:T(128)} %constant.72.clone.1), kind=kCustom, calls=%fused_computation.204 | custom fusion | bytes 24580 | tf_op jit(solution)/shard_map/scatter | solution.py:206
  135.5 121.9 %all-reduce.12.cloned.1.call-done = bf16[1024,2048]{1,0:T(8,128)(2,1)} async-done(((bf16[1024,2048]{1,0:T(8,128)(2,1)}), bf16[1024,2048]{1,0:T(8,128)(2,1)}) %all-reduce.12.cloned.1.call-update) | async-done | bytes 4194320 | tf_op jit(solution)/shard_map/psum | solution.py:189
  257.4 5.0 multiply_reduce_fusion.2
  263.3 4.0 fusion.60
  267.3 49.1 %gather_fusion = bf16[6144,2048]{1,0:T(8,128)(2,1)} fusion(bf16[1024,2048]{1,0:T(8,128)(2,1)} %fusion.60, s32[6144]{0:T(1024)S(1)} %get-tuple-element.391), kind=kCustom, calls=%fused_computation | custom fusion | bytes 50356224 | tf_op jit(solution)/shard_map/gather | solution.py:216
  316.4 12.3 broadcast_select_fusion
  328.7 277.3 %all_to_all.20 = bf16[8,768,2048]{2,1,0:T(8,128)(2,1)} all-to-all(bf16[8,768,2048]{2,1,0:T(8,128)(2,1)S(1)} %broadcast_select_fusion), channel_id=1, replica_groups=mesh['expert'=8,'tensor'=4] {'expert'}, dimensions={0} | all-to-all | bytes 50331648 | tf_op jit(solution)/shard_map/all_to_all | solution.py:219
  606.0 13.3 fusion.36
  619.4 16.6 fusion.65
  636.0 13.7 convert_bitcast_fusion
  649.7 21.1 copy.195
  670.8 8.3 all-to-all-start.1
  679.2 49.2 %gather_fusion.1 = bf16[6144,2048]{1,0:T(8,128)(2,1)} fusion(bf16[1024,2048]{1,0:T(8,128)(2,1)} %param.22, s32[6144]{0:T(1024)S(1)} %get-tuple-element.391), kind=kCustom, calls=%fused_computation.1 | custom fusion | bytes 50356224 | tf_op jit(solution)/shard_map/gather | solution.py:228
  728.5 8.6 fusion.120
  737.8 213.8 %all-to-all-done.1 = bf16[8,2,384,2048]{3,2,1,0:T(8,128)(2,1)} async-done(((bf16[8,2,384,2048]{3,2,1,0:T(8,128)(2,1)}), bf16[8,2,384,2048]{3,2,1,0:T(8,128)(2,1)}, u32[]{:S(2)}, u32[]{:S(2)}) %all-to-all-start.1) | async-done | bytes 25165856 | tf_op jit(solution)/shard_map/all_to_all | solution.py:229
  951.6 20.6 multiply_reduce_fusion.1
  972.2 45.5 %gather_fusion.2 = f32[8192]{0:T(1024)S(1)} fusion(f32[6144]{0:T(1024)S(1)} %reduce_sum.210, s32[8192]{0:T(1024)S(1)} %broadcast_clamp_fusion), kind=kCustom, calls=%fused_computation.2 | custom fusion | bytes 98304 | tf_op jit(solution)/shard_map/jit(_take)/gather | solution.py:235
  1018.9 30.5 %scatter_custom_fusion.1 = f32[6144]{0:T(1024)S(1)} fusion(s32[8192]{0:T(1024)S(1)} %bitcast.234, f32[8192]{0:T(1024)S(1)} %reshape.424, f32[]{:T(128)} %constant.59.clone.1), kind=kCustom, calls=%fused_computation.200 | custom fusion | bytes 24580 | tf_op jit(solution)/shard_map/scatter | solution.py:211
  1049.4 14.5 multiply_convert_fusion.1
  1063.9 278.1 %all_to_all.21 = bf16[8,768,2048]{2,1,0:T(8,128)(2,1)} all-to-all(bf16[8,768,2048]{2,1,0:T(8,128)(2,1)S(1)} %multiply_convert_fusion.1), channel_id=1, replica_groups=mesh['expert'=8,'tensor'=4] {'expert'}, dimensions={0} | all-to-all | bytes 50331648 | tf_op jit(solution)/shard_map/all_to_all | solution.py:245
  1342.0 18.3 fusion.64
  1360.2 21.7 fusion.87
  1381.9 26.7 %fusion.29 = bf16[8,2,384,2048]{3,2,0,1:T(8,128)(2,1)} fusion(f32[2,8,384,2048]{3,2,1,0:T(8,128)} %fusion.87, bf16[8,2,384,256]{3,2,0,1:T(8,128)(2,1)} %get-tuple-element.371, bf16[2,2048,256]{2,1,0:T(8,128)(2,1)S(1)} %copy-done.33), kind=kOutput, calls=%fused_computation.55 | convolution fusion | flops 6467616768 | bytes 80740352 | tf_op jit(solution)/shard_map/secf,edf->secd/dot_general | solution.py:269
  1408.6 21.0 copy.201
  1429.7 7.9 all-to-all-start.3
  1437.7 5.9 fusion.104
  1443.6 266.5 %all-to-all-done.3 = bf16[8,768,2048]{2,1,0:T(8,128)(2,1)} async-done(((bf16[8,768,2048]{2,1,0:T(8,128)(2,1)}), bf16[8,768,2048]{2,1,0:T(8,128)(2,1)}, u32[]{:S(2)}, u32[]{:S(2)}) %all-to-all-start.3) | async-done | bytes 25165856 | tf_op jit(solution)/shard_map/all_to_all | solution.py:271
  1710.1 86.1 %scatter_custom_fusion.3 = f32[1024,2048]{1,0:T(8,128)} fusion(f32[1024,2048]{1,0:T(8,128)} %fusion.104, s32[6144]{0:T(1024)} %get-tuple-element.392, bf16[6144,2048]{1,0:T(8,128)(2,1)} %bitcast.50), kind=kCustom, calls=%fused_computation.49 | custom fusion | flops 25165824 | bytes 33554432 | tf_op jit(solution)/shard_map/scatter-add | solution.py:279
  1796.1 6.0 convert_element_type.228
  1802.2 24.3 bitcast_multiply_fusion
  1826.6 80.9 %scatter_custom_fusion.2 = f32[1024,2048]{1,0:T(8,128)} fusion(s32[6144]{0:T(1024)} %get-tuple-element.392, f32[6144,2048]{1,0:T(8,128)} %bitcast_multiply_fusion, f32[]{:T(128)} %constant.59.clone.1), kind=kCustom, calls=%fused_computation.123 | custom fusion | flops 12582912 | bytes 8389120 | tf_op jit(solution)/shard_map/scatter-add | solution.py:231
  1907.5 6.4 convert_element_type.214
  1914.9 6.4 fusion.80
  1921.4 34.1 %all-reduce.14.cloned.1.call-done = bf16[1024,2048]{1,0:T(8,128)(2,1)} async-done(((bf16[1024,2048]{1,0:T(8,128)(2,1)}), bf16[1024,2048]{1,0:T(8,128)(2,1)}) %all-reduce.14.cloned.1.call-update) | async-done | bytes 4194320 | tf_op jit(solution)/shard_map/psum | solution.py:281
  1955.5 7.2 fusion.53
  1963.8 6.6 fusion.50
  1974.2 37.3 %while.30 = (s32[]{:T(128)}, f32[1024,4,128]{0,2,1:T(8,128)S(1)}, f32[1024,4,128]{0,2,1:T(8,128)}, f32[2,512,4,128]{3,1,0,2:T(8,128)}, s32[2]{0:T(128)S(1)}, /*i...) while((s32[]{:T(128)}, f32[1024,4,128]{0,2,1:T(8,128)S(1)}, ...), condition=%wide.region_30.31_spmd.clone, body=%wide.region_28.30_spmd.clone.sunk | while | flops 2709780992 | bytes 124860920 | solution.py:133
  1981.0 4.1 multiply_reduce_fusion.9
  1999.4 4.1 multiply_reduce_fusion.9
  2016.1 6.6 multiply_add_fusion
  2038.1 8.1 all-reduce.4
  2054.6 6.1 add_convert_fusion.1
  2061.9 7.1 convolution_convert_fusion.1
  2069.1 6.4 convolution_convert_fusion.2
  2077.6 12.2 psum.72
  2089.8 6.4 convolution_convert_fusion.3
  2096.7 16.5 bitcast_convert_fusion.1
  2113.2 13.7 bitcast_convert_fusion
  2126.9 6.6 convolution_convert_fusion.4
  2133.5 16.7 bitcast_convert_fusion.2
  2150.2 203.0 %all-reduce.16.cloned.1.call-done = (bf16[1024,2048]{1,0:T(8,128)(2,1)}, bf16[1024,2048]{1,0:T(8,128)(2,1)}) async-done(((bf16[1024,2048]{1,0:T(8,128)(2,1)}, bf16[1024,2048]{1,0:T(8,128)(2,1)}), (bf16[1024,2048]{1,0:T(8,128)(2,1)}, bf16[1024,2048]{1,0:T(8,128)(2,1)})) %all-reduce.16.cloned.1.call-update) | async-done | bytes 8388624 | tf_op jit(solution)/shard_map/psum | solution.py:232
  2353.2 5.6 fusion.57
  2358.8 23.2 all-reduce.6
  2384.4 13.6 fusion.48
  2398.5 45.0 %reduce-scatter.10.cloned.1.call-done = bf16[256,512]{1,0:T(8,128)(2,1)} async-done(((bf16[2048,512]{1,0:T(8,128)(2,1)}), bf16[256,512]{1,0:T(8,128)(2,1)}) %reduce-scatter.10.cloned.1.call-update) | async-done | bytes 262160 | tf_op jit(solution)/shard_map/reduce_scatter | solution.py:339
  2443.4 45.5 %reduce-scatter.8.cloned.1.call-done = bf16[256,512]{1,0:T(8,128)(2,1)} async-done(((bf16[2048,512]{1,0:T(8,128)(2,1)}), bf16[256,512]{1,0:T(8,128)(2,1)}) %reduce-scatter.8.cloned.1.call-update) | async-done | bytes 262160 | tf_op jit(solution)/shard_map/reduce_scatter | solution.py:336
  2488.9 45.1 %reduce-scatter.6.cloned.1.call-done = bf16[256,512]{1,0:T(8,128)(2,1)} async-done(((bf16[2048,512]{1,0:T(8,128)(2,1)}), bf16[256,512]{1,0:T(8,128)(2,1)}) %reduce-scatter.6.cloned.1.call-update) | async-done | bytes 262160 | tf_op jit(solution)/shard_map/reduce_scatter | solution.py:333
  (325 shorter events, 124.9 us)
Async XLA Ops:
  7.2 628.8 %copy-start = (bf16[2,256,2048]{2,1,0:T(8,128)(2,1)S(1)}, bf16[2,256,2048]{2,1,0:T(8,128)(2,1)}, u32[]{:S(2)}) copy-start(bf16[2,256,2048]{2,1,0:T(8,128)(2,1)} %param.37) | copy-start | bytes 6291460
  7.2 5.2 copy-start.77
  7.2 250.2 %all-reduce.12.cloned.1.call-start = ((), (), s32[]{:S(2)}) async-start(), calls=%async_computation.9 | async-start | bytes 8388608 | tf_op jit(solution)/shard_map/psum | solution.py:189
  12.3 13.8 copy-start.74
  19.2 6.8 copy-start.4
  19.2 6.8 copy-start.85
  26.1 13.6 copy-start.81
  39.6 9.6 copy-start.61
  42.9 6.3 copy-start.79
  60.8 5.0 copy-start.25
  60.8 5.0 copy-start.27
  92.7 9.4 copy-start.14
  92.7 9.4 copy-start.34
  102.8 159.6 %copy-start.44 = (s32[1024,8]{0,1:T(8,128)}, s32[1024,8]{0,1:T(8,128)S(1)}, u32[]{:S(2)}) copy-start(s32[1024,8]{0,1:T(8,128)S(1)} %add_select_fusion) | copy-start | bytes 98308
  103.7 158.7 %copy-start.48 = (s32[8192,1]{0,1:T(1,128)}, s32[8192,1]{0,1:T(1,128)S(1)}, u32[]{:S(2)}) copy-start(s32[8192,1]{0,1:T(1,128)S(1)} %compare_select_fusion) | copy-start | bytes 98308
  134.8 181.6 %copy-start.68 = (pred[8,768]{1,0:T(8,128)(4,1)}, pred[8,768]{1,0:T(8,128)(4,1)S(1)}, u32[]{:S(2)}) copy-start(pred[8,768]{1,0:T(8,128)(4,1)S(1)} %broadcast_in_dim.117) | copy-start | bytes 18436
  135.5 127.0 %copy-start.54 = (f32[2048]{0:T(1024)S(1)}, f32[2048]{0:T(1024)}, u32[]{:S(2)}) copy-start(f32[2048]{0:T(1024)} %param.33) | copy-start | bytes 24580
  257.4 5.1 copy-start.5
  257.4 5.9 copy-start.8
  328.7 277.3 %copy-start.32 = (bf16[2,2048,256]{2,1,0:T(8,128)(2,1)S(1)}, bf16[2,2048,256]{2,1,0:T(8,128)(2,1)}, u32[]{:S(2)}) copy-start(bf16[2,2048,256]{2,1,0:T(8,128)(2,1)} %param.35) | copy-start | bytes 6291460
  670.8 8.4 copy-start.67
  670.8 280.8 %all-to-all-start.1 = ((bf16[8,2,384,2048]{3,2,1,0:T(8,128)(2,1)}), bf16[8,2,384,2048]{3,2,1,0:T(8,128)(2,1)}, u32[]{:S(2)}, u32[]{:S(2)}) async-start(bf16[8,2,384,2048]{3,2,1,0:T(8,128)(2,1)} %copy.195), calls=%async_computation.1 | async-start | bytes 50331648 | tf_op jit(solution)/shard_map/all_to_all | solution.py:229
  679.2 49.2 %copy-start.49 = (s32[8192,1]{0,1:T(1,128)S(1)}, s32[8192,1]{0,1:T(1,128)}, u32[]{:S(2)}) copy-start(s32[8192,1]{0,1:T(1,128)} %copy-done.48) | copy-start | bytes 98308
  679.2 49.2 %copy-start.55 = (f32[2048]{0:T(1024)S(1)}, f32[2048]{0:T(1024)}, u32[]{:S(2)}) copy-start(f32[2048]{0:T(1024)} %param.33) | copy-start | bytes 24580
  679.2 49.2 %copy-start.57 = (bf16[2048,16]{0,1:T(8,128)(2,1)S(1)}, bf16[2048,16]{0,1:T(8,128)(2,1)}, u32[]{:S(2)}) copy-start(bf16[2048,16]{0,1:T(8,128)(2,1)} %param.34) | copy-start | bytes 196612
  679.2 49.2 %copy-start.64 = (f32[1024]{0:T(1024)S(1)}, f32[1024]{0:T(1024)}, u32[]{:S(2)}) copy-start(f32[1024]{0:T(1024)} %copy-done.63) | copy-start | bytes 12292
  737.1 214.5 %copy-start.70 = (f32[1024]{0:T(1024)}, f32[1024]{0:T(1024)S(1)}, u32[]{:S(2)}) copy-start(f32[1024]{0:T(1024)S(1)} %get-tuple-element.399) | copy-start | bytes 12292
  737.7 213.8 %copy-start.72 = (f32[1024]{0:T(1024)}, f32[1024]{0:T(1024)S(1)}, u32[]{:S(2)}) copy-start(f32[1024]{0:T(1024)S(1)} %fusion.103) | copy-start | bytes 12292
  972.2 46.0 %copy-start.45 = (s32[1024,8]{0,1:T(8,128)S(1)}, s32[1024,8]{0,1:T(8,128)}, u32[]{:S(2)}) copy-start(s32[1024,8]{0,1:T(8,128)} %copy-done.44) | copy-start | bytes 98308
  972.2 46.1 %copy-start.47 = (s32[1024,8]{0,1:T(8,128)S(1)}, s32[1024,8]{0,1:T(8,128)}, u32[]{:S(2)}) copy-start(s32[1024,8]{0,1:T(8,128)} %param.24) | copy-start | bytes 98308
  972.2 77.2 %copy-start.69 = (pred[8,768]{1,0:T(8,128)(4,1)S(1)}, pred[8,768]{1,0:T(8,128)(4,1)}, u32[]{:S(2)}) copy-start(pred[8,768]{1,0:T(8,128)(4,1)} %copy-done.68) | copy-start | bytes 18436
  1360.2 21.7 copy-start.33
  1429.7 7.9 copy-start.43
  1429.7 7.9 copy-start.71
  1429.7 8.0 copy-start.73
  1429.7 8.0 copy-start.58
  1429.7 280.4 %all-to-all-start.3 = ((bf16[8,768,2048]{2,1,0:T(8,128)(2,1)}), bf16[8,768,2048]{2,1,0:T(8,128)(2,1)}, u32[]{:S(2)}, u32[]{:S(2)}) async-start(bf16[8,768,2048]{2,1,0:T(8,128)(2,1)} %bitcast.215), calls=%async_computation.3 | async-start | bytes 50331648 | tf_op jit(solution)/shard_map/all_to_all | solution.py:271
  1437.6 517.9 %all-reduce.14.cloned.1.call-start = ((), (), s32[]{:S(2)}) async-start(), calls=%async_computation.10 | async-start | bytes 8388608 | tf_op jit(solution)/shard_map/psum | solution.py:281
  1802.2 275.4 %reduce-scatter.14.cloned.1.call-start = ((), (), s32[]{:S(2)}) async-start(), calls=%async_computation.15 | async-start | bytes 73728 | tf_op jit(solution)/shard_map/reduce_scatter | solution.py:357
  1907.5 6.4 copy-start.6
  1907.5 7.4 copy-start.9
  1907.5 7.4 copy-start.56
  1907.5 7.4 copy-start.65
  1921.3 431.9 %all-reduce.16.cloned.1.call-start = ((), (), s32[]{:S(2)}) async-start(), calls=%async_computation.16 | async-start | bytes 16777216 | tf_op jit(solution)/shard_map/psum | solution.py:232
  1955.5 7.2 copy-start.2
  1955.5 7.2 copy-start.7
  1955.5 8.3 copy-start.10
  1963.8 6.6 copy-start.84
  2022.7 4.8 copy-start.19
  2022.7 4.8 copy-start.60
  2022.7 4.8 copy-start.82
  2030.4 4.8 copy-start.62
  2030.4 4.8 copy-start.80
  2060.7 8.4 copy-start.75
  2060.8 8.4 copy-start.78
  2060.8 337.7 %reduce-scatter.12.cloned.1.call-start = ((), (), s32[]{:S(2)}) async-start(), calls=%async_computation.14 | async-start | bytes 2359296 | tf_op jit(solution)/shard_map/reduce_scatter | solution.py:342
  2069.1 6.6 copy-start.88
  2069.1 20.7 copy-start.39
  2069.1 374.3 %reduce-scatter.10.cloned.1.call-start = ((), (), s32[]{:S(2)}) async-start(), calls=%async_computation.13 | async-start | bytes 2359296 | tf_op jit(solution)/shard_map/reduce_scatter | solution.py:339
  2075.6 413.3 %reduce-scatter.8.cloned.1.call-start = ((), (), s32[]{:S(2)}) async-start(), calls=%async_computation.12 | async-start | bytes 2359296 | tf_op jit(solution)/shard_map/reduce_scatter | solution.py:336
  2096.2 437.7 %reduce-scatter.6.cloned.1.call-start = ((), (), s32[]{:S(2)}) async-start(), calls=%async_computation.11 | async-start | bytes 2359296 | tf_op jit(solution)/shard_map/reduce_scatter | solution.py:333
  2113.2 13.7 copy-start.37
  2353.2 5.6 copy-start.83
  2384.4 149.6 %copy-start.1 = (bf16[2,256,2048]{2,1,0:T(8,128)(2,1)S(1)}, bf16[2,256,2048]{2,1,0:T(8,128)(2,1)}, u32[]{:S(2)}) copy-start(bf16[2,256,2048]{2,1,0:T(8,128)(2,1)} %param.37) | copy-start | bytes 6291460
  (44 other events, 105.0 us)
Sparse Core Ops, SparseCore 0:
  102.2 155.1 all-reduce.11
  1802.3 153.1 all-reduce.13
  1959.1 31.4 reduce-scatter.13
  2060.9 292.2 all-reduce.15
  2357.3 41.1 reduce-scatter.11
  2402.2 41.1 reduce-scatter.9
  2447.6 41.2 reduce-scatter.7
  2492.7 41.1 reduce-scatter.5
where the time goes:
time: 2550 us; the launch traced here: 2540 us
  waiting for transfers between devices  975 us (38%)
  blocking collectives  608 us (24%)
  other arithmetic  343 us (13%)
  local copies, waits for them, and re-layouts  298 us (12%)
  matrix products  275 us (11%)
    all_to_all x1, blocking collectives, shards(): lax.all_to_all(grad_rows, 'expert', split_axis=0, concat_axis=0, tiled=True)  278 us
    all_to_all x1, blocking collectives, shards(): lax.all_to_all(send_rows, 'expert', split_axis=0, concat_axis=0, tiled=True)  277 us
    all_to_all x1, waiting for transfers between devices, shards(): lax.all_to_all(grad_in_rows.reshape(groups, experts_here * capacity, widt...  266 us
    all_to_all x1, waiting for transfers between devices, shards(): lax.all_to_all(partial_value, 'expert', split_axis=0, concat_axis=0, tile...  214 us
    psum x1, waiting for transfers between devices, shards(): moe = lax.psum(moe_part.astype(jnp.bfloat16), 'tensor').astype(jnp.float32)  203 us
    psum x1, waiting for transfers between devices, shards(): lax.psum(jnp.dot(context_low, w_output, preferred_element_type=jnp.float3...  122 us
    scatter-add x1, other arithmetic, shards(): moe_back = jax.ops.segment_sum(back_rows, source_row, num_segments=rows)  86.1 us
    scatter-add x1, other arithmetic, shards(): jax.ops.segment_sum(returned * gate_of[:, None], source_row, num_segments...  80.9 us
  transfers between devices with their start and end apart: 10, of which 9 were waited for; matrix products, arithmetic and copies ran while one was open for 15% of the time, Pallas kernels for 0%

commit v1 on v0

--- a/solution.py
+++ b/solution.py
@@ -1,6 +1,10 @@
+import functools
+
 import jax
 import jax.numpy as jnp
 from jax import lax
+from jax.experimental import pallas as pl
+from jax.experimental.pallas import tpu as pltpu
 from jax.sharding import PartitionSpec as P
 
 HEAD_DIM = 128
@@ -377,6 +381,469 @@
     )
 
 
+F32 = jnp.float32
+BF = jnp.bfloat16
+NN = (((1,), (0,)), ((), ()))
+NT = (((1,), (1,)), ((), ()))
+TN = (((0,), (0,)), ((), ()))
+VMEM_BYTES = 62 * 2**20
+COLUMN_TILE = 512
+ROW_TILE = 512
+QUERY_TILE = 256
+
+
+def mul(left, right, dims=NN):
+    return lax.dot_general(left, right, dims, preferred_element_type=F32)
+
+
+def kernel_params():
+    return pltpu.CompilerParams(vmem_limit_bytes=VMEM_BYTES)
+
+
+def whole(shape):
+    return pl.BlockSpec(shape, lambda i: (0,) * len(shape), pipeline_mode=pl.Buffered(1))
+
+
+def softmax_block(queries, keys, seg_rows, seg_columns, start, scale):
+    scores = mul(queries, keys, NT) * scale
+    rows = start + lax.broadcasted_iota(jnp.int32, scores.shape, 0)
+    columns = lax.broadcasted_iota(jnp.int32, scores.shape, 1)
+    allowed = (seg_rows == seg_columns) & (columns <= rows)
+    scores = jnp.where(allowed, scores, NEG)
+    raised = jnp.exp(scores - jnp.max(scores, axis=-1, keepdims=True))
+    return raised * (1.0 / jnp.sum(raised, axis=-1, keepdims=True))
+
+
+def attention_kernel(
+    q_ref, k_ref, v_ref, qi_ref, ki_ref, qg_ref, kg_ref, cos_ref, sin_ref, row_ref, col_ref,
+    qh_ref, kh_ref, ctx_ref,
+):
+    rows, size = q_ref.shape
+    tile = min(QUERY_TILE, rows)
+    for raw, inverse, gain, low in ((q_ref, qi_ref, qg_ref, qh_ref), (k_ref, ki_ref, kg_ref, kh_ref)):
+        normed = raw[...] * inverse[...] * gain[...]
+        turned = normed * cos_ref[...] + pltpu.roll(normed, size // 2, 1) * sin_ref[...]
+        low[...] = turned.astype(BF)
+    for start in range(0, rows, tile):
+        end = start + tile
+        weights = softmax_block(
+            qh_ref[start:end], kh_ref[:end], row_ref[start:end], col_ref[:, :end], start, size**-0.5
+        )
+        ctx_ref[start:end] = mul(weights.astype(BF), v_ref[:end]).astype(BF)
+
+
+def attention_back_kernel(
+    q_ref, k_ref, v_ref, qi_ref, ki_ref, qg_ref, kg_ref, cos_ref, sin_ref, row_ref, col_ref,
+    qh_ref, kh_ref, dctx_ref,
+    dq_ref, dk_ref, dv_ref, inner_ref, dqg_ref, dkg_ref, dq_total, dk_total, dv_total,
+):
+    rows, size = q_ref.shape
+    scale = size**-0.5
+    tile = min(QUERY_TILE, rows)
+    dk_total[...] = jnp.zeros_like(dk_total)
+    dv_total[...] = jnp.zeros_like(dv_total)
+    for start in range(0, rows, tile):
+        end = start + tile
+        keys = kh_ref[:end]
+        weights = softmax_block(
+            qh_ref[start:end], keys, row_ref[start:end], col_ref[:, :end], start, scale
+        )
+        grad_weights = mul(dctx_ref[start:end], v_ref[:end], NT)
+        inner = jnp.sum(weights * grad_weights, axis=-1, keepdims=True)
+        grad_scores = (weights * (grad_weights - inner)).astype(BF)
+        dq_total[start:end] = mul(grad_scores, keys) * scale
+        dk_total[:end] += mul(grad_scores, qh_ref[start:end], TN) * scale
+        dv_total[:end] += mul(weights.astype(BF), dctx_ref[start:end], TN)
+    dv_ref[...] = dv_total[...].astype(BF)
+    inners = []
+    for total, raw, inverse, gain, out, dgain in (
+        (dq_total, q_ref, qi_ref, qg_ref, dq_ref, dqg_ref),
+        (dk_total, k_ref, ki_ref, kg_ref, dk_ref, dkg_ref),
+    ):
+        grad = total[...]
+        grad = grad * cos_ref[...] - pltpu.roll(grad, size // 2, 1) * sin_ref[...]
+        values = raw[...]
+        dgain[...] = jnp.sum(grad * values * inverse[...], axis=0, keepdims=True)
+        scaled = grad * gain[...]
+        inners.append(jnp.sum(values * scaled, axis=1, keepdims=True))
+        out[...] = scaled
+    inner_ref[0] = jnp.concatenate(inners, axis=1)
+
+
+def head_specs(rows):
+    head = pl.BlockSpec((rows, HEAD_DIM), lambda h: (0, h))
+    gain = pl.BlockSpec((1, HEAD_DIM), lambda h: (0, h))
+    column = whole((rows, 1))
+    table = whole((rows, HEAD_DIM))
+    return head, gain, [head, head, head, column, column, gain, gain, table, table, column, whole((1, rows))]
+
+
+def attention_call(operands, rows, local):
+    head, gain, specs = head_specs(rows)
+    heads = local // HEAD_DIM
+    return pl.pallas_call(
+        attention_kernel,
+        grid=(heads,),
+        in_specs=specs,
+        out_specs=[head] * 3,
+        out_shape=[jax.ShapeDtypeStruct((rows, local), BF)] * 3,
+        compiler_params=kernel_params(),
+        cost_estimate=pl.CostEstimate(
+            flops=2 * rows * rows * local, bytes_accessed=12 * rows * local, transcendentals=rows * rows * heads // 2
+        ),
+        name="attention_rows",
+    )(*operands)
+
+
+def attention_back_call(operands, rows, local):
+    head, gain, specs = head_specs(rows)
+    heads = local // HEAD_DIM
+    return pl.pallas_call(
+        attention_back_kernel,
+        grid=(heads,),
+        in_specs=specs + [head] * 3,
+        out_specs=[head] * 3 + [pl.BlockSpec((1, rows, 2), lambda h: (h, 0, 0)), gain, gain],
+        out_shape=[jax.ShapeDtypeStruct((rows, local), F32)] * 2
+        + [jax.ShapeDtypeStruct((rows, local), BF), jax.ShapeDtypeStruct((heads, rows, 2), F32)]
+        + [jax.ShapeDtypeStruct((1, local), F32)] * 2,
+        scratch_shapes=[pltpu.VMEM((rows, HEAD_DIM), F32)] * 3,
+        compiler_params=kernel_params(),
+        cost_estimate=pl.CostEstimate(
+            flops=8 * rows * rows * local, bytes_accessed=24 * rows * local, transcendentals=rows * rows * heads // 2
+        ),
+        name="attention_rows_back",
+    )(*operands)
+
+
+def rows_kernel(sets, experts, x_ref, dy_ref, gate_ref, *rest):
+    w_refs = rest[:sets]
+    moe_ref, dx_ref, kept_ref, dot_ref, held, moe, dx, sems = rest[sets:]
+    step = pl.program_id(0)
+    slot = lax.rem(step, 2)
+    rows, width = x_ref.shape
+    hid = held.shape[2] // 3
+
+    def fetch(index, place):
+        for number in range(sets):
+
+            @pl.when(index == number)
+            def _():
+                pltpu.make_async_copy(w_refs[number], held.at[place], sems.at[place]).start()
+
+    @pl.when(step == 0)
+    def _():
+        fetch(0, 0)
+        moe[...] = jnp.zeros_like(moe)
+        dx[...] = jnp.zeros_like(dx)
+
+    @pl.when(step + 1 < sets)
+    def _():
+        fetch(step + 1, 1 - slot)
+
+    pltpu.make_async_copy(w_refs[0], held.at[slot], sems.at[slot]).wait()
+    for one in range(experts):
+        base = one * 3 * hid
+        for first in range(0, rows, ROW_TILE):
+            here = slice(first, first + ROW_TILE)
+            both = mul(x_ref[here], held[slot, one, hid:], NT)
+            back = mul(dy_ref[here], held[slot, one, :hid], NT)
+            pre, up = both[:, :hid], both[:, hid:]
+            sigma = 1.0 / (1.0 + jnp.exp(-pre))
+            active = pre * sigma
+            gate = gate_ref[0, here, one : one + 1]
+            hidden = active * up
+            dot_ref[0, here, one : one + 1] = jnp.sum(hidden * back, axis=1, keepdims=True)
+            back = back * gate
+            kept_ref[here, base : base + hid] = (hidden * gate).astype(BF)
+            kept_ref[here, base + hid : base + 2 * hid] = (
+                back * up * sigma * (1.0 + pre * (1.0 - sigma))
+            ).astype(BF)
+            kept_ref[here, base + 2 * hid : base + 3 * hid] = (back * active).astype(BF)
+    for first in range(0, width, COLUMN_TILE):
+        here = slice(first, first + COLUMN_TILE)
+        total = moe[:, here]
+        for one in range(experts):
+            base = one * 3 * hid
+            total = total + mul(kept_ref[:, base : base + hid], held[slot, one, :hid, here])
+        moe[:, here] = total
+        total = dx[:, here]
+        for one in range(experts):
+            base = one * 3 * hid
+            total = total + mul(kept_ref[:, base + hid : base + 3 * hid], held[slot, one, hid:, here])
+        dx[:, here] = total
+
+    @pl.when(step == sets - 1)
+    def _():
+        moe_ref[...] = moe[...].astype(BF)
+        dx_ref[...] = dx[...].astype(BF)
+
+
+def rows_call(moe_in, cotangent, gates, weights):
+    rows, width = moe_in.shape
+    sets = len(weights)
+    experts, depth, _ = weights[0].shape
+    full = whole((rows, width))
+    narrow = pl.BlockSpec((1, rows, experts), lambda i: (i, 0, 0))
+    wide = experts * depth
+    return pl.pallas_call(
+        functools.partial(rows_kernel, sets, experts),
+        grid=(sets,),
+        in_specs=[full, full, narrow] + [pl.BlockSpec(memory_space=pl.ANY)] * sets,
+        out_specs=[full, full, pl.BlockSpec((rows, wide), lambda i: (0, i)), narrow],
+        out_shape=[jax.ShapeDtypeStruct((rows, width), BF)] * 2
+        + [jax.ShapeDtypeStruct((rows, sets * wide), BF), jax.ShapeDtypeStruct((sets, rows, experts), F32)],
+        scratch_shapes=[
+            pltpu.VMEM((2, experts, depth, width), BF),
+            pltpu.VMEM((rows, width), F32),
+            pltpu.VMEM((rows, width), F32),
+            pltpu.SemaphoreType.DMA((2,)),
+        ],
+        compiler_params=kernel_params(),
+        cost_estimate=pl.CostEstimate(
+            flops=4 * rows * width * wide * sets,
+            bytes_accessed=8 * rows * width + 2 * sets * wide * (rows + width),
+            transcendentals=rows * wide * sets // 3,
+        ),
+        name="expert_rows",
+    )(moe_in, cotangent, gates, *weights)
+
+
+def weight_grads_kernel(experts, added, x_ref, dy_ref, kept_ref, *rest):
+    out_ref, turned = rest[-2:]
+    hid = turned.shape[0] // (3 * experts)
+
+    @pl.when(pl.program_id(0) == 0)
+    def _():
+        for one in range(experts):
+            base = one * 3 * hid
+            turned[one * hid : (one + 1) * hid] = kept_ref[:, base : base + hid].T
+            place = experts * hid + one * 2 * hid
+            turned[place : place + 2 * hid] = kept_ref[:, base + hid : base + 3 * hid].T
+
+    down = mul(turned[: experts * hid], dy_ref[...])
+    both = mul(turned[experts * hid :], x_ref[...])
+    for one in range(experts):
+        first, second = down[one * hid : (one + 1) * hid], both[one * 2 * hid : (one + 1) * 2 * hid]
+        if added:
+            first = first + rest[0][one, :hid].astype(F32)
+            second = second + rest[0][one, hid:].astype(F32)
+        out_ref[one, :hid] = first.astype(BF)
+        out_ref[one, hid:] = second.astype(BF)
+
+
+def weight_grads_call(moe_in, cotangent, kept, number, experts, depth, addend=None):
+    rows, width = moe_in.shape
+    tile = COLUMN_TILE
+    column = pl.BlockSpec((rows, tile), lambda i: (0, i))
+    out = pl.BlockSpec((experts, depth, tile), lambda i: (0, 0, i))
+    operands = [moe_in, cotangent, kept]
+    specs = [column, column, pl.BlockSpec((rows, experts * depth), lambda i: (0, number), pipeline_mode=pl.Buffered(1))]
+    if addend is not None:
+        operands.append(addend)
+        specs.append(out)
+    return pl.pallas_call(
+        functools.partial(weight_grads_kernel, experts, addend is not None),
+        grid=(width // tile,),
+        in_specs=specs,
+        out_specs=out,
+        out_shape=jax.ShapeDtypeStruct((experts, depth, width), BF),
+        scratch_shapes=[pltpu.VMEM((experts * depth, rows), BF)],
+        compiler_params=kernel_params(),
+        cost_estimate=pl.CostEstimate(
+            flops=2 * rows * width * experts * depth,
+            bytes_accessed=4 * rows * width + 4 * experts * depth * width,
+            transcendentals=0,
+        ),
+        name="expert_weight_grads",
+    )(*operands)
+
+
+def swap(values, bit):
+    size = lax.axis_size("expert")
+    return lax.ppermute(values, "expert", [(i, i ^ bit) for i in range(size)])
+
+
+def spread_weights(own):
+    held = {0: own}
+    held[1] = swap(own, 1)
+    held[2] = swap(own, 2)
+    held[4] = swap(own, 4)
+    half = own.shape[0] // 2
+    far = (swap(held[2][:half], 4), swap(held[4][half:], 2))
+    held[6] = jnp.concatenate(far, axis=0)
+    for r in (3, 5, 7):
+        held[r] = swap(held[r - 1], 1)
+    return held
+
+
+def collect_weight_grads(part):
+    chip = {}
+    for r in (6, 4, 2, 0):
+        chip[r] = part(r, swap(part(r + 1, None), 1))
+    half = chip[6].shape[0] // 2
+    via_first = swap(chip[6][:half], 2)
+    via_second = swap(chip[6][half:], 4)
+    plus = lambda left, right: (left.astype(F32) + right.astype(F32)).astype(BF)
+    from_four = (swap(plus(chip[4][:half], via_first), 4), swap(chip[4][half:], 4))
+    from_two = (swap(chip[2][:half], 2), swap(plus(chip[2][half:], via_second), 2))
+    total = chip[0].astype(F32) + jnp.concatenate(from_four, axis=0).astype(F32)
+    return total + jnp.concatenate(from_two, axis=0).astype(F32)
+
+
+def shards_near(
+    tokens, cotangent, seq_lengths, expert_ids, slot_index, w_query, w_key, w_value, w_output,
+    query_gain, key_gain, attn_gain, moe_gain, router, w_gate, w_up, w_down,
+):
+    rows, width = tokens.shape
+    local = w_query.shape[1]
+    groups = lax.axis_size("expert")
+    n_tensor = lax.axis_size("tensor")
+    here = lax.axis_index("expert")
+    layer = lax.axis_index("tensor")
+    experts_here, hid = w_gate.shape[0], w_gate.shape[2]
+    experts_all = experts_here * groups
+    own_rows = rows // n_tensor
+
+    packed = jnp.concatenate([w_down, jnp.swapaxes(w_gate, 1, 2), jnp.swapaxes(w_up, 1, 2)], axis=1)
+    weights = spread_weights(packed)
+
+    segment, position = layout(seq_lengths, rows)
+    cosine, sine = rope_angles(position, HEAD_DIM)
+    cos_table = jnp.concatenate([cosine, cosine], axis=1)
+    sin_table = jnp.concatenate([-sine, sine], axis=1)
+    inputs = tokens.astype(F32)
+    normed, inverse_in = norm_rows(inputs, attn_gain)
+    attn_in = normed.astype(BF)
+    query_raw = mul(attn_in, w_query)
+    key_raw = mul(attn_in, w_key)
+    totals = jnp.stack([jnp.sum(query_raw * query_raw, axis=-1), jnp.sum(key_raw * key_raw, axis=-1)])
+    totals = sum_small(totals)
+    values = mul(attn_in, w_value).astype(BF)
+    query_inverse = lax.rsqrt(totals[0] / width + EPS)[:, None]
+    key_inverse = lax.rsqrt(totals[1] / width + EPS)[:, None]
+    operands = [
+        query_raw, key_raw, values, query_inverse, key_inverse, query_gain[None], key_gain[None],
+        cos_table, sin_table, segment[:, None], segment[None],
+    ]
+    queries, keys, context = attention_call(operands, rows, local)
+    attn = lax.psum_scatter(mul(context, w_output).astype(BF), "tensor", scatter_dimension=0, tiled=True)
+
+    own = lambda array: lax.dynamic_slice_in_dim(array, layer * own_rows, own_rows, 0)
+    tokens_own = own(tokens).astype(F32)
+    cotangent_own = own(cotangent).astype(F32)
+    hidden_in = tokens_own + attn.astype(F32)
+    moe_in, inverse_moe = norm_rows(hidden_in, moe_gain)
+    router_wide = router.astype(F32)
+    shares = jax.nn.softmax(jnp.dot(moe_in, router_wide, precision=lax.Precision.HIGHEST), axis=-1)
+    moe_low = lax.all_gather(moe_in.astype(BF), "tensor", tiled=True)
+    shares_all = gather_small(shares)
+
+    number = jnp.arange(experts_all, dtype=jnp.int32)
+    carried = (expert_ids[:, :, None] == number) & (slot_index >= 0)[:, :, None]
+    carried = jnp.sum(carried.astype(F32), axis=1)
+    gates = shares_all * carried
+    order = [0, 1, 2, 3, 4, 5, 6, 7]
+    of_set = lambda array, r: lax.dynamic_slice_in_dim(array, (here ^ r) * experts_here, experts_here, 1)
+    gate_sets = jnp.stack([of_set(gates, r) for r in order])
+    moe_part, dx_part, kept, dots = rows_call(moe_low, cotangent, gate_sets, [weights[r] for r in order])
+
+    dots_all = jnp.zeros((rows, experts_all), F32)
+    for place, r in enumerate(order):
+        dots_all = lax.dynamic_update_slice(dots_all, dots[place], (0, (here ^ r) * experts_here))
+    dshares = scatter_small(dots_all * carried)
+    dlogits = shares * (dshares - jnp.sum(shares * dshares, axis=-1, keepdims=True))
+    router_back = jnp.einsum("te,de->td", dlogits, router_wide, precision=lax.Precision.HIGHEST)
+    router_part = jnp.einsum("td,te->de", moe_in, dlogits, precision=lax.Precision.HIGHEST)
+
+    dx = lax.psum_scatter(dx_part, "tensor", scatter_dimension=0, tiled=True)
+    grad_moe_in = dx.astype(F32) + router_back
+    grad_norm_moe, grad_moe_gain = norm_back(hidden_in, inverse_moe, moe_gain, grad_moe_in)
+    grad_hidden_in = cotangent_own + grad_norm_moe
+    grad_low = lax.all_gather(grad_hidden_in.astype(BF), "tensor", tiled=True)
+    grad_context = mul(grad_low, w_output, NT).astype(BF)
+    dq, dk, value_low, inner, grad_query_gain, grad_key_gain = attention_back_call(
+        operands + [queries, keys, grad_context], rows, local
+    )
+    inner = sum_small(jnp.sum(inner, axis=0).T)
+    moe = lax.psum_scatter(moe_part, "tensor", scatter_dimension=0, tiled=True)
+    out = lax.all_gather((hidden_in + moe.astype(F32)).astype(BF), "tensor", tiled=True)
+
+    def raw_grad(scaled, raw, inverse, total):
+        return (inverse * scaled - raw * inverse * inverse * inverse * (total / width)[:, None]).astype(BF)
+
+    query_low = raw_grad(dq, query_raw, query_inverse, inner[0])
+    key_low = raw_grad(dk, key_raw, key_inverse, inner[1])
+    terms_in = mul(query_low, w_query, NT) + mul(key_low, w_key, NT) + mul(value_low, w_value, NT)
+    grad_normed = lax.psum_scatter(terms_in.astype(BF), "tensor", scatter_dimension=0, tiled=True).astype(F32)
+    inverse_own = lax.dynamic_slice_in_dim(inverse_in, layer * own_rows, own_rows, 0)
+    grad_norm_in, grad_attn_gain = norm_back(tokens_own, inverse_own, attn_gain, grad_normed)
+    grad_input = lax.all_gather((grad_hidden_in + grad_norm_in).astype(BF), "tensor", tiled=True)
+
+    depth = packed.shape[1]
+    part = lambda r, addend: weight_grads_call(moe_low, cotangent, kept, order.index(r), experts_here, depth, addend)
+    expert_grads = collect_weight_grads(part).astype(BF)
+    grad_w_down = expert_grads[:, :hid]
+    grad_w_gate = jnp.swapaxes(expert_grads[:, hid : 2 * hid], 1, 2)
+    grad_w_up = jnp.swapaxes(expert_grads[:, 2 * hid :], 1, 2)
+
+    scatter = lambda array, dim: lax.psum_scatter(array, "expert", scatter_dimension=dim, tiled=True)
+    grad_w_query = scatter(mul(attn_in, query_low, TN).astype(BF), 0)
+    grad_w_key = scatter(mul(attn_in, key_low, TN).astype(BF), 0)
+    grad_w_value = scatter(mul(attn_in, value_low, TN).astype(BF), 0)
+    grad_w_output = scatter(mul(context, grad_low, TN).astype(BF), 1)
+    gains = scatter(jnp.concatenate([
+        grad_query_gain.reshape(groups, -1), grad_key_gain.reshape(groups, -1)], axis=1), 0)[0]
+    span = local // groups
+    both = jnp.concatenate(
+        [router_part, grad_moe_gain[:, None], grad_attn_gain[:, None]], axis=1
+    )
+    both = scatter(lax.psum(both, "tensor"), 0)
+    return (
+        out, grad_input, grad_w_query, grad_w_key, grad_w_value, grad_w_output,
+        gains[:span].astype(BF), gains[span:].astype(BF),
+        both[:, experts_all + 1].astype(BF), both[:, experts_all].astype(BF), both[:, :experts_all].astype(BF),
+        grad_w_gate, grad_w_up, grad_w_down,
+    )
+
+
+def rotations():
+    size = lax.axis_size("tensor")
+    return [[(i, (i + d) % size) for i in range(size)] for d in range(1, size)]
+
+
+def sum_small(values):
+    total = values
+    for pairs in rotations():
+        total = total + lax.ppermute(values, "tensor", pairs)
+    return total
+
+
+def gather_small(values):
+    rows = values.shape[0]
+    size = lax.axis_size("tensor")
+    place = lax.axis_index("tensor")
+    whole_rows = jnp.zeros((rows * size,) + values.shape[1:], values.dtype)
+    whole_rows = lax.dynamic_update_slice_in_dim(whole_rows, values, place * rows, 0)
+    for d, pairs in enumerate(rotations(), 1):
+        came = lax.ppermute(values, "tensor", pairs)
+        whole_rows = lax.dynamic_update_slice_in_dim(whole_rows, came, lax.rem(place + size - d, size) * rows, 0)
+    return whole_rows
+
+
+def scatter_small(values):
+    size = lax.axis_size("tensor")
+    place = lax.axis_index("tensor")
+    rows = values.shape[0] // size
+    cut = lambda index: lax.dynamic_slice_in_dim(values, index * rows, rows, 0)
+    total = cut(place)
+    for d, pairs in enumerate(rotations(), 1):
+        total = total + lax.ppermute(cut(lax.rem(place + d, size)), "tensor", pairs)
+    return total
+
+
+NEAR_GROUPS = 8
+
+
 def solution(mesh):
     placed = (
         P("expert", None),
@@ -398,7 +865,7 @@
         P("expert", "tensor", None),
     )
     return jax.shard_map(
-        shards,
+        shards_near if mesh.shape["expert"] == NEAR_GROUPS else shards,
         mesh=mesh,
         in_specs=placed,
         out_specs=(

time: 2550 us -> 1300 us (0.51)
  blocking collectives: 608 us -> 28.4 us
  other arithmetic: 343 us -> 63.3 us
  Pallas kernels: 0 us -> 274 us
  waiting for transfers between devices: 975 us -> 737 us
  local copies, waits for them, and re-layouts: 298 us -> 74.1 us
  matrix products: 275 us -> 65.1 us
    all_to_all x2 -> x0, blocking collectives: 555 us -> none  [the longest x1 278 us: shards(): lax.all_to_all(grad_rows, 'expert', split_axis=0, concat_axis=0, tiled=True)]
    all_to_all x2 -> x0, waiting for transfers between devices: 480 us -> none  [the longest x1 266 us: shards(): lax.all_to_all(grad_in_rows.reshape(groups, experts_here * capacity, widt...]
    ppermute x0 -> x30, waiting for transfers between devices: none -> 389 us  [the longest x18 323 us: swap(): return lax.ppermute(values, 'expert', [(i, i ^ bit) for i in range(size)])]
    psum x3 -> x0, waiting for transfers between devices: 359 us -> none  [the longest x1 203 us: shards(): moe = lax.psum(moe_part.astype(jnp.bfloat16), 'tensor').astype(jnp.float32)]
    pallas_call x0 -> x11, Pallas kernels: none -> 274 us  [the longest x1 121 us: rows_call(): pl.pallas_call(functools.partial(rows_kernel, sets, experts), grid=(sets,...]
    dot_general x38 -> x15, matrix products: 275 us -> 65.1 us  [the longest x12 56.4 us: mul(): return lax.dot_general(left, right, dims, preferred_element_type=F32)]
    scatter-add x2 -> x0, other arithmetic: 167 us -> none  [the longest x1 86.1 us: shards(): moe_back = jax.ops.segment_sum(back_rows, source_row, num_segments=rows)]
    gather x5 -> x0, local copies, waits for them, and re-layouts: 144 us -> none  [the longest x1 49.2 us: shards(): cotangent[source_row]]
  transfers between devices with their start and end apart: 10 -> 43, of which waited for: 9 -> 23; matrix products, arithmetic and copies ran while one was open for 15% -> 12% of each run, Pallas kernels for 0% -> 10%
where the time goes in v1:
time: 1300 us; the launch traced here: 1290 us
  waiting for transfers between devices  737 us (57%)
  Pallas kernels  274 us (21%)
  local copies, waits for them, and re-layouts  74.1 us (6%)
  matrix products  65.1 us (5%)
  other arithmetic  63.3 us (5%)
  starting transfers between devices  31.5 us (2%)
  blocking collectives  28.4 us (2%)
  between operations  14.8 us (1%)
    ppermute x18, waiting for transfers between devices, swap(): return lax.ppermute(values, 'expert', [(i, i ^ bit) for i in range(size)])  323 us
    pallas_call x1, Pallas kernels, rows_call(): pl.pallas_call(functools.partial(rows_kernel, sets, experts), grid=(sets,...  121 us
    pallas_call x8, Pallas kernels, weight_grads_call(): pl.pallas_call(functools.partial(weight_grads_kernel, experts, addend is...  105 us
    all_gather x1, waiting for transfers between devices, shards_near(): grad_low = lax.all_gather(grad_hidden_in.astype(BF), 'tensor', tiled=True)  79.4 us
    reduce_scatter x1, waiting for transfers between devices, shards_near(): moe = lax.psum_scatter(moe_part, 'tensor', scatter_dimension=0, tiled=True)  76.7 us
    reduce_scatter x1, waiting for transfers between devices, shards_near(): lax.psum_scatter(terms_in.astype(BF), 'tensor', scatter_dimension=0, tile...  75.1 us
    reduce_scatter x1, waiting for transfers between devices, shards_near(): dx = lax.psum_scatter(dx_part, 'tensor', scatter_dimension=0, tiled=True)  62.5 us
    dot_general x12, matrix products, mul(): return lax.dot_general(left, right, dims, preferred_element_type=F32)  56.4 us
  transfers between devices with their start and end apart: 43, of which 23 were waited for; matrix products, arithmetic and copies ran while one was open for 12% of the time, Pallas kernels for 10%

profile of v1, /device:TPU:20, one launch (start us, length us, event | category | flops | bytes accessed | tf_op | source)
XLA Modules:
  0.0 1288.7 jit_solution(17018849561666218188)
XLA Ops:
  7.3 3.2 fusion
  10.7 5.7 multiply_reduce_fusion.4
  16.4 3.9 multiply_reduce_fusion.3
  24.0 2.9 copy.220
  27.0 4.0 copy.221
  30.9 5.5 pad_maximum_fusion.rest_0_
  42.4 5.6 convolution_convert_fusion.6.v_ref
  58.0 8.8 collective-permute-done.2
  69.6 17.7 %attention_rows.1 = (bf16[1024,512]{1,0:T(8,128)(2,1)}, bf16[1024,512]{1,0:T(8,128)(2,1)}, bf16[1024,512]{1,0:T(8,128)(2,1)}) custom-call(f32[1024,512]{1,0:T(8,128)} %copy.216.q_ref, f32[1024,512]{1,0:T(8,128)} %copy.217.k_ref, bf16[1024,512]{1,0:T(8,128)(2,1)} %convolution_convert_fusion.6.v_ref, f32[1024,1]{1,0:T(8,128)} %get-tuple-element.172.qi_ref, ...), custom_call_target="tpu_custom_call" | custom-call | flops 1073741824 | bytes 6291456 | tf_op jit(solution)/shard_map/attention_rows/pallas_call | solution.py:484
  87.3 6.3 convolution_convert_fusion
  94.6 78.6 %collective-permute-done.7.rest_2_ = bf16[2,768,2048]{2,1,0:T(8,128)(2,1)} collective-permute-done((bf16[2,768,2048]{2,1,0:T(8,128)(2,1)}, bf16[2,768,2048]{2,1,0:T(8,128)(2,1)}, u32[]{:S(2)}, u32[]{:S(2)}) %collective-permute-start.7) | collective-permute-done | bytes 6291488 | tf_op jit(solution)/shard_map/ppermute | solution.py:663
  173.3 4.0 slice.121
  177.7 55.0 %collective-permute-done.9.rest_4_ = bf16[2,768,2048]{2,1,0:T(8,128)(2,1)S(1)} collective-permute-done((bf16[2,768,2048]{2,1,0:T(8,128)(2,1)}, bf16[2,768,2048]{2,1,0:T(8,128)(2,1)S(1)}, u32[]{:S(2)}, u32[]{:S(2)}) %collective-permute-start.9) | collective-permute-done | bytes 6291488 | tf_op jit(solution)/shard_map/ppermute | solution.py:663
  240.3 2.9 fusion.15
  243.2 55.9 %collective-permute-done.11 = bf16[1,768,2048]{2,1,0:T(8,128)(2,1)S(1)} collective-permute-done((bf16[1,768,2048]{2,1,0:T(8,128)(2,1)}, bf16[1,768,2048]{2,1,0:T(8,128)(2,1)S(1)}, u32[]{:S(2)}, u32[]{:S(2)}) %collective-permute-start.11) | collective-permute-done | bytes 3145760 | tf_op jit(solution)/shard_map/ppermute | solution.py:663
  301.1 3.7 collective-permute-done.12
  304.8 4.0 constant_dynamic-update-slice_fusion.12.rest_6_
  312.3 4.0 collective-permute-done.3
  317.2 4.1 collective-permute-done.4
  328.1 120.7 %expert_rows.1 = (bf16[1024,2048]{1,0:T(8,128)(2,1)}, bf16[1024,2048]{1,0:T(8,128)(2,1)}, bf16[1024,12288]{1,0:T(8,128)(2,1)}, f32[8,1024,2]{2,1,0:T(8,128)}) custom-call(bf16[1024,2048]{1,0:T(8,128)(2,1)} %all-gather.5.cloned.1.call-done.x_ref, bf16[1024,2048]{1,0:T(8,128)(2,1)} %dy_ref.17, f32[8,1024,2]{2,1,0:T(8,128)} %copy.222.gate_ref, ...), custom_call_target="tpu_custom_call" | custom-call | flops 103079215104 | bytes 92274688 | tf_op jit(solution)/shard_map/expert_rows/pallas_call | solution.py:588
  449.4 3.6 slice_bitcast_fusion.2
  458.9 3.7 collective-permute-start.14
  467.6 62.5 %reduce-scatter.14.cloned.1.call-done = bf16[256,2048]{1,0:T(8,128)(2,1)} async-done(((bf16[1024,2048]{1,0:T(8,128)(2,1)}), bf16[256,2048]{1,0:T(8,128)(2,1)}) %reduce-scatter.14.cloned.1.call-update) | async-done | bytes 1048592 | tf_op jit(solution)/shard_map/reduce_scatter | solution.py:758
  530.1 3.3 multiply_reduce_fusion
  533.4 76.7 %reduce-scatter.12.cloned.1.call-done = bf16[256,2048]{1,0:T(8,128)(2,1)} async-done(((bf16[1024,2048]{1,0:T(8,128)(2,1)}), bf16[256,2048]{1,0:T(8,128)(2,1)}) %reduce-scatter.12.cloned.1.call-update) | async-done | bytes 1048592 | tf_op jit(solution)/shard_map/reduce_scatter | solution.py:768
  610.2 5.5 fusion.44
  615.7 79.4 %all-gather.9.cloned.1.call-done = bf16[1024,2048]{1,0:T(8,128)(2,1)} async-done(((bf16[256,2048]{1,0:T(8,128)(2,1)}), bf16[1024,2048]{1,0:T(8,128)(2,1)}) %all-gather.9.cloned.1.call-update) | async-done | bytes 4194320 | tf_op jit(solution)/shard_map/all_gather | solution.py:762
  695.1 6.3 convolution_convert_fusion.5.dctx_ref
  701.4 30.7 %attention_rows_back.1 = (f32[1024,512]{1,0:T(8,128)}, f32[1024,512]{1,0:T(8,128)}, bf16[1024,512]{1,0:T(8,128)(2,1)}, f32[4,1024,2]{2,1,0:T(8,128)}, f32[1,512]{1,0:T(1,128)}, /*index=5*/f32[1,512]{1,0:T(1,128)}) custom-call(f32[1024,512]{1,0:T(8,128)} %copy.216.q_ref, f32[1024,512]{1,0:T(8,128)} %copy.217.k_ref, ...), custom_call_target="tpu_custom_call" | custom-call | flops 4294967296 | bytes 12582912 | tf_op jit(solution)/shard_map/attention_rows_back/pallas_call | solution.py:501
  736.9 3.2 collective-permute-start.19
  740.0 32.3 %collective-permute-done.17 = f32[2,1024]{0,1:T(8,128)S(1)} collective-permute-done((f32[2,1024]{0,1:T(8,128)}, f32[2,1024]{0,1:T(8,128)S(1)}, u32[]{:S(2)}, u32[]{:S(2)}) %collective-permute-start.17) | collective-permute-done | bytes 8224 | tf_op jit(solution)/shard_map/ppermute | solution.py:817
  772.3 9.7 collective-permute-done.19
  783.8 2.9 subtract_convert_fusion
  791.5 6.0 add_convert_fusion.1
  801.2 75.1 %reduce-scatter.16.cloned.1.call-done = bf16[256,2048]{1,0:T(8,128)(2,1)} async-done(((bf16[1024,2048]{1,0:T(8,128)(2,1)}), bf16[256,2048]{1,0:T(8,128)(2,1)}) %reduce-scatter.16.cloned.1.call-update) | async-done | bytes 1048592 | tf_op jit(solution)/shard_map/reduce_scatter | solution.py:777
  879.4 3.0 fusion.6
  882.9 12.6 expert_weight_grads.12
  895.5 12.3 expert_weight_grads.14
  908.3 12.4 expert_weight_grads.10
  920.7 5.9 convolution_convert_fusion.1
  926.7 13.8 %expert_weight_grads.13 = bf16[2,768,2048]{2,1,0:T(8,128)(2,1)} custom-call(bf16[1024,2048]{1,0:T(8,128)(2,1)} %all-gather.5.cloned.1.call-done.x_ref, bf16[1024,2048]{1,0:T(8,128)(2,1)} %dy_ref.17, bf16[1024,12288]{1,0:T(8,128)(2,1)} %get-tuple-element.39.kept_ref, bf16[2,768,2048]{2,1,0:T(8,128)(2,1)} %collective-permute-done.22.rest_0_), custom_call_target="tpu_custom_call" | custom-call | flops 6442450944 | bytes 20971520 | tf_op jit(solution)/shard_map/expert_weight_grads/pallas_call | solution.py:644
  940.5 6.8 fusion.47
  947.3 4.0 convolution_convert_fusion.2
  953.6 12.3 expert_weight_grads.8
  966.0 13.8 %expert_weight_grads.15 = bf16[2,768,2048]{2,1,0:T(8,128)(2,1)} custom-call(bf16[1024,2048]{1,0:T(8,128)(2,1)} %all-gather.5.cloned.1.call-done.x_ref, bf16[1024,2048]{1,0:T(8,128)(2,1)} %dy_ref.17, bf16[1024,12288]{1,0:T(8,128)(2,1)} %get-tuple-element.39.kept_ref, bf16[2,768,2048]{2,1,0:T(8,128)(2,1)} %collective-permute-done.26.rest_0_), custom_call_target="tpu_custom_call" | custom-call | flops 6442450944 | bytes 20971520 | tf_op jit(solution)/shard_map/expert_weight_grads/pallas_call | solution.py:644
  979.7 4.0 slice.131
  984.3 13.8 %expert_weight_grads.11 = bf16[2,768,2048]{2,1,0:T(8,128)(2,1)} custom-call(bf16[1024,2048]{1,0:T(8,128)(2,1)} %all-gather.5.cloned.1.call-done.x_ref, bf16[1024,2048]{1,0:T(8,128)(2,1)} %dy_ref.17, bf16[1024,12288]{1,0:T(8,128)(2,1)} %get-tuple-element.39.kept_ref, bf16[2,768,2048]{2,1,0:T(8,128)(2,1)} %collective-permute-done.21.rest_0_), custom_call_target="tpu_custom_call" | custom-call | flops 6442450944 | bytes 20971520 | tf_op jit(solution)/shard_map/expert_weight_grads/pallas_call | solution.py:644
  998.1 4.1 slice.130
  1003.7 4.0 convolution_convert_fusion.4
  1008.0 15.6 %collective-permute-done.28 = bf16[1,768,2048]{2,1,0:T(8,128)(2,1)} collective-permute-done((bf16[1,768,2048]{2,1,0:T(8,128)(2,1)}, bf16[1,768,2048]{2,1,0:T(8,128)(2,1)}, u32[]{:S(2)}, u32[]{:S(2)}) %collective-permute-start.28) | collective-permute-done | bytes 3145760 | tf_op jit(solution)/shard_map/ppermute | solution.py:663
  1023.7 6.1 add_convert_fusion.2
  1031.2 6.2 add_convert_fusion.3
  1038.0 4.0 convolution_convert_fusion.3
  1042.6 13.9 %expert_weight_grads.9 = bf16[2,768,2048]{2,1,0:T(8,128)(2,1)} custom-call(bf16[1024,2048]{1,0:T(8,128)(2,1)} %all-gather.5.cloned.1.call-done.x_ref, bf16[1024,2048]{1,0:T(8,128)(2,1)} %dy_ref.17, bf16[1024,12288]{1,0:T(8,128)(2,1)} %get-tuple-element.39.kept_ref, bf16[2,768,2048]{2,1,0:T(8,128)(2,1)} %collective-permute-done.20.rest_0_), custom_call_target="tpu_custom_call" | custom-call | flops 6442450944 | bytes 20971520 | tf_op jit(solution)/shard_map/expert_weight_grads/pallas_call | solution.py:644
  1056.5 35.1 %collective-permute-done.27 = bf16[1,768,2048]{2,1,0:T(8,128)(2,1)} collective-permute-done((bf16[1,768,2048]{2,1,0:T(8,128)(2,1)}, bf16[1,768,2048]{2,1,0:T(8,128)(2,1)}, u32[]{:S(2)}, u32[]{:S(2)}) %collective-permute-start.27) | collective-permute-done | bytes 3145760 | tf_op jit(solution)/shard_map/ppermute | solution.py:663
  1091.7 78.7 %collective-permute-done.29 = bf16[1,768,2048]{2,1,0:T(8,128)(2,1)} collective-permute-done((bf16[1,768,2048]{2,1,0:T(8,128)(2,1)}, bf16[1,768,2048]{2,1,0:T(8,128)(2,1)}, u32[]{:S(2)}, u32[]{:S(2)}) %collective-permute-start.29) | collective-permute-done | bytes 3145760 | tf_op jit(solution)/shard_map/ppermute | solution.py:663
  1170.4 8.6 add_convert_fusion
  1179.0 3.0 fusion.46
  1182.0 4.0 copy.237
  1190.5 13.1 %all-reduce = bf16[8,128]{1,0:T(8,128)(2,1)S(1)} all-reduce(f32[8,128]{1,0:T(8,128)S(1)} %pad_maximum_fusion.5), channel_id=10, replica_groups=mesh['expert'=8,'tensor'=4] {'expert'}, use_global_device_ids=true, to_apply=%region_23.24.clone | all-reduce | flops 1024 | bytes 6144
  1204.8 15.3 %psum.8 = bf16[256,18]{0,1:T(8,128)(2,1)S(1)} all-reduce(f32[256,18]{0,1:T(8,128)} %reduce-scatter.26.cloned.1.call-done), channel_id=1, replica_groups=mesh['expert'=8,'tensor'=4] {'tensor'}, use_global_device_ids=true, to_apply=%region_26.27 | all-reduce | flops 4608 | bytes 27648 | tf_op jit(solution)/shard_map/psum | solution.py:800
  1221.3 8.6 reduce-scatter.18.cloned.1.call-done
  1229.9 45.1 %reduce-scatter.20.cloned.1.call-done = bf16[256,512]{1,0:T(8,128)(2,1)} async-done(((bf16[2048,512]{1,0:T(8,128)(2,1)}), bf16[256,512]{1,0:T(8,128)(2,1)}) %reduce-scatter.20.cloned.1.call-update) | async-done | bytes 262160 | tf_op jit(solution)/shard_map/reduce_scatter | solution.py:789
  1274.9 4.9 copy.256
  (242 shorter events, 91.6 us)
Async XLA Ops:
  7.2 301.6 %copy-start = (bf16[2048,16]{0,1:T(8,128)(2,1)S(1)}, bf16[2048,16]{0,1:T(8,128)(2,1)}, u32[]{:S(2)}) copy-start(bf16[2048,16]{0,1:T(8,128)(2,1)} %param.30) | copy-start | bytes 196612
  7.2 231.1 %reduce-scatter.10.cloned.1.call-start = ((), (), s32[]{:S(2)}) async-start(), calls=%async_computation.9 | async-start | bytes 5242880 | tf_op jit(solution)/shard_map/reduce_scatter | solution.py:729
  10.7 31.7 %copy-start.27 = (f32[1024]{0:T(1024)}, f32[1024]{0:T(1024)S(1)}, u32[]{:S(2)}) copy-start(f32[1024]{0:T(1024)S(1)} %add_rsqrt_fusion) | copy-start | bytes 12292
  10.7 5.7 copy-start.32
  20.6 37.4 %collective-permute-start = (f32[2,1024]{0,1:T(8,128)S(1)}, f32[2,1024]{0,1:T(8,128)}, u32[]{:S(2)}, u32[]{:S(2)}) collective-permute-start(f32[2,1024]{0,1:T(8,128)S(1)} %copy.210), channel_id=1, source_target_pairs={{0,1},{1,2},{2,3},{3,0},{4,5},{5,6},{6,7},{7,4},{8,9},{9,10},{10,1... | collective-permute-start | bytes 24584 | tf_op jit(solution)/shard_map/ppermute | solution.py:817
  22.2 35.8 %collective-permute-start.1 = (f32[2,1024]{0,1:T(8,128)S(1)}, f32[2,1024]{0,1:T(8,128)}, u32[]{:S(2)}, u32[]{:S(2)}) collective-permute-start(f32[2,1024]{0,1:T(8,128)S(1)} %copy.210), channel_id=1, source_target_pairs={{0,2},{1,3},{2,0},{3,1},{4,6},{5,7},{6,4},{7,5},{8,10},{9,11},{10,... | collective-permute-start | bytes 24584 | tf_op jit(solution)/shard_map/ppermute | solution.py:817
  22.5 44.3 %collective-permute-start.2 = (f32[2,1024]{0,1:T(8,128)S(1)}, f32[2,1024]{0,1:T(8,128)}, u32[]{:S(2)}, u32[]{:S(2)}) collective-permute-start(f32[2,1024]{0,1:T(8,128)S(1)} %copy.210), channel_id=1, source_target_pairs={{0,3},{1,0},{2,1},{3,2},{4,7},{5,4},{6,5},{7,6},{8,11},{9,8},{10,9... | collective-permute-start | bytes 24584 | tf_op jit(solution)/shard_map/ppermute | solution.py:817
  30.9 7.0 copy-start.35
  36.4 6.0 copy-start.12
  36.4 136.9 %collective-permute-start.7 = (bf16[2,768,2048]{2,1,0:T(8,128)(2,1)}, bf16[2,768,2048]{2,1,0:T(8,128)(2,1)}, u32[]{:S(2)}, u32[]{:S(2)}) collective-permute-start(bf16[2,768,2048]{2,1,0:T(8,128)(2,1)} %pad_maximum_fusion.rest_0_), channel_id=1, source_target_pairs={{0,8},{4,12},{8,0},{12,4},{16,24},{20,28},{24,16},{28,20},{1,9},{5... | collective-permute-start | bytes 18874376 | tf_op jit(solution)/shard_map/ppermute | solution.py:663
  93.6 234.5 %all-gather.5.cloned.1.call-start = ((), (), s32[]{:S(2)}) async-start(), calls=%async_computation.10 | async-start | bytes 5242880 | tf_op jit(solution)/shard_map/all_gather | solution.py:738
  94.0 138.7 %collective-permute-start.9 = (bf16[2,768,2048]{2,1,0:T(8,128)(2,1)}, bf16[2,768,2048]{2,1,0:T(8,128)(2,1)S(1)}, u32[]{:S(2)}, u32[]{:S(2)}) collective-permute-start(bf16[2,768,2048]{2,1,0:T(8,128)(2,1)} %pad_maximum_fusion.rest_0_), channel_id=1, source_target_pairs={{0,16},{4,20},{8,24},{12,28},{16,0},{20,4},{24,8},{28,12},{1,17},{... | collective-permute-start | bytes 18874376 | tf_op jit(solution)/shard_map/ppermute | solution.py:663
  177.2 63.0 %copy-start.26 = (f32[2048]{0:T(1024)S(1)}, f32[2048]{0:T(1024)}, u32[]{:S(2)}) copy-start(f32[2048]{0:T(1024)} %param.29) | copy-start | bytes 24580
  177.2 121.9 %collective-permute-start.11 = (bf16[1,768,2048]{2,1,0:T(8,128)(2,1)}, bf16[1,768,2048]{2,1,0:T(8,128)(2,1)S(1)}, u32[]{:S(2)}, u32[]{:S(2)}) collective-permute-start(bf16[1,768,2048]{2,1,0:T(8,128)(2,1)} %slice.121), channel_id=1, source_target_pairs={{0,16},{4,20},{8,24},{12,28},{16,0},{20,4},{24,8},{28,12},{1,17},{... | collective-permute-start | bytes 9437192 | tf_op jit(solution)/shard_map/ppermute | solution.py:663
  236.3 68.6 %collective-permute-start.12 = (bf16[1,768,2048]{2,1,0:T(8,128)(2,1)}, bf16[1,768,2048]{2,1,0:T(8,128)(2,1)}, u32[]{:S(2)}, u32[]{:S(2)}) collective-permute-start(bf16[1,768,2048]{2,1,0:T(8,128)(2,1)} %slice.122), channel_id=1, source_target_pairs={{0,8},{4,12},{8,0},{12,4},{16,24},{20,28},{24,16},{28,20},{1,9},{5... | collective-permute-start | bytes 9437192 | tf_op jit(solution)/shard_map/ppermute | solution.py:663
  237.8 90.2 %collective-permute-start.6 = (bf16[2,768,2048]{2,1,0:T(8,128)(2,1)}, bf16[2,768,2048]{2,1,0:T(8,128)(2,1)}, u32[]{:S(2)}, u32[]{:S(2)}) collective-permute-start(bf16[2,768,2048]{2,1,0:T(8,128)(2,1)} %pad_maximum_fusion.rest_0_), channel_id=1, source_target_pairs={{0,4},{4,0},{8,12},{12,8},{16,20},{20,16},{24,28},{28,24},{1,5},{5... | collective-permute-start | bytes 18874376 | tf_op jit(solution)/shard_map/ppermute | solution.py:663
  237.8 90.2 %collective-permute-start.10 = (bf16[2,768,2048]{2,1,0:T(8,128)(2,1)}, bf16[2,768,2048]{2,1,0:T(8,128)(2,1)}, u32[]{:S(2)}, u32[]{:S(2)}) collective-permute-start(bf16[2,768,2048]{2,1,0:T(8,128)(2,1)} %copy-done.15), channel_id=1, source_target_pairs={{0,4},{4,0},{8,12},{12,8},{16,20},{20,16},{24,28},{28,24},{1,5},{5... | collective-permute-start | bytes 18874376 | tf_op jit(solution)/shard_map/ppermute | solution.py:663
  238.3 89.7 %collective-permute-start.8 = (bf16[2,768,2048]{2,1,0:T(8,128)(2,1)}, bf16[2,768,2048]{2,1,0:T(8,128)(2,1)}, u32[]{:S(2)}, u32[]{:S(2)}) collective-permute-start(bf16[2,768,2048]{2,1,0:T(8,128)(2,1)} %collective-permute-done.7.rest_2_), channel_id=1, source_target_pairs={{0,4},{4,0},{8,12},{12,8},{16,20},{20,16},{24,28},{28,24},{1,5},{5... | collective-permute-start | bytes 18874376 | tf_op jit(solution)/shard_map/ppermute | solution.py:663
  243.2 286.9 %reduce-scatter.14.cloned.1.call-start = ((), (), s32[]{:S(2)}) async-start(), calls=%async_computation.13 | async-start | bytes 5242880 | tf_op jit(solution)/shard_map/reduce_scatter | solution.py:758
  301.1 7.7 copy-start.24
  301.1 7.7 copy-start.8
  301.1 11.0 copy-start.25
  308.8 19.2 %collective-permute-start.13 = (bf16[2,768,2048]{2,1,0:T(8,128)(2,1)}, bf16[2,768,2048]{2,1,0:T(8,128)(2,1)}, u32[]{:S(2)}, u32[]{:S(2)}) collective-permute-start(bf16[2,768,2048]{2,1,0:T(8,128)(2,1)} %constant_dynamic-update-slice_fusion.12.rest_6_), channel_id=1, source_target_pairs={{0,4},{4,0},{8,12},{12,8},{16,20},{20,16},{24,28},{28,24},{1,5},{5... | collective-permute-start | bytes 18874376 | tf_op jit(solution)/shard_map/ppermute | solution.py:663
  311.6 4.8 collective-permute-start.3
  316.3 5.0 collective-permute-start.4
  321.3 3.7 collective-permute-start.5
  448.8 161.4 %reduce-scatter.12.cloned.1.call-start = ((), (), s32[]{:S(2)}) async-start(), calls=%async_computation.11 | async-start | bytes 5242880 | tf_op jit(solution)/shard_map/reduce_scatter | solution.py:768
  449.3 245.7 %all-gather.9.cloned.1.call-start = ((), (), s32[]{:S(2)}) async-start(), calls=%async_computation.14 | async-start | bytes 5242880 | tf_op jit(solution)/shard_map/all_gather | solution.py:762
  458.9 6.8 collective-permute-start.14
  462.6 5.0 collective-permute-start.15
  462.6 5.0 collective-permute-start.16
  615.6 260.6 %reduce-scatter.16.cloned.1.call-start = ((), (), s32[]{:S(2)}) async-start(), calls=%async_computation.15 | async-start | bytes 5242880 | tf_op jit(solution)/shard_map/reduce_scatter | solution.py:777
  732.1 51.6 %copy-start.6 = (f32[1024,512]{1,0:T(8,128)S(1)}, f32[1024,512]{1,0:T(8,128)}, u32[]{:S(2)}) copy-start(f32[1024,512]{1,0:T(8,128)} %copy.216.q_ref) | copy-start | bytes 6291460
  734.9 48.9 %copy-start.7 = (f32[1024,512]{1,0:T(8,128)S(1)}, f32[1024,512]{1,0:T(8,128)}, u32[]{:S(2)}) copy-start(f32[1024,512]{1,0:T(8,128)} %copy.217.k_ref) | copy-start | bytes 6291460
  734.9 37.5 %collective-permute-start.17 = (f32[2,1024]{0,1:T(8,128)}, f32[2,1024]{0,1:T(8,128)S(1)}, u32[]{:S(2)}, u32[]{:S(2)}) collective-permute-start(f32[2,1024]{0,1:T(8,128)} %bitcast.86), channel_id=1, source_target_pairs={{0,1},{1,2},{2,3},{3,0},{4,5},{5,6},{6,7},{7,4},{8,9},{9,10},{10,1... | collective-permute-start | bytes 24584 | tf_op jit(solution)/shard_map/ppermute | solution.py:817
  735.3 37.0 %collective-permute-start.18 = (f32[2,1024]{0,1:T(8,128)}, f32[2,1024]{0,1:T(8,128)S(1)}, u32[]{:S(2)}, u32[]{:S(2)}) collective-permute-start(f32[2,1024]{0,1:T(8,128)} %bitcast.87), channel_id=1, source_target_pairs={{0,2},{1,3},{2,0},{3,1},{4,6},{5,7},{6,4},{7,5},{8,10},{9,11},{10,... | collective-permute-start | bytes 24584 | tf_op jit(solution)/shard_map/ppermute | solution.py:817
  736.9 45.2 %collective-permute-start.19 = (f32[2,1024]{0,1:T(8,128)}, f32[2,1024]{0,1:T(8,128)S(1)}, u32[]{:S(2)}, u32[]{:S(2)}) collective-permute-start(f32[2,1024]{0,1:T(8,128)} %bitcast.88), channel_id=1, source_target_pairs={{0,3},{1,0},{2,1},{3,2},{4,7},{5,4},{6,5},{7,6},{8,11},{9,8},{10,9... | collective-permute-start | bytes 24584 | tf_op jit(solution)/shard_map/ppermute | solution.py:817
  797.5 78.8 %copy-start.23 = (f32[2048]{0:T(1024)S(1)}, f32[2048]{0:T(1024)}, u32[]{:S(2)}) copy-start(f32[2048]{0:T(1024)} %param.28) | copy-start | bytes 24580
  797.6 81.8 %copy-start.9 = (f32[256,2048]{1,0:T(8,128)S(1)}, f32[256,2048]{1,0:T(8,128)}, u32[]{:S(2)}) copy-start(f32[256,2048]{1,0:T(8,128)} %get-tuple-element.152) | copy-start | bytes 6291460
  797.6 392.8 %all-gather.7.cloned.1.call-start = ((), (), s32[]{:S(2)}) async-start(), calls=%async_computation.12 | async-start | bytes 5242880 | tf_op jit(solution)/shard_map/all_gather | solution.py:769
  798.3 406.5 %reduce-scatter.26.cloned.1.call-start = ((), (), s32[]{:S(2)}) async-start(), calls=%async_computation.21 | async-start | bytes 221184 | tf_op jit(solution)/shard_map/reduce_scatter | solution.py:789
  879.3 342.0 %all-gather.11.cloned.1.call-start = ((), (), s32[]{:S(2)}) async-start(), calls=%async_computation.16 | async-start | bytes 5242880 | tf_op jit(solution)/shard_map/all_gather | solution.py:780
  882.4 338.9 %reduce-scatter.24.cloned.1.call-start = ((), (), s32[]{:S(2)}) async-start(), calls=%async_computation.20 | async-start | bytes 2359296 | tf_op jit(solution)/shard_map/reduce_scatter | solution.py:789
  895.5 31.3 %collective-permute-start.22 = (bf16[2,768,2048]{2,1,0:T(8,128)(2,1)}, bf16[2,768,2048]{2,1,0:T(8,128)(2,1)}, u32[]{:S(2)}, u32[]{:S(2)}) collective-permute-start(bf16[2,768,2048]{2,1,0:T(8,128)(2,1)} %expert_weight_grads.12), channel_id=1, source_target_pairs={{0,4},{4,0},{8,12},{12,8},{16,20},{20,16},{24,28},{28,24},{1,5},{5... | collective-permute-start | bytes 18874376 | tf_op jit(solution)/shard_map/ppermute | solution.py:663
  907.8 12.9 %copy-start.34 = (bf16[1024,512]{1,0:T(8,128)(2,1)S(1)}, bf16[1024,512]{1,0:T(8,128)(2,1)}, u32[]{:S(2)}) copy-start(bf16[1024,512]{1,0:T(8,128)(2,1)} %get-tuple-element.27) | copy-start | bytes 3145732
  907.8 58.2 %collective-permute-start.26 = (bf16[2,768,2048]{2,1,0:T(8,128)(2,1)}, bf16[2,768,2048]{2,1,0:T(8,128)(2,1)}, u32[]{:S(2)}, u32[]{:S(2)}) collective-permute-start(bf16[2,768,2048]{2,1,0:T(8,128)(2,1)} %expert_weight_grads.14), channel_id=1, source_target_pairs={{0,4},{4,0},{8,12},{12,8},{16,20},{20,16},{24,28},{28,24},{1,5},{5... | collective-permute-start | bytes 18874376 | tf_op jit(solution)/shard_map/ppermute | solution.py:663
  920.6 63.7 %collective-permute-start.21 = (bf16[2,768,2048]{2,1,0:T(8,128)(2,1)}, bf16[2,768,2048]{2,1,0:T(8,128)(2,1)}, u32[]{:S(2)}, u32[]{:S(2)}) collective-permute-start(bf16[2,768,2048]{2,1,0:T(8,128)(2,1)} %expert_weight_grads.10), channel_id=1, source_target_pairs={{0,4},{4,0},{8,12},{12,8},{16,20},{20,16},{24,28},{28,24},{1,5},{5... | collective-permute-start | bytes 18874376 | tf_op jit(solution)/shard_map/ppermute | solution.py:663
  926.7 294.6 %reduce-scatter.22.cloned.1.call-start = ((), (), s32[]{:S(2)}) async-start(), calls=%async_computation.19 | async-start | bytes 2359296 | tf_op jit(solution)/shard_map/reduce_scatter | solution.py:789
  940.5 6.8 copy-start.3
  940.5 6.8 copy-start.19
  951.4 278.5 %reduce-scatter.18.cloned.1.call-start = ((), (), s32[]{:S(2)}) async-start(), calls=%async_computation.17 | async-start | bytes 2359296 | tf_op jit(solution)/shard_map/reduce_scatter | solution.py:789
  951.6 72.1 %collective-permute-start.28 = (bf16[1,768,2048]{2,1,0:T(8,128)(2,1)}, bf16[1,768,2048]{2,1,0:T(8,128)(2,1)}, u32[]{:S(2)}, u32[]{:S(2)}) collective-permute-start(bf16[1,768,2048]{2,1,0:T(8,128)(2,1)} %get-tuple-element.160), channel_id=1, source_target_pairs={{0,16},{4,20},{8,24},{12,28},{16,0},{20,4},{24,8},{28,12},{1,17},{... | collective-permute-start | bytes 9437192 | tf_op jit(solution)/shard_map/ppermute | solution.py:663
  952.2 79.0 %collective-permute-start.23 = (bf16[1,768,2048]{2,1,0:T(8,128)(2,1)}, bf16[1,768,2048]{2,1,0:T(8,128)(2,1)}, u32[]{:S(2)}, u32[]{:S(2)}) collective-permute-start(bf16[1,768,2048]{2,1,0:T(8,128)(2,1)} %get-tuple-element.161), channel_id=1, source_target_pairs={{0,8},{4,12},{8,0},{12,4},{16,24},{20,28},{24,16},{28,20},{1,9},{5... | collective-permute-start | bytes 9437192 | tf_op jit(solution)/shard_map/ppermute | solution.py:663
  965.9 76.7 %collective-permute-start.20 = (bf16[2,768,2048]{2,1,0:T(8,128)(2,1)}, bf16[2,768,2048]{2,1,0:T(8,128)(2,1)}, u32[]{:S(2)}, u32[]{:S(2)}) collective-permute-start(bf16[2,768,2048]{2,1,0:T(8,128)(2,1)} %expert_weight_grads.8), channel_id=1, source_target_pairs={{0,4},{4,0},{8,12},{12,8},{16,20},{20,16},{24,28},{28,24},{1,5},{5... | collective-permute-start | bytes 18874376 | tf_op jit(solution)/shard_map/ppermute | solution.py:663
  983.7 107.9 %collective-permute-start.27 = (bf16[1,768,2048]{2,1,0:T(8,128)(2,1)}, bf16[1,768,2048]{2,1,0:T(8,128)(2,1)}, u32[]{:S(2)}, u32[]{:S(2)}) collective-permute-start(bf16[1,768,2048]{2,1,0:T(8,128)(2,1)} %slice.131), channel_id=1, source_target_pairs={{0,8},{4,12},{8,0},{12,4},{16,24},{20,28},{24,16},{28,20},{1,9},{5... | collective-permute-start | bytes 9437192 | tf_op jit(solution)/shard_map/ppermute | solution.py:663
  998.1 5.6 copy-start.4
  998.1 5.6 copy-start.21
  1002.2 89.4 %collective-permute-start.25 = (bf16[1,768,2048]{2,1,0:T(8,128)(2,1)}, bf16[1,768,2048]{2,1,0:T(8,128)(2,1)}, u32[]{:S(2)}, u32[]{:S(2)}) collective-permute-start(bf16[1,768,2048]{2,1,0:T(8,128)(2,1)} %slice.130), channel_id=1, source_target_pairs={{0,16},{4,20},{8,24},{12,28},{16,0},{20,4},{24,8},{28,12},{1,17},{... | collective-permute-start | bytes 9437192 | tf_op jit(solution)/shard_map/ppermute | solution.py:663
  1007.8 267.2 %reduce-scatter.20.cloned.1.call-start = ((), (), s32[]{:S(2)}) async-start(), calls=%async_computation.18 | async-start | bytes 2359296 | tf_op jit(solution)/shard_map/reduce_scatter | solution.py:789
  1029.7 8.2 copy-start.5
  1029.7 8.2 copy-start.17
  1029.7 140.6 %collective-permute-start.29 = (bf16[1,768,2048]{2,1,0:T(8,128)(2,1)}, bf16[1,768,2048]{2,1,0:T(8,128)(2,1)}, u32[]{:S(2)}, u32[]{:S(2)}) collective-permute-start(bf16[1,768,2048]{2,1,0:T(8,128)(2,1)} %add_convert_fusion.2), channel_id=1, source_target_pairs={{0,8},{4,12},{8,0},{12,4},{16,24},{20,28},{24,16},{28,20},{1,9},{5... | collective-permute-start | bytes 9437192 | tf_op jit(solution)/shard_map/ppermute | solution.py:663
  1037.4 133.0 %collective-permute-start.24 = (bf16[1,768,2048]{2,1,0:T(8,128)(2,1)}, bf16[1,768,2048]{2,1,0:T(8,128)(2,1)}, u32[]{:S(2)}, u32[]{:S(2)}) collective-permute-start(bf16[1,768,2048]{2,1,0:T(8,128)(2,1)} %add_convert_fusion.3), channel_id=1, source_target_pairs={{0,16},{4,20},{8,24},{12,28},{16,0},{20,4},{24,8},{28,12},{1,17},{... | collective-permute-start | bytes 9437192 | tf_op jit(solution)/shard_map/ppermute | solution.py:663
  1274.9 7.0 copy-start.1
  (16 other events, 51.3 us)
Sparse Core Ops, SparseCore 0:
  93.7 79.4 reduce-scatter.9
  243.3 81.6 all-gather.4
  448.9 81.2 reduce-scatter.13
  532.9 77.2 reduce-scatter.11
  615.8 79.2 all-gather.8
  797.7 78.5 reduce-scatter.15
  877.9 79.2 all-gather.6
  960.2 41.2 reduce-scatter.25
  1003.2 79.3 all-gather.10
  1086.6 49.8 reduce-scatter.23
  1140.4 44.1 reduce-scatter.21
  1188.6 41.2 reduce-scatter.17
  1233.7 41.1 reduce-scatter.19

commit v2 on v1

--- a/solution.py
+++ b/solution.py
@@ -8,6 +8,8 @@
 from jax.sharding import PartitionSpec as P
 
 HEAD_DIM = 128
+EXPERT = "expert"
+TENSOR = "tensor"
 TOP = 8
 
 
@@ -162,7 +164,7 @@
     rows, width = tokens.shape
     local = w_query.shape[1]
     heads_here = local // HEAD_DIM
-    groups = lax.axis_size("expert")
+    groups = lax.axis_size(EXPERT)
     experts_here = w_gate.shape[0]
     experts_all = experts_here * groups
     capacity = max(2, 3 * rows * TOP // (4 * experts_all))
@@ -177,7 +179,7 @@
     key_raw = jnp.dot(attn_in, w_key, preferred_element_type=jnp.float32)
     value_raw = jnp.dot(attn_in, w_value, preferred_element_type=jnp.float32)
     query_total, key_total = lax.psum(
-        (jnp.sum(query_raw * query_raw, axis=-1), jnp.sum(key_raw * key_raw, axis=-1)), "tensor"
+        (jnp.sum(query_raw * query_raw, axis=-1), jnp.sum(key_raw * key_raw, axis=-1)), TENSOR
     )
     query_inverse = lax.rsqrt(query_total / width + EPS)[:, None]
     key_inverse = lax.rsqrt(key_total / width + EPS)[:, None]
@@ -192,7 +194,7 @@
     context_low = context.reshape(rows, local).astype(jnp.bfloat16)
     attn = lax.psum(
         jnp.dot(context_low, w_output, preferred_element_type=jnp.float32).astype(jnp.bfloat16),
-        "tensor",
+        TENSOR,
     ).astype(jnp.float32)
     hidden_in = inputs + attn
     moe_in, inverse_moe = norm_rows(hidden_in, moe_gain)
@@ -220,7 +222,7 @@
     send_rows = jnp.where(filled, moe_low[source_row], jnp.zeros((), jnp.bfloat16)).reshape(
         groups, experts_here * capacity, width
     )
-    arrived = lax.all_to_all(send_rows, "expert", split_axis=0, concat_axis=0, tiled=True)
+    arrived = lax.all_to_all(send_rows, EXPERT, split_axis=0, concat_axis=0, tiled=True)
     arrived = arrived.reshape(groups, experts_here, capacity, width)
     gate_pre = jnp.einsum("secd,edf->secf", arrived, w_gate, preferred_element_type=jnp.float32)
     up_pre = jnp.einsum("secd,edf->secf", arrived, w_up, preferred_element_type=jnp.float32)
@@ -230,10 +232,10 @@
         "secf,efd->secd", hidden, w_down, preferred_element_type=jnp.float32
     ).astype(jnp.bfloat16)
     dy_rows = jnp.where(filled, cotangent[source_row], jnp.zeros((), jnp.bfloat16))
-    returned = lax.all_to_all(partial_value, "expert", split_axis=0, concat_axis=0, tiled=True)
+    returned = lax.all_to_all(partial_value, EXPERT, split_axis=0, concat_axis=0, tiled=True)
     returned = returned.reshape(experts_all * capacity, width).astype(jnp.float32)
     moe_part = jax.ops.segment_sum(returned * gate_of[:, None], source_row, num_segments=rows)
-    moe = lax.psum(moe_part.astype(jnp.bfloat16), "tensor").astype(jnp.float32)
+    moe = lax.psum(moe_part.astype(jnp.bfloat16), TENSOR).astype(jnp.float32)
     row_dots = jnp.sum(dy_rows.astype(jnp.float32) * returned, axis=-1)
     out = (hidden_in + moe).astype(jnp.bfloat16)
     grad_gate = jnp.take(row_dots, target_slot, mode="fill", fill_value=0.0).reshape(rows, TOP)
@@ -246,7 +248,7 @@
         .astype(jnp.bfloat16)
         .reshape(groups, experts_here * capacity, width)
     )
-    grad_arrived = lax.all_to_all(grad_rows, "expert", split_axis=0, concat_axis=0, tiled=True)
+    grad_arrived = lax.all_to_all(grad_rows, EXPERT, split_axis=0, concat_axis=0, tiled=True)
     grad_arrived = grad_arrived.reshape(groups, experts_here, capacity, width)
     grad_hidden = jnp.einsum(
         "secd,efd->secf", grad_arrived, w_down, preferred_element_type=jnp.float32
@@ -274,7 +276,7 @@
     ).astype(jnp.bfloat16)
     back_rows = lax.all_to_all(
         grad_in_rows.reshape(groups, experts_here * capacity, width),
-        "expert",
+        EXPERT,
         split_axis=0,
         concat_axis=0,
         tiled=True,
@@ -282,8 +284,8 @@
     back_rows = back_rows.reshape(experts_all * capacity, width).astype(jnp.float32)
     moe_back = jax.ops.segment_sum(back_rows, source_row, num_segments=rows)
     grad_moe_in, grad_router_rows = (
-        lax.psum((moe_back + router_back).astype(jnp.bfloat16), "tensor").astype(jnp.float32),
-        lax.psum(router_part.astype(jnp.bfloat16), "tensor").astype(jnp.float32),
+        lax.psum((moe_back + router_back).astype(jnp.bfloat16), TENSOR).astype(jnp.float32),
+        lax.psum(router_part.astype(jnp.bfloat16), TENSOR).astype(jnp.float32),
     )
     grad_norm_moe, grad_moe_gain = norm_back(hidden_in, inverse_moe, moe_gain, grad_moe_in)
     grad_hidden_in = cotangent.astype(jnp.float32) + grad_norm_moe
@@ -305,7 +307,7 @@
     key_scaled = grad_key_normed * key_gain
     query_inner, key_inner = lax.psum(
         (jnp.sum(query_raw * query_scaled, axis=-1), jnp.sum(key_raw * key_scaled, axis=-1)),
-        "tensor",
+        TENSOR,
     )
     grad_query_raw = (
         query_inverse * query_scaled
@@ -330,36 +332,36 @@
     terms_in = terms_in + jnp.einsum(
         "tf,df->td", value_low, w_value, preferred_element_type=jnp.float32
     )
-    grad_normed = lax.psum(terms_in.astype(jnp.bfloat16), "tensor").astype(jnp.float32)
+    grad_normed = lax.psum(terms_in.astype(jnp.bfloat16), TENSOR).astype(jnp.float32)
     grad_norm_in, grad_attn_gain = norm_back(inputs, inverse_in, attn_gain, grad_normed)
     grad_input = (grad_hidden_in + grad_norm_in).astype(jnp.bfloat16)
     sums = (
         lax.psum_scatter(
-            grad_w_query.astype(jnp.bfloat16), "expert", scatter_dimension=0, tiled=True
+            grad_w_query.astype(jnp.bfloat16), EXPERT, scatter_dimension=0, tiled=True
         ).astype(jnp.float32),
         lax.psum_scatter(
-            grad_w_key.astype(jnp.bfloat16), "expert", scatter_dimension=0, tiled=True
+            grad_w_key.astype(jnp.bfloat16), EXPERT, scatter_dimension=0, tiled=True
         ).astype(jnp.float32),
         lax.psum_scatter(
-            grad_w_value.astype(jnp.bfloat16), "expert", scatter_dimension=0, tiled=True
+            grad_w_value.astype(jnp.bfloat16), EXPERT, scatter_dimension=0, tiled=True
         ).astype(jnp.float32),
         lax.psum_scatter(
-            grad_w_output.astype(jnp.bfloat16), "expert", scatter_dimension=1, tiled=True
+            grad_w_output.astype(jnp.bfloat16), EXPERT, scatter_dimension=1, tiled=True
         ).astype(jnp.float32),
         lax.psum_scatter(
-            grad_query_gain.astype(jnp.bfloat16), "expert", scatter_dimension=0, tiled=True
+            grad_query_gain.astype(jnp.bfloat16), EXPERT, scatter_dimension=0, tiled=True
         ).astype(jnp.float32),
         lax.psum_scatter(
-            grad_key_gain.astype(jnp.bfloat16), "expert", scatter_dimension=0, tiled=True
+            grad_key_gain.astype(jnp.bfloat16), EXPERT, scatter_dimension=0, tiled=True
         ).astype(jnp.float32),
         lax.psum_scatter(
-            grad_attn_gain.astype(jnp.bfloat16), "expert", scatter_dimension=0, tiled=True
+            grad_attn_gain.astype(jnp.bfloat16), EXPERT, scatter_dimension=0, tiled=True
         ).astype(jnp.float32),
         lax.psum_scatter(
-            grad_moe_gain.astype(jnp.bfloat16), "expert", scatter_dimension=0, tiled=True
+            grad_moe_gain.astype(jnp.bfloat16), EXPERT, scatter_dimension=0, tiled=True
         ).astype(jnp.float32),
         lax.psum_scatter(
-            grad_router_rows.astype(jnp.bfloat16), "expert", scatter_dimension=0, tiled=True
+            grad_router_rows.astype(jnp.bfloat16), EXPERT, scatter_dimension=0, tiled=True
         ).astype(jnp.float32),
     )
     lows = tuple((item.astype(jnp.bfloat16) for item in sums))
@@ -390,6 +392,9 @@
 COLUMN_TILE = 512
 ROW_TILE = 512
 QUERY_TILE = 256
+EXPERT_STEP = 2
+HIDDEN_TILE = 256
+LANES = 128
 
 
 def mul(left, right, dims=NN):
@@ -412,6 +417,47 @@
     scores = jnp.where(allowed, scores, NEG)
     raised = jnp.exp(scores - jnp.max(scores, axis=-1, keepdims=True))
     return raised * (1.0 / jnp.sum(raised, axis=-1, keepdims=True))
+
+
+ANYWHERE = pl.BlockSpec(memory_space=pl.ANY)
+
+
+def front_kernel(tokens_ref, gain_ref, wq_ref, wk_ref, wv_ref, *refs):
+    low_ref, inverse_ref, q_ref, k_ref, v_ref, sums_ref = refs[-6:]
+    rows = tokens_ref[...].astype(F32)
+    inverse = lax.rsqrt(jnp.mean(rows * rows, axis=1, keepdims=True) + EPS)
+    low = (rows * inverse * gain_ref[...]).astype(BF)
+    low_ref[...] = low
+    inverse_ref[...] = inverse
+    sums = []
+    for w_ref, out_ref in ((wq_ref, q_ref), (wk_ref, k_ref)):
+        raw = mul(low, w_ref[...])
+        out_ref[...] = raw
+        sums.append(jnp.sum(raw * raw, axis=1, keepdims=True))
+    v_ref[...] = mul(low, wv_ref[...]).astype(BF)
+    sums_ref[...] = jnp.concatenate(sums, axis=1)
+
+
+def front_call(tokens, gain, w_query, w_key, w_value, waits):
+    rows, width = tokens.shape
+    local = w_query.shape[1]
+    tile = min(HIDDEN_TILE, rows)
+    row = lambda c: pl.BlockSpec((tile, c), lambda i: (i, 0))
+    shape = jax.ShapeDtypeStruct
+    return pl.pallas_call(
+        front_kernel,
+        grid=(rows // tile,),
+        in_specs=[row(width), whole((1, width))] + [whole(w_query.shape)] * 3 + [ANYWHERE] * len(waits),
+        out_specs=[row(width), row(1)] + [row(local)] * 3 + [row(2)],
+        out_shape=[shape((rows, width), BF), shape((rows, 1), F32)]
+        + [shape((rows, local), F32)] * 2
+        + [shape((rows, local), BF), shape((rows, 2), F32)],
+        compiler_params=kernel_params(),
+        cost_estimate=pl.CostEstimate(
+            flops=6 * rows * width * local, bytes_accessed=4 * rows * width + 6 * width * local, transcendentals=0
+        ),
+        name="front_rows",
+    )(tokens, gain, w_query, w_key, w_value, *waits)
 
 
 def attention_kernel(
@@ -434,9 +480,9 @@
 
 def attention_back_kernel(
     q_ref, k_ref, v_ref, qi_ref, ki_ref, qg_ref, kg_ref, cos_ref, sin_ref, row_ref, col_ref,
-    qh_ref, kh_ref, dctx_ref,
-    dq_ref, dk_ref, dv_ref, inner_ref, dqg_ref, dkg_ref, dq_total, dk_total, dv_total,
+    qh_ref, kh_ref, dctx_ref, *rest,
 ):
+    dq_ref, dk_ref, dv_ref, inner_ref, dqg_ref, dkg_ref, dq_total, dk_total, dv_total = rest[-9:]
     rows, size = q_ref.shape
     scale = size**-0.5
     tile = min(QUERY_TILE, rows)
@@ -495,13 +541,13 @@
     )(*operands)
 
 
-def attention_back_call(operands, rows, local):
+def attention_back_call(operands, rows, local, waits=()):
     head, gain, specs = head_specs(rows)
     heads = local // HEAD_DIM
     return pl.pallas_call(
         attention_back_kernel,
         grid=(heads,),
-        in_specs=specs + [head] * 3,
+        in_specs=specs + [head] * 3 + [ANYWHERE] * len(waits),
         out_specs=[head] * 3 + [pl.BlockSpec((1, rows, 2), lambda h: (h, 0, 0)), gain, gain],
         out_shape=[jax.ShapeDtypeStruct((rows, local), F32)] * 2
         + [jax.ShapeDtypeStruct((rows, local), BF), jax.ShapeDtypeStruct((heads, rows, 2), F32)]
@@ -512,47 +558,139 @@
             flops=8 * rows * rows * local, bytes_accessed=24 * rows * local, transcendentals=rows * rows * heads // 2
         ),
         name="attention_rows_back",
-    )(*operands)
-
-
-def rows_kernel(sets, experts, x_ref, dy_ref, gate_ref, *rest):
-    w_refs = rest[:sets]
-    moe_ref, dx_ref, kept_ref, dot_ref, held, moe, dx, sems = rest[sets:]
+    )(*operands, *waits)
+
+
+def hidden_kernel(pieces, core_ref, tokens_ref, gain_ref, *refs):
+    ctx_refs, w_ref = refs[:pieces], refs[pieces]
+    hidden_ref, low_ref, inverse_ref = refs[pieces + 1 :]
+    local = ctx_refs[0].shape[1]
+    half = local // 2
+    near = pl.ds(pl.multiple_of(core_ref[0] * half, half), half)
+    far = pl.ds(pl.multiple_of((1 - core_ref[0]) * half, half), half)
+    total = tokens_ref[...].astype(F32) + mul(ctx_refs[0][...], w_ref[:local])
+    for number in range(1, pieces):
+        mine = local + (number - 1) * half
+        other = mine + (pieces - 1) * half
+        total = total + mul(ctx_refs[number][:, near], w_ref[mine : mine + half])
+        total = total + mul(ctx_refs[number][:, far], w_ref[other : other + half])
+    inverse = lax.rsqrt(jnp.mean(total * total, axis=1, keepdims=True) + EPS)
+    hidden_ref[...] = total
+    low_ref[...] = (total * inverse * gain_ref[...]).astype(BF)
+    inverse_ref[...] = inverse
+
+
+def hidden_call(core, tokens, gain, context, weights):
+    rows, width = tokens.shape
+    tile = min(HIDDEN_TILE, rows)
+    row = lambda c: pl.BlockSpec((tile, c), lambda i: (i, 0))
+    return pl.pallas_call(
+        functools.partial(hidden_kernel, len(context)),
+        grid=(rows // tile,),
+        in_specs=[pl.BlockSpec(memory_space=pltpu.SMEM), row(width), whole((1, width))]
+        + [row(context[0].shape[1])] * len(context)
+        + [whole(weights.shape)],
+        out_specs=[row(width), row(width), row(1)],
+        out_shape=[
+            jax.ShapeDtypeStruct((rows, width), F32),
+            jax.ShapeDtypeStruct((rows, width), BF),
+            jax.ShapeDtypeStruct((rows, 1), F32),
+        ],
+        compiler_params=kernel_params(),
+        cost_estimate=pl.CostEstimate(
+            flops=2 * rows * width * width, bytes_accessed=10 * rows * width + 2 * width * width, transcendentals=0
+        ),
+        name="hidden_rows",
+    )(core, tokens, gain, *context, weights)
+
+
+def rows_kernel(arrays, first_number, each_device, added, waits, *refs):
+    parts = 2
+    core_ref, router_ref = refs[:2]
+    x_refs, dy_refs, carried_refs = refs[2:4], refs[4:6], refs[6:8]
+    w_refs = refs[8 : 8 + arrays]
+    rest = refs[8 + arrays :]
+    if added:
+        before, rest = rest[:4], rest[4:]
+    rest = rest[waits:]
+    moe_refs, dx_refs = rest[:2], rest[2:4]
+    kept_ref, share_ref, held, moe, dx, gates, dots, sems, before_sems = rest[4:]
     step = pl.program_id(0)
     slot = lax.rem(step, 2)
-    rows, width = x_ref.shape
+    blocks, _, own, width = x_refs[0].shape
+    rows = blocks * own
+    experts = held.shape[1]
+
+    def take(ref, first, count):
+        part = ref[first // own : (first + count) // own, 0]
+        return part.reshape(count, part.shape[-1])
+
     hid = held.shape[2] // 3
+    tile = min(ROW_TILE, rows)
+    each = w_refs[0].shape[0] // experts
+    sets = each * arrays
+
+    def source(number):
+        return w_refs[number // each].at[pl.ds(number % each * experts, experts)]
 
     def fetch(index, place):
         for number in range(sets):
 
             @pl.when(index == number)
             def _():
-                pltpu.make_async_copy(w_refs[number], held.at[place], sems.at[place]).start()
+                pltpu.make_async_copy(source(number), held.at[place], sems.at[place]).start()
 
     @pl.when(step == 0)
     def _():
         fetch(0, 0)
-        moe[...] = jnp.zeros_like(moe)
-        dx[...] = jnp.zeros_like(dx)
+        earlier = []
+        if added:
+            for number, place in enumerate((*moe_refs, *dx_refs)):
+                earlier.append(pltpu.make_async_copy(before[number], place, before_sems.at[number]))
+                earlier[-1].start()
+        for number in range(parts):
+            here = slice(number * rows, (number + 1) * rows)
+            logits = mul(take(x_refs[number], 0, rows), router_ref[...])
+            raised = jnp.exp(logits - jnp.max(logits, axis=1, keepdims=True))
+            shares = raised / jnp.sum(raised, axis=1, keepdims=True)
+            if number == 0:
+                share_ref[...] = shares
+            gates[here] = shares * take(carried_refs[number], 0, rows).astype(F32)
+        for copy in earlier:
+            copy.wait()
+        if added:
+            for number in range(parts):
+                here = slice(number * rows, (number + 1) * rows)
+                moe[here] = moe_refs[number][...].astype(F32)
+                dx[here] = dx_refs[number][:, :width].astype(F32)
+                dots[here] = dx_refs[number][:, width:].astype(F32)
+        else:
+            moe[...] = jnp.zeros_like(moe)
+            dx[...] = jnp.zeros_like(dx)
+            dots[...] = jnp.zeros_like(dots)
 
     @pl.when(step + 1 < sets)
     def _():
         fetch(step + 1, 1 - slot)
 
-    pltpu.make_async_copy(w_refs[0], held.at[slot], sems.at[slot]).wait()
+    pltpu.make_async_copy(source(0), held.at[slot], sems.at[slot]).wait()
     for one in range(experts):
         base = one * 3 * hid
-        for first in range(0, rows, ROW_TILE):
-            here = slice(first, first + ROW_TILE)
-            both = mul(x_ref[here], held[slot, one, hid:], NT)
-            back = mul(dy_ref[here], held[slot, one, :hid], NT)
+        chip = lax.rem(step, each) * experts + one
+        index = (chip * 2 + core_ref[0]) * each_device + first_number + step // each
+        for first in range(0, parts * rows, tile):
+            here = slice(first, first + tile)
+            both = mul(take(x_refs[first // rows], first % rows, tile), held[slot, one, hid:], NT)
+            back = mul(take(dy_refs[first // rows], first % rows, tile), held[slot, one, :hid], NT)
             pre, up = both[:, :hid], both[:, hid:]
-            sigma = 1.0 / (1.0 + jnp.exp(-pre))
+            sigma = 0.5 * jnp.tanh(0.5 * pre) + 0.5
             active = pre * sigma
-            gate = gate_ref[0, here, one : one + 1]
+            chosen = lax.broadcasted_iota(jnp.int32, (tile, gates.shape[1]), 1) == index
+            gate = jnp.sum(jnp.where(chosen, gates[here], 0.0), axis=1, keepdims=True)
+            column = lax.broadcasted_iota(jnp.int32, (tile, LANES), 1) == index
             hidden = active * up
-            dot_ref[0, here, one : one + 1] = jnp.sum(hidden * back, axis=1, keepdims=True)
+            dot = jnp.sum(hidden * back, axis=1, keepdims=True)
+            dots[here] += jnp.where(column, dot, 0.0)
             back = back * gate
             kept_ref[here, base : base + hid] = (hidden * gate).astype(BF)
             kept_ref[here, base + hid : base + 2 * hid] = (
@@ -574,120 +712,204 @@
 
     @pl.when(step == sets - 1)
     def _():
-        moe_ref[...] = moe[...].astype(BF)
-        dx_ref[...] = dx[...].astype(BF)
-
-
-def rows_call(moe_in, cotangent, gates, weights):
-    rows, width = moe_in.shape
-    sets = len(weights)
-    experts, depth, _ = weights[0].shape
+        for number in range(parts):
+            here = slice(number * rows, (number + 1) * rows)
+            moe_refs[number][...] = moe[here].astype(BF)
+            dx_refs[number][:, :width] = dx[here].astype(BF)
+            dx_refs[number][:, width:] = dots[here].astype(BF)
+
+
+def rows_call(core, router, moe_in, cotangent, carried, place, weights, first_number, each_device, before=None, waits=()):
+    blocks, _, own, width = moe_in[0].shape
+    rows = blocks * own
+    parts = 2
+    chips, depth, _ = weights[0].shape
+    experts = EXPERT_STEP
+    sets = len(weights) * chips // experts
+    number = router.shape[1]
     full = whole((rows, width))
-    narrow = pl.BlockSpec((1, rows, experts), lambda i: (i, 0, 0))
     wide = experts * depth
+    wider = whole((rows, width + LANES))
+    operands = [core, router, *moe_in, *cotangent, *carried, *weights]
+
+    def half(columns):
+        return pl.BlockSpec((blocks, 1, own, columns), lambda i: (0, place, 0, 0), pipeline_mode=pl.Buffered(1))
+
+    specs = [pl.BlockSpec(memory_space=pltpu.SMEM), whole(router.shape)] + [half(width)] * 4 + [half(number)] * 2
+    specs += [pl.BlockSpec(memory_space=pl.ANY)] * len(weights)
+    if before is not None:
+        operands += before
+        specs += [ANYWHERE] * 4
+    operands += waits
+    specs += [ANYWHERE] * len(waits)
     return pl.pallas_call(
-        functools.partial(rows_kernel, sets, experts),
+        functools.partial(rows_kernel, len(weights), first_number, each_device, before is not None, len(waits)),
         grid=(sets,),
-        in_specs=[full, full, narrow] + [pl.BlockSpec(memory_space=pl.ANY)] * sets,
-        out_specs=[full, full, pl.BlockSpec((rows, wide), lambda i: (0, i)), narrow],
+        in_specs=specs,
+        out_specs=[full] * 2
+        + [wider] * 2
+        + [pl.BlockSpec((parts * rows, wide), lambda i: (0, i)), whole((rows, number))],
         out_shape=[jax.ShapeDtypeStruct((rows, width), BF)] * 2
-        + [jax.ShapeDtypeStruct((rows, sets * wide), BF), jax.ShapeDtypeStruct((sets, rows, experts), F32)],
+        + [jax.ShapeDtypeStruct((rows, width + LANES), BF)] * 2
+        + [
+            jax.ShapeDtypeStruct((parts * rows, sets * wide), BF),
+            jax.ShapeDtypeStruct((rows, number), F32),
+        ],
         scratch_shapes=[
             pltpu.VMEM((2, experts, depth, width), BF),
-            pltpu.VMEM((rows, width), F32),
-            pltpu.VMEM((rows, width), F32),
+            pltpu.VMEM((parts * rows, width), F32),
+            pltpu.VMEM((parts * rows, width), F32),
+            pltpu.VMEM((parts * rows, number), F32),
+            pltpu.VMEM((parts * rows, LANES), F32),
             pltpu.SemaphoreType.DMA((2,)),
+            pltpu.SemaphoreType.DMA((4,)),
         ],
         compiler_params=kernel_params(),
         cost_estimate=pl.CostEstimate(
-            flops=4 * rows * width * wide * sets,
-            bytes_accessed=8 * rows * width + 2 * sets * wide * (rows + width),
-            transcendentals=rows * wide * sets // 3,
+            flops=4 * parts * rows * width * wide * sets,
+            bytes_accessed=8 * parts * rows * width + 2 * sets * wide * (parts * rows + width),
+            transcendentals=parts * rows * wide * sets // 3,
         ),
         name="expert_rows",
-    )(moe_in, cotangent, gates, *weights)
-
-
-def weight_grads_kernel(experts, added, x_ref, dy_ref, kept_ref, *rest):
-    out_ref, turned = rest[-2:]
-    hid = turned.shape[0] // (3 * experts)
+    )(*operands)
+
+
+def weight_grads_kernel(sides, halves, outs, added, skipped, order_ref, *refs):
+    parts = sides * halves
+    x_refs, dy_refs = refs[:parts], refs[parts : 2 * parts]
+    kept_refs = refs[2 * parts : 2 * parts + 2 * halves]
+    add_refs = refs[2 * parts + 2 * halves : 2 * parts + 2 * halves + added]
+    out_refs, turned = refs[2 * parts + 2 * halves + added + skipped : -1], refs[-1]
+    hid = turned.shape[0] // 6
+    span = kept_refs[0].shape[0]
+    rows = span // sides
 
     @pl.when(pl.program_id(0) == 0)
     def _():
-        for one in range(experts):
-            base = one * 3 * hid
-            turned[one * hid : (one + 1) * hid] = kept_ref[:, base : base + hid].T
-            place = experts * hid + one * 2 * hid
-            turned[place : place + 2 * hid] = kept_ref[:, base + hid : base + 3 * hid].T
-
-    down = mul(turned[: experts * hid], dy_ref[...])
-    both = mul(turned[experts * hid :], x_ref[...])
-    for one in range(experts):
-        first, second = down[one * hid : (one + 1) * hid], both[one * 2 * hid : (one + 1) * 2 * hid]
-        if added:
-            first = first + rest[0][one, :hid].astype(F32)
-            second = second + rest[0][one, hid:].astype(F32)
-        out_ref[one, :hid] = first.astype(BF)
-        out_ref[one, hid:] = second.astype(BF)
-
-
-def weight_grads_call(moe_in, cotangent, kept, number, experts, depth, addend=None):
-    rows, width = moe_in.shape
+        for h in range(halves):
+            there = slice(h * span, (h + 1) * span)
+            for one in range(2):
+                kept_ref = kept_refs[2 * h + one]
+                turned[one * hid : (one + 1) * hid, there] = kept_ref[:, :hid].T
+                place = 2 * hid + one * 2 * hid
+                turned[place : place + 2 * hid, there] = kept_ref[:, hid:].T
+
+    def total(first, last, refs):
+        return sum(
+            mul(turned[first:last, p * rows : (p + 1) * rows], ref[:, 0].reshape(rows, ref.shape[-1]))
+            for p, ref in enumerate(refs)
+        )
+
+    down = total(0, 2 * hid, dy_refs)
+    both = total(2 * hid, 6 * hid, x_refs)
+    for one in range(2):
+        value = jnp.concatenate(
+            [down[one * hid : (one + 1) * hid], both[one * 2 * hid : (one + 1) * 2 * hid]], axis=0
+        )
+        if outs == 1:
+            out_refs[0][one] = value.astype(BF)
+            continue
+        middle = value.shape[0] // 2
+        for number, part in enumerate((value[:middle], value[middle:])):
+            if added and number == one:
+                part = part + add_refs[one][...].astype(F32)
+            out_refs[2 * one + number][...] = part.astype(BF)
+
+
+def weight_grads_call(moe_in, cotangent, kept, order, depth, addends=(), waits=(), pair=None, into=None):
+    blocks, halves, own, width = moe_in[0].shape
+    sides = len(moe_in)
     tile = COLUMN_TILE
-    column = pl.BlockSpec((rows, tile), lambda i: (0, i))
-    out = pl.BlockSpec((experts, depth, tile), lambda i: (0, 0, i))
-    operands = [moe_in, cotangent, kept]
-    specs = [column, column, pl.BlockSpec((rows, experts * depth), lambda i: (0, number), pipeline_mode=pl.Buffered(1))]
-    if addend is not None:
-        operands.append(addend)
-        specs.append(out)
+    span = kept[0].shape[0]
+    parts = [(h, side) for h in range(halves) for side in range(sides)]
+
+    def column(h):
+        return pl.BlockSpec((blocks, 1, own, tile), lambda i, order: (0, h, 0, i))
+
+    def expert(one):
+        return pl.BlockSpec((span, depth), lambda i, order: (0, order[one]), pipeline_mode=pl.Buffered(1))
+
+    operands = [moe_in[side] for _, side in parts] + [cotangent[side] for _, side in parts]
+    operands += [kept[h] for h in range(halves) for _ in range(2)]
+    specs = [column(h) for h, _ in parts] * 2 + [expert(one) for _ in range(halves) for one in range(2)]
+    operands += addends
+    specs += [pl.BlockSpec((addend.shape[0], tile), lambda i, order: (0, i)) for addend in addends]
+    aliases = {}
+    if into is not None:
+        waits = [into, *waits]
+        aliases = {1 + len(operands): 0}
+    if pair is None:
+        outs = 4
+        out_specs = [pl.BlockSpec((depth // 2, tile), lambda i, order: (0, i))] * 4
+        out_shape = [jax.ShapeDtypeStruct((depth // 2, width), BF)] * 4
+    else:
+        outs = 1
+        out_specs = pl.BlockSpec((2, depth, tile), lambda i, order: (pair, 0, i))
+        out_shape = jax.ShapeDtypeStruct((kept[0].shape[1] // depth, depth, width), BF)
     return pl.pallas_call(
-        functools.partial(weight_grads_kernel, experts, addend is not None),
-        grid=(width // tile,),
-        in_specs=specs,
-        out_specs=out,
-        out_shape=jax.ShapeDtypeStruct((experts, depth, width), BF),
-        scratch_shapes=[pltpu.VMEM((experts * depth, rows), BF)],
+        functools.partial(weight_grads_kernel, sides, halves, outs, len(addends), len(waits)),
+        grid_spec=pltpu.PrefetchScalarGridSpec(
+            num_scalar_prefetch=1,
+            grid=(width // tile,),
+            in_specs=specs + [ANYWHERE] * len(waits),
+            out_specs=out_specs,
+            scratch_shapes=[pltpu.VMEM((2 * depth, halves * span), BF)],
+        ),
+        out_shape=out_shape,
+        input_output_aliases=aliases,
         compiler_params=kernel_params(),
         cost_estimate=pl.CostEstimate(
-            flops=2 * rows * width * experts * depth,
-            bytes_accessed=4 * rows * width + 4 * experts * depth * width,
+            flops=4 * halves * span * width * depth,
+            bytes_accessed=4 * halves * span * width + 8 * depth * width,
             transcendentals=0,
         ),
         name="expert_weight_grads",
-    )(*operands)
+    )(order, *operands, *waits)
 
 
 def swap(values, bit):
-    size = lax.axis_size("expert")
-    return lax.ppermute(values, "expert", [(i, i ^ bit) for i in range(size)])
-
-
-def spread_weights(own):
-    held = {0: own}
-    held[1] = swap(own, 1)
-    held[2] = swap(own, 2)
-    held[4] = swap(own, 4)
-    half = own.shape[0] // 2
-    far = (swap(held[2][:half], 4), swap(held[4][half:], 2))
-    held[6] = jnp.concatenate(far, axis=0)
-    for r in (3, 5, 7):
-        held[r] = swap(held[r - 1], 1)
-    return held
-
-
-def collect_weight_grads(part):
-    chip = {}
-    for r in (6, 4, 2, 0):
-        chip[r] = part(r, swap(part(r + 1, None), 1))
-    half = chip[6].shape[0] // 2
-    via_first = swap(chip[6][:half], 2)
-    via_second = swap(chip[6][half:], 4)
-    plus = lambda left, right: (left.astype(F32) + right.astype(F32)).astype(BF)
-    from_four = (swap(plus(chip[4][:half], via_first), 4), swap(chip[4][half:], 4))
-    from_two = (swap(chip[2][:half], 2), swap(plus(chip[2][half:], via_second), 2))
-    total = chip[0].astype(F32) + jnp.concatenate(from_four, axis=0).astype(F32)
-    return total + jnp.concatenate(from_two, axis=0).astype(F32)
+    size = lax.axis_size(EXPERT)
+    return lax.ppermute(values, EXPERT, [(i, i ^ bit) for i in range(size)])
+
+
+def plus(left, right):
+    return (left.astype(F32) + right.astype(F32)).astype(BF)
+
+
+def relative_columns(values):
+    here = lax.axis_index(EXPERT)
+    size = lax.axis_size(EXPERT)
+    span = values.shape[1] // size
+    order = [*range(0, size, 2), *range(1, size, 2)]
+    return jnp.concatenate(
+        [lax.dynamic_slice_in_dim(values, (here ^ r) * span, span, 1) for r in order], axis=1
+    )
+
+
+def block_terms(values):
+    rows = values.shape[0] // 4
+    mine, to_two, to_four, across = (values[n * rows : (n + 1) * rows] for n in range(4))
+    return (across[: rows // 2], across[rows // 2 :]), to_four, to_two, mine
+
+
+def beside(terms, via):
+    _, to_four, to_two, _ = terms
+    middle = to_four.shape[0] // 2
+    return (
+        jnp.concatenate([plus(to_four[:middle], via[0]), to_four[middle:]], axis=0),
+        jnp.concatenate([to_two[:middle], plus(to_two[middle:], via[1])], axis=0),
+    )
+
+
+def join(*values):
+    return lax.optimization_barrier(values)
+
+
+def scatter_tensor(values):
+    return lax.psum_scatter(values, TENSOR, scatter_dimension=0, tiled=True)
+
+
+HALVES = 2
 
 
 def shards_near(
@@ -696,148 +918,383 @@
 ):
     rows, width = tokens.shape
     local = w_query.shape[1]
-    groups = lax.axis_size("expert")
-    n_tensor = lax.axis_size("tensor")
-    here = lax.axis_index("expert")
-    layer = lax.axis_index("tensor")
+    groups = lax.axis_size(EXPERT)
+    n_tensor = lax.axis_size(TENSOR)
+    here = lax.axis_index(EXPERT)
+    layer = lax.axis_index(TENSOR)
     experts_here, hid = w_gate.shape[0], w_gate.shape[2]
     experts_all = experts_here * groups
     own_rows = rows // n_tensor
-
-    packed = jnp.concatenate([w_down, jnp.swapaxes(w_gate, 1, 2), jnp.swapaxes(w_up, 1, 2)], axis=1)
-    weights = spread_weights(packed)
-
+    own = lambda array: lax.dynamic_slice_in_dim(array, layer * own_rows, own_rows, 0)
+    view = lambda array: array.reshape(n_tensor, HALVES, own_rows // HALVES, array.shape[-1])
+    half = range(HALVES)
+
+    chips = groups // 2
+    sides_of = [[2 * chip + core for chip in range(chips)] for core in (0, 1)]
+    core = lax.rem(here, 2)
+
+    core_rows = local // 2
+    w_half = lax.dynamic_slice_in_dim(w_output, core * core_rows, core_rows, 0)
+    w_mine = [swap_tensor(w_half, bits) for bits in (1, 2)]
+
+    def pack(gate, up, down):
+        return jnp.concatenate([down, gate.T, up.T], axis=0)
+
+    def spread(value):
+        return lax.all_gather(value, EXPERT, axis_index_groups=sides_of)
+
+    depth = 3 * hid
+    packed = [pack(w_gate[j], w_up[j], w_down[j]) for j in range(experts_here)]
+    weights = [spread(packed[0])]
+    number = jnp.arange(experts_all, dtype=jnp.int32)
+    carried = (expert_ids[:, :, None] == number) & (slot_index >= 0)[:, :, None]
+    carried = jnp.sum(carried.astype(BF), axis=1)
     segment, position = layout(seq_lengths, rows)
     cosine, sine = rope_angles(position, HEAD_DIM)
     cos_table = jnp.concatenate([cosine, cosine], axis=1)
     sin_table = jnp.concatenate([-sine, sine], axis=1)
-    inputs = tokens.astype(F32)
-    normed, inverse_in = norm_rows(inputs, attn_gain)
-    attn_in = normed.astype(BF)
-    query_raw = mul(attn_in, w_query)
-    key_raw = mul(attn_in, w_key)
-    totals = jnp.stack([jnp.sum(query_raw * query_raw, axis=-1), jnp.sum(key_raw * key_raw, axis=-1)])
-    totals = sum_small(totals)
-    values = mul(attn_in, w_value).astype(BF)
-    query_inverse = lax.rsqrt(totals[0] / width + EPS)[:, None]
-    key_inverse = lax.rsqrt(totals[1] / width + EPS)[:, None]
+    attn_in, inverse_in, query_raw, key_raw, values, totals = front_call(
+        tokens, attn_gain[None], w_query, w_key, w_value, [*packed, cos_table, sin_table]
+    )
+    total = sum_small(totals.T.reshape(-1, LANES)).reshape(2, rows)
+    total, w_mine[0], w_mine[1] = join(total, *w_mine)
+    w_mine.append(swap_tensor(w_mine[1], 1))
+    query_inverse = lax.rsqrt(total[0] / width + EPS)[:, None]
+    key_inverse = lax.rsqrt(total[1] / width + EPS)[:, None]
     operands = [
         query_raw, key_raw, values, query_inverse, key_inverse, query_gain[None], key_gain[None],
         cos_table, sin_table, segment[:, None], segment[None],
     ]
     queries, keys, context = attention_call(operands, rows, local)
-    attn = lax.psum_scatter(mul(context, w_output).astype(BF), "tensor", scatter_dimension=0, tiled=True)
-
-    own = lambda array: lax.dynamic_slice_in_dim(array, layer * own_rows, own_rows, 0)
-    tokens_own = own(tokens).astype(F32)
-    cotangent_own = own(cotangent).astype(F32)
-    hidden_in = tokens_own + attn.astype(F32)
-    moe_in, inverse_moe = norm_rows(hidden_in, moe_gain)
+    far_context = swap_tensor(context, 2)
+    near_context = swap_tensor(context, 1)
+    packed[1], w_mine[2], context = join(packed[1], w_mine[2], context)
+    weights.append(spread(packed[1]))
+    near_context, far_context, *w_mine = join(near_context, far_context, *w_mine)
+    contexts = [context, near_context, far_context, swap_tensor(far_context, 1)]
+    w_mine = jnp.concatenate(w_mine, axis=0)
+    w_all = jnp.concatenate([w_output, w_mine, swap(w_mine, 1)], axis=0)
+    carried_later, cotangent_later, contexts[0] = lax.optimization_barrier((carried, cotangent, contexts[0]))
+    carried_sides = [view(carried), view(swap(carried_later, 1))]
+    cotangent_sides = [view(cotangent), view(swap(cotangent_later, 1))]
+    hidden, moe_low, inverse_moe = hidden_call(core[None], tokens, moe_gain[None], contexts, w_all)
+    sides = [view(moe_low), view(swap(moe_low, 1))]
     router_wide = router.astype(F32)
-    shares = jax.nn.softmax(jnp.dot(moe_in, router_wide, precision=lax.Precision.HIGHEST), axis=-1)
-    moe_low = lax.all_gather(moe_in.astype(BF), "tensor", tiled=True)
-    shares_all = gather_small(shares)
-
-    number = jnp.arange(experts_all, dtype=jnp.int32)
-    carried = (expert_ids[:, :, None] == number) & (slot_index >= 0)[:, :, None]
-    carried = jnp.sum(carried.astype(F32), axis=1)
-    gates = shares_all * carried
-    order = [0, 1, 2, 3, 4, 5, 6, 7]
-    of_set = lambda array, r: lax.dynamic_slice_in_dim(array, (here ^ r) * experts_here, experts_here, 1)
-    gate_sets = jnp.stack([of_set(gates, r) for r in order])
-    moe_part, dx_part, kept, dots = rows_call(moe_low, cotangent, gate_sets, [weights[r] for r in order])
-
-    dots_all = jnp.zeros((rows, experts_all), F32)
-    for place, r in enumerate(order):
-        dots_all = lax.dynamic_update_slice(dots_all, dots[place], (0, (here ^ r) * experts_here))
-    dshares = scatter_small(dots_all * carried)
-    dlogits = shares * (dshares - jnp.sum(shares * dshares, axis=-1, keepdims=True))
+    calls, kept, shares = [None, None], [{}, {}], [None, None]
+
+    def run(h, j, *waits):
+        before = None if calls[h] is None else calls[h][:4]
+        calls[h] = rows_call(
+            core[None], router, sides, cotangent_sides, carried_sides, h, [weights[j]], j, experts_here, before, waits
+        )
+        kept[h][j] = calls[h][4]
+        shares[h] = calls[h][5]
+
+    def send_back(h):
+        terms = plus(calls[h][2], swap(calls[h][3], 1))
+        return terms, scatter_tensor(terms)
+
+    chip = here // 2
+
+    def part(j, first, second, *rest, **more):
+        order = jnp.stack([first, second]).astype(jnp.int32)
+        return weight_grads_call(
+            sides, cotangent_sides, [kept[h][j] for h in half], order, depth, *rest, **more
+        )
+
+    def send(terms, bits):
+        return [swap(term, bit) for term, bit in zip(terms, bits)]
+
+    run(0, 0)
+    run(1, 0, calls[0][4])
+    *far, mine_low, mine_high = part(0, chip ^ 3, chip)
+    via = send(far, (2, 4))
+    run(0, 1, *far)
+    *calls[0], via[0], via[1] = join(*calls[0], *via)
+    kept[0][1] = calls[0][4]
+    terms, sums_first = send_back(0)
+    run(1, 1, terms)
+    *calls[1], sums_first = join(*calls[1], sums_first)
+    kept[1][1] = calls[1][4]
+    terms, sums_second = send_back(1)
+    near = part(0, chip ^ 2, chip ^ 1, via, [terms])
+    near_low = send(near[::2], (4, 2))
+    second = part(1, 0 * chip, 0 * chip + 1, (), [near[0]], pair=0)
+    sums_second, second, attn_in, *moe_terms = join(sums_second, second, attn_in, *calls[0][:2], *calls[1][:2])
+    moe_terms = [plus(moe_terms[2 * h], swap(moe_terms[2 * h + 1], 1)) for h in half]
+    moe_terms = jnp.stack([term.reshape(n_tensor, -1, width) for term in moe_terms], axis=1).reshape(rows, width)
+    sums = jnp.concatenate([sums_first, sums_second], axis=0)
+    dshares = sums[:, width : width + experts_all].astype(F32) * own(carried).astype(F32)
+    share = jnp.concatenate(
+        [lax.dynamic_slice_in_dim(item, layer * (own_rows // HALVES), own_rows // HALVES, 0) for item in shares], axis=0
+    )
+    hidden_own, inverse_own = own(hidden), own(inverse_moe)
+    moe_in = hidden_own * inverse_own * moe_gain
+    dlogits = share * (dshares - jnp.sum(share * dshares, axis=-1, keepdims=True))
     router_back = jnp.einsum("te,de->td", dlogits, router_wide, precision=lax.Precision.HIGHEST)
-    router_part = jnp.einsum("td,te->de", moe_in, dlogits, precision=lax.Precision.HIGHEST)
-
-    dx = lax.psum_scatter(dx_part, "tensor", scatter_dimension=0, tiled=True)
-    grad_moe_in = dx.astype(F32) + router_back
-    grad_norm_moe, grad_moe_gain = norm_back(hidden_in, inverse_moe, moe_gain, grad_moe_in)
-    grad_hidden_in = cotangent_own + grad_norm_moe
-    grad_low = lax.all_gather(grad_hidden_in.astype(BF), "tensor", tiled=True)
-    grad_context = mul(grad_low, w_output, NT).astype(BF)
-    dq, dk, value_low, inner, grad_query_gain, grad_key_gain = attention_back_call(
-        operands + [queries, keys, grad_context], rows, local
-    )
-    inner = sum_small(jnp.sum(inner, axis=0).T)
-    moe = lax.psum_scatter(moe_part, "tensor", scatter_dimension=0, tiled=True)
-    out = lax.all_gather((hidden_in + moe.astype(F32)).astype(BF), "tensor", tiled=True)
+    grad_norm_moe, grad_moe_gain = norm_back(
+        hidden_own, inverse_own, moe_gain, sums[:, :width].astype(F32) + router_back
+    )
+    grad_hidden = own(cotangent).astype(F32) + grad_norm_moe
+    grad_low = grad_hidden.astype(BF)
+
+    by_head = mul(grad_low, w_all, NT).astype(BF)
+    core_columns = local // 2
+    grad_context = jnp.zeros((rows, local), BF)
+    for bits in range(n_tensor):
+        if bits == 0:
+            came = by_head[:, :local]
+        else:
+            begin = local + (bits - 1) * core_columns
+            mine = by_head[:, begin : begin + core_columns]
+            begin += (n_tensor - 1) * core_columns
+            other = by_head[:, begin : begin + core_columns]
+            lower = jnp.where(core == 0, mine, other)
+            upper = jnp.where(core == 0, other, mine)
+            came = swap_tensor(jnp.concatenate([lower, upper], axis=1), bits)
+        grad_context = lax.dynamic_update_slice_in_dim(grad_context, came, (layer ^ bits) * own_rows, 0)
+    heads_own = jnp.concatenate([own(item) for item in contexts], axis=1)
+    output_grads = mul(relative_columns(grad_low), heads_own, TN).astype(BF)
+    output_grads = [output_grads[: width // 2], output_grads[width // 2 :]]
+    attn_relative = relative_columns(attn_in)
+    grad_context, moe_terms, attn_relative, *output_grads = join(
+        grad_context, moe_terms, attn_relative, *output_grads
+    )
+    moe = scatter_tensor(moe_terms)
+    came = swap(output_grads[1], 1)
+    back = attention_back_call(
+        operands + [queries, keys, grad_context], rows, local, [output_grads[1]]
+    )
+    *back, came, near_low[0], near_low[1] = join(*back, came, *near_low)
+    near_high = send(near[1::2], (4, 2))
+    dq, dk, value_low, inner, grad_query_gain, grad_key_gain = back
+    inner = jnp.sum(inner, axis=0).T
+    inner = sum_small(inner.reshape(-1, LANES)).reshape(inner.shape)
+    output_grads = block_terms(plus(output_grads[0], came))
+    output_via = send(output_grads[0], (2, 4))
+    second = part(1, 0 * chip + 2, 0 * chip + 3, (), [inner], pair=1, into=second)
+    inner, moe, second, *output_via, near_high[0], near_high[1] = join(inner, moe, second, *output_via, *near_high)
+    grads_one = lax.psum_scatter(
+        second.reshape(-1, width), EXPERT, scatter_dimension=0, axis_index_groups=sides_of, tiled=True
+    )
+    out_own = (hidden_own + moe.astype(F32)).astype(BF)
+    came = exchange(out_own, out_own)
 
     def raw_grad(scaled, raw, inverse, total):
         return (inverse * scaled - raw * inverse * inverse * inverse * (total / width)[:, None]).astype(BF)
 
     query_low = raw_grad(dq, query_raw, query_inverse, inner[0])
     key_low = raw_grad(dk, key_raw, key_inverse, inner[1])
-    terms_in = mul(query_low, w_query, NT) + mul(key_low, w_key, NT) + mul(value_low, w_value, NT)
-    grad_normed = lax.psum_scatter(terms_in.astype(BF), "tensor", scatter_dimension=0, tiled=True).astype(F32)
-    inverse_own = lax.dynamic_slice_in_dim(inverse_in, layer * own_rows, own_rows, 0)
-    grad_norm_in, grad_attn_gain = norm_back(tokens_own, inverse_own, attn_gain, grad_normed)
-    grad_input = lax.all_gather((grad_hidden_in + grad_norm_in).astype(BF), "tensor", tiled=True)
-
-    depth = packed.shape[1]
-    part = lambda r, addend: weight_grads_call(moe_low, cotangent, kept, order.index(r), experts_here, depth, addend)
-    expert_grads = collect_weight_grads(part).astype(BF)
-    grad_w_down = expert_grads[:, :hid]
-    grad_w_gate = jnp.swapaxes(expert_grads[:, hid : 2 * hid], 1, 2)
-    grad_w_up = jnp.swapaxes(expert_grads[:, 2 * hid :], 1, 2)
-
-    scatter = lambda array, dim: lax.psum_scatter(array, "expert", scatter_dimension=dim, tiled=True)
-    grad_w_query = scatter(mul(attn_in, query_low, TN).astype(BF), 0)
-    grad_w_key = scatter(mul(attn_in, key_low, TN).astype(BF), 0)
-    grad_w_value = scatter(mul(attn_in, value_low, TN).astype(BF), 0)
-    grad_w_output = scatter(mul(context, grad_low, TN).astype(BF), 1)
-    gains = scatter(jnp.concatenate([
-        grad_query_gain.reshape(groups, -1), grad_key_gain.reshape(groups, -1)], axis=1), 0)[0]
-    span = local // groups
-    both = jnp.concatenate(
-        [router_part, grad_moe_gain[:, None], grad_attn_gain[:, None]], axis=1
-    )
-    both = scatter(lax.psum(both, "tensor"), 0)
+    lows = jnp.concatenate([query_low, key_low, value_low], axis=1)
+    wide = jnp.concatenate([w_query, w_key, w_value], axis=1)
+    terms_in = mul(lows, wide, NT).astype(BF)
+    def expert_outputs(grads):
+        return grads[hid : 2 * hid].T, grads[2 * hid :].T, grads[:hid]
+
+    outputs_zero = jnp.concatenate([
+        (mine.astype(F32) + near[0].astype(F32) + near[1].astype(F32)).astype(BF)
+        for mine, near in ((mine_low, near_low), (mine_high, near_high))], axis=0)
+    outputs_zero = list(expert_outputs(outputs_zero))
+    output_near = send(beside(output_grads, output_via), (4, 2))
+    *came, terms_in, lows = join(*came, terms_in, lows)
+    out_above, out_below = [from_above(came)], [from_below(came)]
+    chunk = lambda place: lax.dynamic_slice_in_dim(terms_in, jnp.clip(place, 0, n_tensor - 1) * own_rows, own_rows, 0)
+    sum_above = sum_below = jnp.zeros((), BF)
+    for step in range(1, n_tensor):
+        came = exchange(
+            jnp.where(
+                layer >= n_tensor - step, plus(chunk(layer - n_tensor + step), sum_above), out_above[-1]
+            ),
+            jnp.where(layer < step, plus(chunk(layer + n_tensor - step), sum_below), out_below[-1]),
+        )
+        if step == 1:
+            grad_attn_gain = jnp.sum(terms_in.astype(F32) * tokens.astype(F32) * inverse_in, axis=0)
+            router_part = jnp.einsum("td,te->de", moe_in, dlogits, precision=lax.Precision.HIGHEST)
+            own_width, span = width // groups, local // groups
+            spread_gain = lambda gain: jnp.pad(
+                gain.reshape(groups, span), ((0, 0), (0, own_width - span))
+            ).reshape(width, 1)
+            small = jnp.concatenate([
+                router_part, grad_moe_gain[:, None], grad_attn_gain[:, None],
+                spread_gain(grad_query_gain), spread_gain(grad_key_gain)], axis=1).astype(BF)
+            small = jnp.pad(small, ((0, 0), (0, LANES - small.shape[1])))
+            blocks = jnp.concatenate([
+                mul(attn_relative, lows, TN).astype(BF), relative_columns(small.T).T], axis=1)
+            blocks = [blocks[: width // 2], blocks[width // 2 :]]
+            *came, blocks[0], blocks[1] = join(*came, *blocks)
+            blocks_came = swap(blocks[1], 1)
+        elif step == 2:
+            came[0], came[1], blocks_came, *outputs_zero = join(*came, blocks_came, *outputs_zero)
+            blocks = block_terms(plus(blocks[0], blocks_came))
+            via = send(blocks[0], (2, 4))
+        else:
+            *came, via[0], via[1] = join(*came, *via)
+        above, below = from_above(came), from_below(came)
+        sum_above = jnp.where(layer == n_tensor - 1, 0, above)
+        sum_below = jnp.where(layer == 0, 0, below)
+        if step < n_tensor - 1:
+            out_above.append(above)
+            out_below.append(below)
+    grad_normed = own(terms_in).astype(F32) + sum_above.astype(F32) + sum_below.astype(F32)
+    out = end_line(out_own, out_above, out_below)
+
+    grad_norm_in, _ = norm_back(own(tokens).astype(F32), own(inverse_in), attn_gain, grad_normed)
+    grad_input = (grad_hidden + grad_norm_in).astype(BF)
+    input_above, input_below = [grad_input], [grad_input]
+    for step in range(1, n_tensor):
+        came = exchange(input_above[-1], input_below[-1])
+        if step == 1:
+            near = send(beside(blocks, via), (4, 2))
+            *came, output_near[0], output_near[1] = join(*came, *output_near)
+        if step == 2:
+            *came, near[0], near[1], grads_one = join(*came, *near, grads_one)
+        input_above.append(from_above(came))
+        input_below.append(from_below(came))
+    projections = sum((item.astype(F32) for item in near), blocks[3].astype(F32))
+    small = projections[:, 3 * local :]
+    projections = projections[:, : 3 * local].astype(BF)
+    by_index = sum((item.astype(F32) for item in output_near), output_grads[3].astype(F32))
+    grad_w_output, shared = by_index[:, :local], small
+    for bits in range(1, n_tensor):
+        terms = jnp.concatenate([by_index[:, bits * local : (bits + 1) * local], small], axis=1)
+        came = swap_tensor(terms.astype(BF), bits).astype(F32)
+        grad_w_output, shared = grad_w_output + came[:, :local], shared + came[:, local:]
+    grad_w_output = grad_w_output.T
+    grad_input = end_line(grad_input, input_above[1:], input_below[1:])
+
+    gains = small[:span, experts_all + 2 : experts_all + 4].astype(BF)
     return (
-        out, grad_input, grad_w_query, grad_w_key, grad_w_value, grad_w_output,
-        gains[:span].astype(BF), gains[span:].astype(BF),
-        both[:, experts_all + 1].astype(BF), both[:, experts_all].astype(BF), both[:, :experts_all].astype(BF),
-        grad_w_gate, grad_w_up, grad_w_down,
-    )
+        out, grad_input,
+        projections[:, :local], projections[:, local : 2 * local], projections[:, 2 * local : 3 * local],
+        grad_w_output.astype(BF),
+        gains[:, 0], gains[:, 1], shared[:, experts_all + 1].astype(BF), shared[:, experts_all].astype(BF),
+        shared[:, :experts_all].astype(BF),
+        *(jnp.stack(pair) for pair in zip(outputs_zero, expert_outputs(grads_one))),
+    )
+
+
+def swap_tensor(values, bit):
+    size = lax.axis_size(TENSOR)
+    return lax.ppermute(values, TENSOR, [(i, i ^ bit) for i in range(size)])
+
+
+def scatter_halving(values):
+    place = lax.axis_index(TENSOR)
+    rows = values.shape[0] // lax.axis_size(TENSOR)
+    cut = lambda bits: lax.dynamic_slice_in_dim(values, (place ^ bits) * rows, rows, 0)
+    passed = swap_tensor(plus(cut(2), swap_tensor(cut(3), 1)), 2)
+    return cut(0).astype(F32) + swap_tensor(cut(1), 1).astype(F32) + passed.astype(F32), passed
+
+
+def scatter_direct(values):
+    place = lax.axis_index(TENSOR)
+    size = lax.axis_size(TENSOR)
+    rows = values.shape[0] // size
+    cut = lambda bits: lax.dynamic_slice_in_dim(values, (place ^ bits) * rows, rows, 0)
+    return sum((swap_tensor(cut(bits), bits).astype(F32) for bits in range(1, size)), cut(0).astype(F32))
+
+
+def exchange(to_below, to_above):
+    place = lax.axis_index(TENSOR)
+    even = lax.rem(place, 2) == 0
+    outer = lax.ppermute(jnp.where(even, to_above, to_below), TENSOR, [(0, 1), (1, 0), (2, 3), (3, 2)])
+    inner = lax.ppermute(jnp.where(even, to_below, to_above), TENSOR, [(1, 2), (2, 1), (0, 0), (3, 3)])
+    return [outer, inner]
+
+
+def from_above(came):
+    return jnp.where(lax.rem(lax.axis_index(TENSOR), 2) == 0, came[0], came[1])
+
+
+def from_below(came):
+    return jnp.where(lax.rem(lax.axis_index(TENSOR), 2) == 0, came[1], came[0])
+
+
+def end_line(values, above, below):
+    place = lax.axis_index(TENSOR)
+    size = lax.axis_size(TENSOR)
+    rows = values.shape[0]
+    everything = jnp.zeros((rows * size,) + values.shape[1:], values.dtype)
+    everything = lax.dynamic_update_slice_in_dim(everything, values, place * rows, 0)
+    for ahead in range(1, size):
+        piece = jnp.where(place + ahead < size, above[ahead - 1], below[size - ahead - 1])
+        everything = lax.dynamic_update_slice_in_dim(everything, piece, lax.rem(place + ahead, size) * rows, 0)
+    return everything
+
+
+def exchange_doubling(values):
+    far = swap_tensor(values, 2)
+    return [swap_tensor(values, 1), far, swap_tensor(far, 1)]
+
+
+def start_gather(values):
+    return [swap_tensor(values, bits) for bits in range(1, lax.axis_size(TENSOR))]
+
+
+def end_gather(values, came):
+    place = lax.axis_index(TENSOR)
+    rows = values.shape[0]
+    everything = jnp.zeros((rows * (1 + len(came)),) + values.shape[1:], values.dtype)
+    for bits, piece in enumerate((values, *came)):
+        everything = lax.dynamic_update_slice_in_dim(everything, piece, (place ^ bits) * rows, 0)
+    return everything
+
+
+def gather_doubling(values):
+    place = lax.axis_index(TENSOR)
+    rows = values.shape[0]
+    far = swap_tensor(values, 2)
+    pieces = {0: values, 1: swap_tensor(values, 1), 2: far, 3: swap_tensor(far, 1)}
+    everything = jnp.zeros((rows * lax.axis_size(TENSOR),) + values.shape[1:], values.dtype)
+    for bits, piece in pieces.items():
+        everything = lax.dynamic_update_slice_in_dim(everything, piece, (place ^ bits) * rows, 0)
+    return everything
+
+
+def mix_halves(values):
+    size = lax.axis_size(TENSOR)
+    view = values.reshape(HALVES, size, -1, values.shape[-1])
+    return jnp.swapaxes(view, 0, 1).reshape(values.shape)
+
+
+def unmix_halves(values):
+    size = lax.axis_size(TENSOR)
+    view = values.reshape(size, HALVES, -1, values.shape[-1])
+    return jnp.swapaxes(view, 0, 1).reshape(values.shape)
 
 
 def rotations():
-    size = lax.axis_size("tensor")
+    size = lax.axis_size(TENSOR)
     return [[(i, (i + d) % size) for i in range(size)] for d in range(1, size)]
 
 
 def sum_small(values):
     total = values
     for pairs in rotations():
-        total = total + lax.ppermute(values, "tensor", pairs)
+        total = total + lax.ppermute(values, TENSOR, pairs)
     return total
 
 
 def gather_small(values):
     rows = values.shape[0]
-    size = lax.axis_size("tensor")
-    place = lax.axis_index("tensor")
+    size = lax.axis_size(TENSOR)
+    place = lax.axis_index(TENSOR)
     whole_rows = jnp.zeros((rows * size,) + values.shape[1:], values.dtype)
     whole_rows = lax.dynamic_update_slice_in_dim(whole_rows, values, place * rows, 0)
     for d, pairs in enumerate(rotations(), 1):
-        came = lax.ppermute(values, "tensor", pairs)
+        came = lax.ppermute(values, TENSOR, pairs)
         whole_rows = lax.dynamic_update_slice_in_dim(whole_rows, came, lax.rem(place + size - d, size) * rows, 0)
     return whole_rows
 
 
 def scatter_small(values):
-    size = lax.axis_size("tensor")
-    place = lax.axis_index("tensor")
+    size = lax.axis_size(TENSOR)
+    place = lax.axis_index(TENSOR)
     rows = values.shape[0] // size
     cut = lambda index: lax.dynamic_slice_in_dim(values, index * rows, rows, 0)
     total = cut(place)
     for d, pairs in enumerate(rotations(), 1):
-        total = total + lax.ppermute(cut(lax.rem(place + d, size)), "tensor", pairs)
+        total = total + lax.ppermute(cut(lax.rem(place + d, size)), TENSOR, pairs)
     return total
 
 
@@ -846,43 +1303,43 @@
 
 def solution(mesh):
     placed = (
-        P("expert", None),
-        P("expert", None),
-        P("expert"),
-        P("expert", None),
-        P("expert", None),
-        P(None, "tensor"),
-        P(None, "tensor"),
-        P(None, "tensor"),
-        P("tensor", None),
-        P("tensor"),
-        P("tensor"),
+        P(EXPERT, None),
+        P(EXPERT, None),
+        P(EXPERT),
+        P(EXPERT, None),
+        P(EXPERT, None),
+        P(None, TENSOR),
+        P(None, TENSOR),
+        P(None, TENSOR),
+        P(TENSOR, None),
+        P(TENSOR),
+        P(TENSOR),
         P(),
         P(),
         P(),
-        P("expert", None, "tensor"),
-        P("expert", None, "tensor"),
-        P("expert", "tensor", None),
+        P(EXPERT, None, TENSOR),
+        P(EXPERT, None, TENSOR),
+        P(EXPERT, TENSOR, None),
     )
     return jax.shard_map(
-        shards_near if mesh.shape["expert"] == NEAR_GROUPS else shards,
+        shards_near if mesh.shape[EXPERT] == NEAR_GROUPS else shards,
         mesh=mesh,
         in_specs=placed,
         out_specs=(
-            P("expert", None),
-            P("expert", None),
-            P("expert", "tensor"),
-            P("expert", "tensor"),
-            P("expert", "tensor"),
-            P("tensor", "expert"),
-            P(("tensor", "expert")),
-            P(("tensor", "expert")),
-            P("expert"),
-            P("expert"),
-            P("expert", None),
-            P("expert", None, "tensor"),
-            P("expert", None, "tensor"),
-            P("expert", "tensor", None),
+            P(EXPERT, None),
+            P(EXPERT, None),
+            P(EXPERT, TENSOR),
+            P(EXPERT, TENSOR),
+            P(EXPERT, TENSOR),
+            P(TENSOR, EXPERT),
+            P((TENSOR, EXPERT)),
+            P((TENSOR, EXPERT)),
+            P(EXPERT),
+            P(EXPERT),
+            P(EXPERT, None),
+            P(EXPERT, None, TENSOR),
+            P(EXPERT, None, TENSOR),
+            P(EXPERT, TENSOR, None),
         ),
         check_vma=False,
     )

time: 1300 us -> 861 us (0.66)
  waiting for transfers between devices: 737 us -> 235 us
  Pallas kernels: 274 us -> 340 us
  starting transfers between devices: 31.5 us -> 67.7 us
  matrix products: 65.1 us -> 30.8 us
  other arithmetic: 63.3 us -> 91.8 us
  blocking collectives: 28.4 us -> 0 us
    reduce_scatter x9 -> x4, waiting for transfers between devices: 268 us -> 2.07 us  [the longest x3 2.07 us: scatter_tensor(): return lax.psum_scatter(values, TENSOR, scatter_dimension=0, tiled=True)]
    ppermute x30 -> x56, waiting for transfers between devices: 389 us -> 233 us  [the longest x12 82.2 us: swap_tensor(): return lax.ppermute(values, TENSOR, [(i, i ^ bit) for i in range(size)])]
    all_gather x4 -> x2, waiting for transfers between devices: 79.4 us -> 0.01 us  [spread(): return lax.all_gather(value, EXPERT, axis_index_groups=sides_of)]
    pallas_call x9 -> x10, Pallas kernels: 226 us -> 291 us  [the longest x4 175 us: rows_call(): pl.pallas_call(functools.partial(rows_kernel, len(weights), first_number,...]
    ppermute x30 -> x56, starting transfers between devices: 29.8 us -> 67.2 us  [the longest x7 18.5 us: exchange(): lax.ppermute(jnp.where(even, to_below, to_above), TENSOR, [(1, 2), (2, 1)...]
    dot_general x12 -> x4, matrix products: 56.4 us -> 24.3 us  [mul(): return lax.dot_general(left, right, dims, preferred_element_type=F32)]
    psum x1 -> x0, blocking collectives: 15.3 us -> none  [shards_near(): both = scatter(lax.psum(both, 'tensor'), 0)]
    unnamed x1 -> x0, blocking collectives: 13.1 us -> none
  transfers between devices with their start and end apart: 43 -> 62, of which waited for: 23 -> 35; matrix products, arithmetic and copies ran while one was open for 12% -> 15% of each run, Pallas kernels for 10% -> 40%
where the time goes in v2:
time: 861 us; the launch traced here: 851 us
  Pallas kernels  340 us (39%)
  waiting for transfers between devices  235 us (27%)
  other arithmetic  91.8 us (11%)
  local copies, waits for them, and re-layouts  69.6 us (8%)
  starting transfers between devices  67.7 us (8%)
  matrix products  30.8 us (4%)
  between operations  16.2 us (2%)
    pallas_call x4, Pallas kernels, rows_call(): pl.pallas_call(functools.partial(rows_kernel, len(weights), first_number,...  175 us
    pallas_call x4, Pallas kernels, weight_grads_call(): pl.pallas_call(functools.partial(weight_grads_kernel, sides, halves, outs...  87.4 us
    ppermute x12, waiting for transfers between devices, swap_tensor(): return lax.ppermute(values, TENSOR, [(i, i ^ bit) for i in range(size)])  82.2 us
    ppermute x24, waiting for transfers between devices, swap(): return lax.ppermute(values, EXPERT, [(i, i ^ bit) for i in range(size)])  64.8 us
    ppermute x7, waiting for transfers between devices, exchange(): lax.ppermute(jnp.where(even, to_above, to_below), TENSOR, [(0, 1), (1, 0)...  46.5 us
    unnamed x211, local copies, waits for them, and re-layouts  34.6 us
    pallas_call x1, Pallas kernels, attention_back_call(): pl.pallas_call(attention_back_kernel, grid=(heads,), in_specs=specs + [he...  30.9 us
    ppermute x7, waiting for transfers between devices, exchange(): lax.ppermute(jnp.where(even, to_below, to_above), TENSOR, [(1, 2), (2, 1)...  24.9 us
  transfers between devices with their start and end apart: 62, of which 35 were waited for; matrix products, arithmetic and copies ran while one was open for 15% of the time, Pallas kernels for 40%

profile of v2, /device:TPU:20, one launch (start us, length us, event | category | flops | bytes accessed | tf_op | source)
XLA Modules:
  0.0 850.8 jit_solution(13600936680632913417)
XLA Ops:
  7.2 2.8 fusion.56
  13.9 2.9 pad_maximum_fusion.3.refs_0_
  24.7 3.2 fusion.39
  27.8 3.0 pad_maximum_fusion.2.refs_1_
  35.4 12.2 %front_rows.1 = (bf16[1024,2048]{1,0:T(8,128)(2,1)}, f32[1024,1]{1,0:T(8,128)}, f32[1024,512]{1,0:T(8,128)}, f32[1024,512]{1,0:T(8,128)}, bf16[1024,512]{1,0:T(8,128)(2,1)}, /*index=5*/f32[1024,2]{1,0:T(8,128)}) custom-call(bf16[1024,2048]{1,0:T(8,128)(2,1)} %tokens_ref.3, f32[1,2048]{1,0:T(1,128)} %bitcast.152, bf16[2048,512]{1,0:T(8,128)(2,1)} %wq_ref.1, ...), custom_call_target="tpu_custom_call" | custom-call | flops 6442450944 | bytes 14680064 | tf_op jit(solution)/shard_map/front_rows/pallas_call | solution.py:447
  49.3 2.7 collective-permute-start.1
  52.0 2.6 collective-permute-start.2
  54.6 14.3 %collective-permute-done = f32[16,128]{1,0:T(8,128)S(1)} collective-permute-done((f32[16,128]{1,0:T(8,128)S(1)}, f32[16,128]{1,0:T(8,128)S(1)}, u32[]{:S(2)}, u32[]{:S(2)}) %collective-permute-start) | collective-permute-done | bytes 8224 | tf_op jit(solution)/shard_map/ppermute | solution.py:1274
  74.6 17.6 %attention_rows.1 = (bf16[1024,512]{1,0:T(8,128)(2,1)}, bf16[1024,512]{1,0:T(8,128)(2,1)}, bf16[1024,512]{1,0:T(8,128)(2,1)}) custom-call(f32[1024,512]{1,0:T(8,128)} %get-tuple-element.146.q_ref, f32[1024,512]{1,0:T(8,128)} %get-tuple-element.147.k_ref, bf16[1024,512]{1,0:T(8,128)(2,1)} %get-tuple-element.148.v_ref, f32[1024,1]{1,0:T(8,128)} %copy.173.qi_ref, ...), custom_call_target="tpu_custom_call" | custom-call | flops 1073741824 | bytes 6291456 | tf_op jit(solution)/shard_map/attention_rows/pallas_call | solution.py:530
  96.8 42.0 %collective-permute-done.6.refs_1_ = bf16[1024,512]{1,0:T(8,128)(2,1)S(1)} collective-permute-done((bf16[1024,512]{1,0:T(8,128)(2,1)}, bf16[1024,512]{1,0:T(8,128)(2,1)S(1)}, u32[]{:S(2)}, u32[]{:S(2)}) %collective-permute-start.6) | collective-permute-done | bytes 1048608 | tf_op jit(solution)/shard_map/ppermute | solution.py:1178
  149.9 4.3 copy-done.57
  154.2 15.5 %collective-permute-done.8.refs_3_ = bf16[1024,512]{1,0:T(8,128)(2,1)S(1)} collective-permute-done((bf16[1024,512]{1,0:T(8,128)(2,1)S(1)}, bf16[1024,512]{1,0:T(8,128)(2,1)S(1)}, u32[]{:S(2)}, u32[]{:S(2)}) %collective-permute-start.8) | collective-permute-done | bytes 1048608 | tf_op jit(solution)/shard_map/ppermute | solution.py:1178
  170.8 16.4 %hidden_rows.1 = (f32[1024,2048]{1,0:T(8,128)}, bf16[1024,2048]{1,0:T(8,128)(2,1)}, f32[1024,1]{1,0:T(8,128)}) custom-call(s32[1]{0:T(128)} %bitcast.core_ref.refs_0_, bf16[1024,2048]{1,0:T(8,128)(2,1)} %tokens_ref.3, f32[1,2048]{1,0:T(1,128)} %bitcast.155, bf16[1024,512]{1,0:T(8,128)(2,1)} %get-tuple-element.152.refs_0_, bf16[1024,512]{1,0:T(8,128)(2,1)} %copy-done.72, ...), custom_call_target="tpu_custom_call" | custom-call | flops 8589934592 | bytes 29360128 | tf_op jit(solution)/shard_map/hidden_rows/pallas_call | solution.py:587
  190.2 3.0 collective-permute-done.12
  194.8 41.0 %expert_rows.4 = (bf16[512,2048]{1,0:T(8,128)(2,1)}, bf16[512,2048]{1,0:T(8,128)(2,1)}, bf16[512,2176]{1,0:T(8,128)(2,1)}, bf16[512,2176]{1,0:T(8,128)(2,1)}, bf...) custom-call(s32[1]{0:T(128)} %bitcast.core_ref.refs_0_, bf16[2048,16]{1,0:T(8,128)(2,1)} %copy.180.refs_1_, ...), custom_call_target="tpu_custom_call" | custom-call | flops 25769803776 | bytes 35651584 | tf_op jit(solution)/shard_map/expert_rows/pallas_call | solution.py:745
  235.8 49.1 %expert_rows.5 = (bf16[512,2048]{1,0:T(8,128)(2,1)}, bf16[512,2048]{1,0:T(8,128)(2,1)}, bf16[512,2176]{1,0:T(8,128)(2,1)}, bf16[512,2176]{1,0:T(8,128)(2,1)}, bf...) custom-call(s32[1]{0:T(128)} %bitcast.core_ref.refs_0_, bf16[2048,16]{1,0:T(8,128)(2,1)} %copy.180.refs_1_, ...), custom_call_target="tpu_custom_call" | custom-call | flops 25769803776 | bytes 35651584 | tf_op jit(solution)/shard_map/expert_rows/pallas_call | solution.py:745
  284.9 21.7 %expert_weight_grads.4 = (bf16[384,2048]{1,0:T(8,128)(2,1)}, bf16[384,2048]{1,0:T(8,128)(2,1)}, bf16[384,2048]{1,0:T(8,128)(2,1)}, bf16[384,2048]{1,0:T(8,128)(2,1)}) custom-call(s32[2]{0:T(128)} %pad_add_fusion.order_ref, bf16[4,2,128,2048]{3,2,1,0:T(8,128)(2,1)} %bitcast.111, bf16[4,2,128,2048]{3,2,1,0:T(8,128)(2,1)} %bitcast.25.refs_3_.refs_1_, ...), custom_call_target="tpu_custom_call" | custom-call | flops 12884901888 | bytes 29360128 | tf_op jit(solution)/shard_map/expert_weight_grads/pallas_call | solution.py:849
  308.7 42.6 %expert_rows.6 = (bf16[512,2048]{1,0:T(8,128)(2,1)}, bf16[512,2048]{1,0:T(8,128)(2,1)}, bf16[512,2176]{1,0:T(8,128)(2,1)}, bf16[512,2176]{1,0:T(8,128)(2,1)}, bf...) custom-call(s32[1]{0:T(128)} %bitcast.core_ref.refs_0_, bf16[2048,16]{1,0:T(8,128)(2,1)} %copy.180.refs_1_, ...), custom_call_target="tpu_custom_call" | custom-call | flops 25769803776 | bytes 35651584 | tf_op jit(solution)/shard_map/expert_rows/pallas_call | solution.py:745
  351.4 4.5 collective-permute-done.15
  355.9 3.5 add_convert_fusion.3.refs_13_
  359.5 42.6 %expert_rows.7 = (bf16[512,2048]{1,0:T(8,128)(2,1)}, bf16[512,2048]{1,0:T(8,128)(2,1)}, bf16[512,2176]{1,0:T(8,128)(2,1)}, bf16[512,2176]{1,0:T(8,128)(2,1)}, bf...) custom-call(s32[1]{0:T(128)} %bitcast.core_ref.refs_0_, bf16[2048,16]{1,0:T(8,128)(2,1)} %copy.180.refs_1_, ...), custom_call_target="tpu_custom_call" | custom-call | flops 25769803776 | bytes 35651584 | tf_op jit(solution)/shard_map/expert_rows/pallas_call | solution.py:745
  404.1 4.6 collective-permute-done.16
  408.7 3.5 add_convert_fusion.2.refs_14_
  419.4 22.0 %expert_weight_grads.5 = (bf16[384,2048]{1,0:T(8,128)(2,1)}, bf16[384,2048]{1,0:T(8,128)(2,1)}, bf16[384,2048]{1,0:T(8,128)(2,1)}, bf16[384,2048]{1,0:T(8,128)(2,1)}) custom-call(s32[2]{0:T(128)} %pad_add_fusion.1.order_ref, bf16[4,2,128,2048]{3,2,1,0:T(8,128)(2,1)} %bitcast.115, bf16[4,2,128,2048]{3,2,1,0:T(8,128)(2,1)} %bitcast.25.refs_3_.refs_1_, ...), custom_call_target="tpu_custom_call" | custom-call | flops 12884901888 | bytes 29360128 | tf_op jit(solution)/shard_map/expert_weight_grads/pallas_call | solution.py:849
  441.9 21.9 %expert_weight_grads.6.refs_12_ = bf16[4,768,2048]{2,1,0:T(8,128)(2,1)} custom-call(s32[2]{0:T(128)} %iota.29.order_ref, bf16[4,2,128,2048]{3,2,1,0:T(8,128)(2,1)} %bitcast.117, bf16[4,2,128,2048]{3,2,1,0:T(8,128)(2,1)} %bitcast.25.refs_3_.refs_1_, bf16[4,2,128,2048]{3,2,1,0:T(8,128)(2,1)} %bitcast.118, bf16[4,2,128,2048]{3,2,1,0:T(8,128)(2,1)} %bitcast.25.refs_3_.refs_1_, ...), custom_call_target="tpu_custom_call" | custom-call | flops 12884901888 | bytes 29360128 | tf_op jit(solution)/shard_map/expert_weight_grads/pallas_call | solution.py:849
  465.1 3.4 multiply_reduce_fusion.1
  468.5 4.0 fusion.52
  472.5 5.9 convolution_convert_fusion.2
  479.7 2.9 collective-permute-start.18
  486.1 3.8 fusion.53
  490.2 9.8 %collective-permute-done.17 = bf16[256,512]{1,0:T(8,128)(2,1)S(1)} collective-permute-done((bf16[256,512]{1,0:T(8,128)(2,1)S(1)}, bf16[256,512]{1,0:T(8,128)(2,1)S(1)}, u32[]{:S(2)}, u32[]{:S(2)}) %collective-permute-start.17) | collective-permute-done | bytes 262176 | tf_op jit(solution)/shard_map/ppermute | solution.py:1178
  500.0 2.8 collective-permute-done.18
  512.2 30.9 %attention_rows_back.1 = (f32[1024,512]{1,0:T(8,128)}, f32[1024,512]{1,0:T(8,128)}, bf16[1024,512]{1,0:T(8,128)(2,1)}, f32[4,1024,2]{2,1,0:T(8,128)}, f32[1,512]{1,0:T(1,128)}, /*index=5*/f32[1,512]{1,0:T(1,128)}) custom-call(f32[1024,512]{1,0:T(8,128)} %get-tuple-element.146.q_ref, f32[1024,512]{1,0:T(8,128)} %get-tuple-element.147.k_ref, ...), custom_call_target="tpu_custom_call" | custom-call | flops 4294967296 | bytes 12582912 | tf_op jit(solution)/shard_map/attention_rows_back/pallas_call | solution.py:547
  548.2 3.7 collective-permute-start.25
  551.9 2.6 collective-permute-start.27
  554.5 5.4 add_convert_fusion
  566.9 21.9 %expert_weight_grads.7 = bf16[4,768,2048]{2,1,0:T(8,128)(2,1)} custom-call(s32[2]{0:T(128)} %constant.101.clone.1.order_ref, bf16[4,2,128,2048]{3,2,1,0:T(8,128)(2,1)} %bitcast.119, bf16[4,2,128,2048]{3,2,1,0:T(8,128)(2,1)} %bitcast.25.refs_3_.refs_1_, bf16[4,2,128,2048]{3,2,1,0:T(8,128)(2,1)} %bitcast.120, ...), custom_call_target="tpu_custom_call", output_to_operand_aliasing={{}: (13, {})} | custom-call | flops 12884901888 | bytes 29360128 | tf_op jit(solution)/shard_map/expert_weight_grads/pallas_call | solution.py:849
  592.1 3.1 convolution_convert_fusion.3
  598.1 3.7 collective-permute-start.32
  608.9 8.6 %fusion.6 = bf16[1024,2048]{1,0:T(8,128)(2,1)S(1)} fusion(bf16[2048,512]{1,0:T(8,128)(2,1)} %wv_ref.1, bf16[2048,512]{1,0:T(8,128)(2,1)} %wk_ref.1, bf16[2048,512]{1,0:T(8,128)(2,1)S(1)} %copy-done.84, bf16[1024,512]{1,0:T(8,128)(2,1)S(1)} %copy-done.49, bf16[1024,512]{1,0:T(8,128)(2,1)S(1)} %subtract_convert_fusion, ...), kind=kOutput, calls=%fused_computation.18 | convolution fusion | flops 6472859648 | bytes 13631488 | tf_op jit(solution)/shard_map/dot_general | solution.py:401
  617.5 7.0 collective-permute-done.32
  624.5 3.3 collective-permute-done.33
  629.6 2.6 broadcast_select_fusion.16
  632.5 3.1 collective-permute-start.35
  635.7 7.4 convolution_convert_fusion
  643.9 12.2 %collective-permute-done.34 = bf16[256,2048]{1,0:T(8,128)(2,1)S(1)} collective-permute-done((bf16[256,2048]{1,0:T(8,128)(2,1)S(1)}, bf16[256,2048]{1,0:T(8,128)(2,1)S(1)}, u32[]{:S(2)}, u32[]{:S(2)}) %collective-permute-start.34) | collective-permute-done | bytes 1048608 | tf_op jit(solution)/shard_map/ppermute | solution.py:1200
  660.6 2.8 add_convert_fusion.6
  665.2 2.6 collective-permute-start.37
  671.0 19.7 %collective-permute-done.36 = bf16[256,2048]{1,0:T(8,128)(2,1)S(1)} collective-permute-done((bf16[256,2048]{1,0:T(8,128)(2,1)S(1)}, bf16[256,2048]{1,0:T(8,128)(2,1)S(1)}, u32[]{:S(2)}, u32[]{:S(2)}) %collective-permute-start.36) | collective-permute-done | bytes 1048608 | tf_op jit(solution)/shard_map/ppermute | solution.py:1200
  696.8 2.7 collective-permute-start.40
  704.5 17.6 %collective-permute-done.41 = bf16[128,1664]{1,0:T(8,128)(2,1)S(1)} collective-permute-done((bf16[128,1664]{1,0:T(8,128)(2,1)S(1)}, bf16[128,1664]{1,0:T(8,128)(2,1)S(1)}, u32[]{:S(2)}, u32[]{:S(2)}) %collective-permute-start.41) | collective-permute-done | bytes 426016 | tf_op jit(solution)/shard_map/ppermute | solution.py:872
  731.9 12.7 %collective-permute-done.46 = bf16[256,2048]{1,0:T(8,128)(2,1)S(1)} collective-permute-done((bf16[256,2048]{1,0:T(8,128)(2,1)S(1)}, bf16[256,2048]{1,0:T(8,128)(2,1)S(1)}, u32[]{:S(2)}, u32[]{:S(2)}) %collective-permute-start.46) | collective-permute-done | bytes 1048608 | tf_op jit(solution)/shard_map/ppermute | solution.py:872
  745.8 5.9 collective-permute-done.43
  754.6 2.5 collective-permute-start.48
  762.4 13.4 %collective-permute-done.49 = bf16[256,1664]{1,0:T(8,128)(2,1)S(1)} collective-permute-done((bf16[256,1664]{1,0:T(8,128)(2,1)S(1)}, bf16[256,1664]{1,0:T(8,128)(2,1)S(1)}, u32[]{:S(2)}, u32[]{:S(2)}) %collective-permute-start.49) | collective-permute-done | bytes 852000 | tf_op jit(solution)/shard_map/ppermute | solution.py:872
  779.4 3.4 slice_bitcast_fusion.1
  788.3 3.1 broadcast_select_fusion
  791.4 2.9 collective-permute-start.51
  797.7 2.5 copy.192
  800.2 4.1 copy.191
  808.9 8.4 collective-permute-done.55
  823.4 12.9 %collective-permute-done.51 = bf16[256,2048]{1,0:T(8,128)(2,1)S(1)} collective-permute-done((bf16[256,2048]{1,0:T(8,128)(2,1)}, bf16[256,2048]{1,0:T(8,128)(2,1)S(1)}, u32[]{:S(2)}, u32[]{:S(2)}) %collective-permute-start.51) | collective-permute-done | bytes 1048608 | tf_op jit(solution)/shard_map/ppermute | solution.py:1201
  837.9 3.0 select_dynamic-update-slice_fusion.1
  840.9 2.9 select_dynamic-update-slice_fusion
  (427 shorter events, 164.2 us)
Async XLA Ops:
  7.2 187.6 %all-gather.7.cloned.1.call-start = ((), (), s32[]{:S(2)}) async-start(), calls=%async_computation.9 | async-start | bytes 15728640 | tf_op jit(solution)/shard_map/all_gather | solution.py:944
  16.8 291.9 %all-gather.5.cloned.1.call-start = ((), (), s32[]{:S(2)}) async-start(), calls=%async_computation.8 | async-start | bytes 15728640 | tf_op jit(solution)/shard_map/all_gather | solution.py:944
  19.4 49.5 %collective-permute-start.3 = (bf16[256,2048]{1,0:T(8,128)(2,1)}, bf16[256,2048]{1,0:T(8,128)(2,1)S(1)}, u32[]{:S(2)}, u32[]{:S(2)}) collective-permute-start(bf16[256,2048]{1,0:T(8,128)(2,1)} %constant_dynamic-slice_fusion.6), channel_id=1, source_target_pairs={{0,1},{1,0},{2,3},{3,2},{4,5},{5,4},{6,7},{7,6},{8,9},{9,8},{10,11... | collective-permute-start | bytes 3145736 | tf_op jit(solution)/shard_map/ppermute | solution.py:1178
  21.0 47.9 %collective-permute-start.4 = (bf16[256,2048]{1,0:T(8,128)(2,1)}, bf16[256,2048]{1,0:T(8,128)(2,1)}, u32[]{:S(2)}, u32[]{:S(2)}) collective-permute-start(bf16[256,2048]{1,0:T(8,128)(2,1)} %constant_dynamic-slice_fusion.6), channel_id=1, source_target_pairs={{0,2},{1,3},{2,0},{3,1},{4,6},{5,7},{6,4},{7,5},{8,10},{9,11},{10,... | collective-permute-start | bytes 3145736 | tf_op jit(solution)/shard_map/ppermute | solution.py:1178
  48.8 20.0 %collective-permute-start = (f32[16,128]{1,0:T(8,128)S(1)}, f32[16,128]{1,0:T(8,128)S(1)}, u32[]{:S(2)}, u32[]{:S(2)}) collective-permute-start(f32[16,128]{1,0:T(8,128)S(1)} %reshape.249), channel_id=1, source_target_pairs={{0,1},{1,2},{2,3},{3,0},{4,5},{5,6},{6,7},{7,4},{8,9},{9,10},{10,1... | collective-permute-start | bytes 24584 | tf_op jit(solution)/shard_map/ppermute | solution.py:1274
  49.3 19.5 %collective-permute-start.1 = (f32[16,128]{1,0:T(8,128)S(1)}, f32[16,128]{1,0:T(8,128)S(1)}, u32[]{:S(2)}, u32[]{:S(2)}) collective-permute-start(f32[16,128]{1,0:T(8,128)S(1)} %reshape.249), channel_id=1, source_target_pairs={{0,2},{1,3},{2,0},{3,1},{4,6},{5,7},{6,4},{7,5},{8,10},{9,11},{10,... | collective-permute-start | bytes 24584 | tf_op jit(solution)/shard_map/ppermute | solution.py:1274
  52.0 16.9 %collective-permute-start.2 = (f32[16,128]{1,0:T(8,128)S(1)}, f32[16,128]{1,0:T(8,128)S(1)}, u32[]{:S(2)}, u32[]{:S(2)}) collective-permute-start(f32[16,128]{1,0:T(8,128)S(1)} %reshape.249), channel_id=1, source_target_pairs={{0,3},{1,0},{2,1},{3,2},{4,7},{5,4},{6,5},{7,6},{8,11},{9,8},{10,9... | collective-permute-start | bytes 24584 | tf_op jit(solution)/shard_map/ppermute | solution.py:1274
  68.9 24.3 %collective-permute-start.5 = (bf16[256,2048]{1,0:T(8,128)(2,1)}, bf16[256,2048]{1,0:T(8,128)(2,1)}, u32[]{:S(2)}, u32[]{:S(2)}) collective-permute-start(bf16[256,2048]{1,0:T(8,128)(2,1)} %collective-permute-done.4), channel_id=1, source_target_pairs={{0,1},{1,0},{2,3},{3,2},{4,5},{5,4},{6,7},{7,6},{8,9},{9,8},{10,11... | collective-permute-start | bytes 3145736 | tf_op jit(solution)/shard_map/ppermute | solution.py:1178
  93.2 50.7 %copy-start.80 = (s32[1024,8]{0,1:T(8,128)S(1)}, s32[1024,8]{0,1:T(8,128)}, u32[]{:S(2)}) copy-start(s32[1024,8]{0,1:T(8,128)} %param.20) | copy-start | bytes 98308
  93.2 50.8 %copy-start.14 = (bf16[512,2048]{1,0:T(8,128)(2,1)S(1)}, bf16[512,2048]{1,0:T(8,128)(2,1)}, u32[]{:S(2)}) copy-start(bf16[512,2048]{1,0:T(8,128)(2,1)} %param.25) | copy-start | bytes 6291460
  93.3 310.9 %reduce-scatter.5.cloned.1.call-start = ((), (), s32[]{:S(2)}) async-start(), calls=%async_computation.4 | async-start | bytes 2785280 | tf_op jit(solution)/shard_map/reduce_scatter | solution.py:909
  93.6 45.3 %collective-permute-start.6 = (bf16[1024,512]{1,0:T(8,128)(2,1)}, bf16[1024,512]{1,0:T(8,128)(2,1)S(1)}, u32[]{:S(2)}, u32[]{:S(2)}) collective-permute-start(bf16[1024,512]{1,0:T(8,128)(2,1)} %get-tuple-element.152.refs_0_), channel_id=1, source_target_pairs={{0,1},{1,0},{2,3},{3,2},{4,5},{5,4},{6,7},{7,6},{8,9},{9,8},{10,11... | collective-permute-start | bytes 3145736 | tf_op jit(solution)/shard_map/ppermute | solution.py:1178
  95.4 46.4 %collective-permute-start.7 = (bf16[1024,512]{1,0:T(8,128)(2,1)}, bf16[1024,512]{1,0:T(8,128)(2,1)S(1)}, u32[]{:S(2)}, u32[]{:S(2)}) collective-permute-start(bf16[1024,512]{1,0:T(8,128)(2,1)} %get-tuple-element.152.refs_0_), channel_id=1, source_target_pairs={{0,2},{1,3},{2,0},{3,1},{4,6},{5,7},{6,4},{7,5},{8,10},{9,11},{10,... | collective-permute-start | bytes 3145736 | tf_op jit(solution)/shard_map/ppermute | solution.py:1178
  143.8 5.7 collective-permute-start.9
  144.2 25.6 %collective-permute-start.8 = (bf16[1024,512]{1,0:T(8,128)(2,1)S(1)}, bf16[1024,512]{1,0:T(8,128)(2,1)S(1)}, u32[]{:S(2)}, u32[]{:S(2)}) collective-permute-start(bf16[1024,512]{1,0:T(8,128)(2,1)S(1)} %collective-permute-done.7.refs_2_), channel_id=1, source_target_pairs={{0,1},{1,0},{2,3},{3,2},{4,5},{5,4},{6,7},{7,6},{8,9},{9,8},{10,11... | collective-permute-start | bytes 3145736 | tf_op jit(solution)/shard_map/ppermute | solution.py:1178
  144.7 49.3 %collective-permute-start.11 = (bf16[1024,2048]{1,0:T(8,128)(2,1)}, bf16[1024,2048]{1,0:T(8,128)(2,1)}, u32[]{:S(2)}, u32[]{:S(2)}) collective-permute-start(bf16[1024,2048]{1,0:T(8,128)(2,1)} %param.18), channel_id=1, source_target_pairs={{0,4},{4,0},{8,12},{12,8},{16,20},{20,16},{24,28},{28,24},{1,5},{5... | collective-permute-start | bytes 12582920 | tf_op jit(solution)/shard_map/ppermute | solution.py:872
  187.2 7.5 collective-permute-start.10
  187.2 5.9 collective-permute-start.12
  306.6 44.7 %collective-permute-start.13 = (bf16[384,2048]{1,0:T(8,128)(2,1)}, bf16[384,2048]{1,0:T(8,128)(2,1)S(1)}, u32[]{:S(2)}, u32[]{:S(2)}) collective-permute-start(bf16[384,2048]{1,0:T(8,128)(2,1)} %get-tuple-element.178.refs_13_), channel_id=1, source_target_pairs={{0,8},{4,12},{8,0},{12,4},{16,24},{20,28},{24,16},{28,20},{1,9},{5... | collective-permute-start | bytes 4718600 | tf_op jit(solution)/shard_map/ppermute | solution.py:872
  308.2 43.1 %collective-permute-start.14 = (bf16[384,2048]{1,0:T(8,128)(2,1)}, bf16[384,2048]{1,0:T(8,128)(2,1)}, u32[]{:S(2)}, u32[]{:S(2)}) collective-permute-start(bf16[384,2048]{1,0:T(8,128)(2,1)} %get-tuple-element.179.refs_14_), channel_id=1, source_target_pairs={{0,16},{4,20},{8,24},{12,28},{16,0},{20,4},{24,8},{28,12},{1,17},{... | collective-permute-start | bytes 4718600 | tf_op jit(solution)/shard_map/ppermute | solution.py:872
  351.3 4.6 collective-permute-start.15
  359.4 104.4 %reduce-scatter.7.cloned.1.call-start = ((), (), s32[]{:S(2)}) async-start(), calls=%async_computation.5 | async-start | bytes 2785280 | tf_op jit(solution)/shard_map/reduce_scatter | solution.py:909
  404.1 4.6 collective-permute-start.16
  412.2 178.1 %reduce-scatter.9.cloned.1.call-start = ((), (), s32[]{:S(2)}) async-start(), calls=%async_computation.6 | async-start | bytes 5242880 | tf_op jit(solution)/shard_map/reduce_scatter | solution.py:909
  479.0 23.9 %collective-permute-start.20 = (bf16[512,2048]{1,0:T(8,128)(2,1)}, bf16[512,2048]{1,0:T(8,128)(2,1)S(1)}, u32[]{:S(2)}, u32[]{:S(2)}) collective-permute-start(bf16[512,2048]{1,0:T(8,128)(2,1)} %get-tuple-element.209), channel_id=1, source_target_pairs={{0,4},{4,0},{8,12},{12,8},{16,20},{20,16},{24,28},{28,24},{1,5},{5... | collective-permute-start | bytes 6291464 | tf_op jit(solution)/shard_map/ppermute | solution.py:872
  479.2 24.6 %collective-permute-start.21 = (bf16[512,2048]{1,0:T(8,128)(2,1)}, bf16[512,2048]{1,0:T(8,128)(2,1)S(1)}, u32[]{:S(2)}, u32[]{:S(2)}) collective-permute-start(bf16[512,2048]{1,0:T(8,128)(2,1)} %get-tuple-element.211), channel_id=1, source_target_pairs={{0,4},{4,0},{8,12},{12,8},{16,20},{20,16},{24,28},{28,24},{1,5},{5... | collective-permute-start | bytes 6291464 | tf_op jit(solution)/shard_map/ppermute | solution.py:872
  479.6 23.1 %collective-permute-start.19 = (bf16[256,512]{1,0:T(8,128)(2,1)S(1)}, bf16[256,512]{1,0:T(8,128)(2,1)S(1)}, u32[]{:S(2)}, u32[]{:S(2)}) collective-permute-start(bf16[256,512]{1,0:T(8,128)(2,1)S(1)} %pad_maximum_fusion.21), channel_id=1, source_target_pairs={{0,3},{1,2},{2,1},{3,0},{4,7},{5,6},{6,5},{7,4},{8,11},{9,10},{10,... | collective-permute-start | bytes 786440 | tf_op jit(solution)/shard_map/ppermute | solution.py:1178
  479.7 23.0 %collective-permute-start.18 = (bf16[256,512]{1,0:T(8,128)(2,1)S(1)}, bf16[256,512]{1,0:T(8,128)(2,1)S(1)}, u32[]{:S(2)}, u32[]{:S(2)}) collective-permute-start(bf16[256,512]{1,0:T(8,128)(2,1)S(1)} %pad_maximum_fusion.20), channel_id=1, source_target_pairs={{0,2},{1,3},{2,0},{3,1},{4,6},{5,7},{6,4},{7,5},{8,10},{9,11},{10,... | collective-permute-start | bytes 786440 | tf_op jit(solution)/shard_map/ppermute | solution.py:1178
  482.6 17.3 %collective-permute-start.17 = (bf16[256,512]{1,0:T(8,128)(2,1)S(1)}, bf16[256,512]{1,0:T(8,128)(2,1)S(1)}, u32[]{:S(2)}, u32[]{:S(2)}) collective-permute-start(bf16[256,512]{1,0:T(8,128)(2,1)S(1)} %pad_maximum_fusion.19), channel_id=1, source_target_pairs={{0,1},{1,0},{2,3},{3,2},{4,5},{5,4},{6,7},{7,6},{8,9},{9,8},{10,11... | collective-permute-start | bytes 786440 | tf_op jit(solution)/shard_map/ppermute | solution.py:1178
  507.9 271.5 %reduce-scatter.11.cloned.1.call-start = ((), (), s32[]{:S(2)}) async-start(), calls=%async_computation.7 | async-start | bytes 15728640 | tf_op jit(solution)/shard_map/reduce_scatter | solution.py:1077
  508.0 38.2 %collective-permute-start.22 = (bf16[1024,2048]{1,0:T(8,128)(2,1)}, bf16[1024,2048]{1,0:T(8,128)(2,1)}, u32[]{:S(2)}, u32[]{:S(2)}) collective-permute-start(bf16[1024,2048]{1,0:T(8,128)(2,1)} %get-tuple-element.214.rest_0_), channel_id=1, source_target_pairs={{0,4},{4,0},{8,12},{12,8},{16,20},{20,16},{24,28},{28,24},{1,5},{5... | collective-permute-start | bytes 12582920 | tf_op jit(solution)/shard_map/ppermute | solution.py:872
  508.1 37.5 %collective-permute-start.23 = (bf16[384,2048]{1,0:T(8,128)(2,1)}, bf16[384,2048]{1,0:T(8,128)(2,1)S(1)}, u32[]{:S(2)}, u32[]{:S(2)}) collective-permute-start(bf16[384,2048]{1,0:T(8,128)(2,1)} %get-tuple-element.201.refs_12_), channel_id=1, source_target_pairs={{0,16},{4,20},{8,24},{12,28},{16,0},{20,4},{24,8},{28,12},{1,17},{... | collective-permute-start | bytes 4718600 | tf_op jit(solution)/shard_map/ppermute | solution.py:872
  508.6 37.6 %collective-permute-start.24 = (bf16[384,2048]{1,0:T(8,128)(2,1)}, bf16[384,2048]{1,0:T(8,128)(2,1)}, u32[]{:S(2)}, u32[]{:S(2)}) collective-permute-start(bf16[384,2048]{1,0:T(8,128)(2,1)} %get-tuple-element.221), channel_id=1, source_target_pairs={{0,8},{4,12},{8,0},{12,4},{16,24},{20,28},{24,16},{28,20},{1,9},{5... | collective-permute-start | bytes 4718600 | tf_op jit(solution)/shard_map/ppermute | solution.py:872
  510.2 78.7 %collective-permute-start.30 = (bf16[384,2048]{1,0:T(8,128)(2,1)}, bf16[384,2048]{1,0:T(8,128)(2,1)}, u32[]{:S(2)}, u32[]{:S(2)}) collective-permute-start(bf16[384,2048]{1,0:T(8,128)(2,1)} %get-tuple-element.227), channel_id=1, source_target_pairs={{0,16},{4,20},{8,24},{12,28},{16,0},{20,4},{24,8},{28,12},{1,17},{... | collective-permute-start | bytes 4718600 | tf_op jit(solution)/shard_map/ppermute | solution.py:872
  511.6 77.3 %collective-permute-start.31 = (bf16[384,2048]{1,0:T(8,128)(2,1)}, bf16[384,2048]{1,0:T(8,128)(2,1)}, u32[]{:S(2)}, u32[]{:S(2)}) collective-permute-start(bf16[384,2048]{1,0:T(8,128)(2,1)} %get-tuple-element.228), channel_id=1, source_target_pairs={{0,8},{4,12},{8,0},{12,4},{16,24},{20,28},{24,16},{28,20},{1,9},{5... | collective-permute-start | bytes 4718600 | tf_op jit(solution)/shard_map/ppermute | solution.py:872
  548.2 15.1 %collective-permute-start.25 = (f32[16,128]{1,0:T(8,128)S(1)}, f32[16,128]{1,0:T(8,128)S(1)}, u32[]{:S(2)}, u32[]{:S(2)}) collective-permute-start(f32[16,128]{1,0:T(8,128)S(1)} %reshape.258), channel_id=1, source_target_pairs={{0,1},{1,2},{2,3},{3,0},{4,5},{5,6},{6,7},{7,4},{8,9},{9,10},{10,1... | collective-permute-start | bytes 24584 | tf_op jit(solution)/shard_map/ppermute | solution.py:1274
  551.9 13.0 %collective-permute-start.26 = (f32[16,128]{1,0:T(8,128)S(1)}, f32[16,128]{1,0:T(8,128)S(1)}, u32[]{:S(2)}, u32[]{:S(2)}) collective-permute-start(f32[16,128]{1,0:T(8,128)S(1)} %reshape.258), channel_id=1, source_target_pairs={{0,2},{1,3},{2,0},{3,1},{4,6},{5,7},{6,4},{7,5},{8,10},{9,11},{10,... | collective-permute-start | bytes 24584 | tf_op jit(solution)/shard_map/ppermute | solution.py:1274
  551.9 14.4 %collective-permute-start.27 = (f32[16,128]{1,0:T(8,128)S(1)}, f32[16,128]{1,0:T(8,128)S(1)}, u32[]{:S(2)}, u32[]{:S(2)}) collective-permute-start(f32[16,128]{1,0:T(8,128)S(1)} %reshape.258), channel_id=1, source_target_pairs={{0,3},{1,0},{2,1},{3,2},{4,7},{5,4},{6,5},{7,6},{8,11},{9,8},{10,9... | collective-permute-start | bytes 24584 | tf_op jit(solution)/shard_map/ppermute | solution.py:1274
  563.3 26.9 %collective-permute-start.28 = (bf16[128,2048]{1,0:T(8,128)(2,1)}, bf16[128,2048]{1,0:T(8,128)(2,1)S(1)}, u32[]{:S(2)}, u32[]{:S(2)}) collective-permute-start(bf16[128,2048]{1,0:T(8,128)(2,1)} %get-tuple-element.393), channel_id=1, source_target_pairs={{0,8},{4,12},{8,0},{12,4},{16,24},{20,28},{24,16},{28,20},{1,9},{5... | collective-permute-start | bytes 1572872 | tf_op jit(solution)/shard_map/ppermute | solution.py:872
  564.9 25.4 %collective-permute-start.29 = (bf16[128,2048]{1,0:T(8,128)(2,1)}, bf16[128,2048]{1,0:T(8,128)(2,1)S(1)}, u32[]{:S(2)}, u32[]{:S(2)}) collective-permute-start(bf16[128,2048]{1,0:T(8,128)(2,1)} %get-tuple-element.392), channel_id=1, source_target_pairs={{0,16},{4,20},{8,24},{12,28},{16,0},{20,4},{24,8},{28,12},{1,17},{... | collective-permute-start | bytes 1572872 | tf_op jit(solution)/shard_map/ppermute | solution.py:872
  598.1 26.4 %collective-permute-start.32 = (bf16[256,2048]{1,0:T(8,128)(2,1)S(1)}, bf16[256,2048]{1,0:T(8,128)(2,1)S(1)}, u32[]{:S(2)}, u32[]{:S(2)}) collective-permute-start(bf16[256,2048]{1,0:T(8,128)(2,1)S(1)} %get-tuple-element.383), channel_id=1, source_target_pairs={{0,1},{1,0},{2,3},{3,2},{4,5},{5,4},{6,7},{7,6},{8,9},{9,8},{10,11... | collective-permute-start | bytes 3145736 | tf_op jit(solution)/shard_map/ppermute | solution.py:1200
  601.9 26.0 %collective-permute-start.33 = (bf16[256,2048]{1,0:T(8,128)(2,1)S(1)}, bf16[256,2048]{1,0:T(8,128)(2,1)S(1)}, u32[]{:S(2)}, u32[]{:S(2)}) collective-permute-start(bf16[256,2048]{1,0:T(8,128)(2,1)S(1)} %get-tuple-element.383), channel_id=1, source_target_pairs={{1,2},{2,1},{0,0},{3,3},{5,6},{6,5},{4,4},{7,7},{9,10},{10,9},{8,8... | collective-permute-start | bytes 3145736 | tf_op jit(solution)/shard_map/ppermute | solution.py:1201
  632.4 23.7 %collective-permute-start.34 = (bf16[256,2048]{1,0:T(8,128)(2,1)S(1)}, bf16[256,2048]{1,0:T(8,128)(2,1)S(1)}, u32[]{:S(2)}, u32[]{:S(2)}) collective-permute-start(bf16[256,2048]{1,0:T(8,128)(2,1)S(1)} %broadcast_select_fusion.17), channel_id=1, source_target_pairs={{0,1},{1,0},{2,3},{3,2},{4,5},{5,4},{6,7},{7,6},{8,9},{9,8},{10,11... | collective-permute-start | bytes 3145736 | tf_op jit(solution)/shard_map/ppermute | solution.py:1200
  632.5 25.7 %collective-permute-start.35 = (bf16[256,2048]{1,0:T(8,128)(2,1)S(1)}, bf16[256,2048]{1,0:T(8,128)(2,1)S(1)}, u32[]{:S(2)}, u32[]{:S(2)}) collective-permute-start(bf16[256,2048]{1,0:T(8,128)(2,1)S(1)} %get-tuple-element.379), channel_id=1, source_target_pairs={{1,2},{2,1},{0,0},{3,3},{5,6},{6,5},{4,4},{7,7},{9,10},{10,9},{8,8... | collective-permute-start | bytes 3145736 | tf_op jit(solution)/shard_map/ppermute | solution.py:1201
  658.1 34.6 %collective-permute-start.38 = (bf16[1024,1664]{1,0:T(8,128)(2,1)S(1)}, bf16[1024,1664]{1,0:T(8,128)(2,1)S(1)}, u32[]{:S(2)}, u32[]{:S(2)}) collective-permute-start(bf16[1024,1664]{1,0:T(8,128)(2,1)S(1)} %get-tuple-element.244), channel_id=1, source_target_pairs={{0,4},{4,0},{8,12},{12,8},{16,20},{20,16},{24,28},{28,24},{1,5},{5... | collective-permute-start | bytes 10223624 | tf_op jit(solution)/shard_map/ppermute | solution.py:872
  665.1 25.6 %collective-permute-start.36 = (bf16[256,2048]{1,0:T(8,128)(2,1)S(1)}, bf16[256,2048]{1,0:T(8,128)(2,1)S(1)}, u32[]{:S(2)}, u32[]{:S(2)}) collective-permute-start(bf16[256,2048]{1,0:T(8,128)(2,1)S(1)} %broadcast_select_fusion.13), channel_id=1, source_target_pairs={{0,1},{1,0},{2,3},{3,2},{4,5},{5,4},{6,7},{7,6},{8,9},{9,8},{10,11... | collective-permute-start | bytes 3145736 | tf_op jit(solution)/shard_map/ppermute | solution.py:1200
  665.2 27.5 %collective-permute-start.37 = (bf16[256,2048]{1,0:T(8,128)(2,1)S(1)}, bf16[256,2048]{1,0:T(8,128)(2,1)S(1)}, u32[]{:S(2)}, u32[]{:S(2)}) collective-permute-start(bf16[256,2048]{1,0:T(8,128)(2,1)S(1)} %get-tuple-element.376), channel_id=1, source_target_pairs={{1,2},{2,1},{0,0},{3,3},{5,6},{6,5},{4,4},{7,7},{9,10},{10,9},{8,8... | collective-permute-start | bytes 3145736 | tf_op jit(solution)/shard_map/ppermute | solution.py:1201
  696.8 25.9 %collective-permute-start.39 = (bf16[256,2048]{1,0:T(8,128)(2,1)}, bf16[256,2048]{1,0:T(8,128)(2,1)S(1)}, u32[]{:S(2)}, u32[]{:S(2)}) collective-permute-start(bf16[256,2048]{1,0:T(8,128)(2,1)} %broadcast_select_fusion.9), channel_id=1, source_target_pairs={{0,1},{1,0},{2,3},{3,2},{4,5},{5,4},{6,7},{7,6},{8,9},{9,8},{10,11... | collective-permute-start | bytes 3145736 | tf_op jit(solution)/shard_map/ppermute | solution.py:1200
  696.8 26.7 %collective-permute-start.40 = (bf16[256,2048]{1,0:T(8,128)(2,1)S(1)}, bf16[256,2048]{1,0:T(8,128)(2,1)S(1)}, u32[]{:S(2)}, u32[]{:S(2)}) collective-permute-start(bf16[256,2048]{1,0:T(8,128)(2,1)S(1)} %get-tuple-element.373), channel_id=1, source_target_pairs={{1,2},{2,1},{0,0},{3,3},{5,6},{6,5},{4,4},{7,7},{9,10},{10,9},{8,8... | collective-permute-start | bytes 3145736 | tf_op jit(solution)/shard_map/ppermute | solution.py:1201
  700.6 21.5 %collective-permute-start.41 = (bf16[128,1664]{1,0:T(8,128)(2,1)S(1)}, bf16[128,1664]{1,0:T(8,128)(2,1)S(1)}, u32[]{:S(2)}, u32[]{:S(2)}) collective-permute-start(bf16[128,1664]{1,0:T(8,128)(2,1)S(1)} %get-tuple-element.399), channel_id=1, source_target_pairs={{0,8},{4,12},{8,0},{12,4},{16,24},{20,28},{24,16},{28,20},{1,9},{5... | collective-permute-start | bytes 1277960 | tf_op jit(solution)/shard_map/ppermute | solution.py:872
  701.9 20.8 %collective-permute-start.42 = (bf16[128,1664]{1,0:T(8,128)(2,1)S(1)}, bf16[128,1664]{1,0:T(8,128)(2,1)S(1)}, u32[]{:S(2)}, u32[]{:S(2)}) collective-permute-start(bf16[128,1664]{1,0:T(8,128)(2,1)S(1)} %get-tuple-element.398), channel_id=1, source_target_pairs={{0,16},{4,20},{8,24},{12,28},{16,0},{20,4},{24,8},{28,12},{1,17},{... | collective-permute-start | bytes 1277960 | tf_op jit(solution)/shard_map/ppermute | solution.py:872
  703.1 41.5 %collective-permute-start.46 = (bf16[256,2048]{1,0:T(8,128)(2,1)S(1)}, bf16[256,2048]{1,0:T(8,128)(2,1)S(1)}, u32[]{:S(2)}, u32[]{:S(2)}) collective-permute-start(bf16[256,2048]{1,0:T(8,128)(2,1)S(1)} %pad_maximum_fusion.11), channel_id=1, source_target_pairs={{0,8},{4,12},{8,0},{12,4},{16,24},{20,28},{24,16},{28,20},{1,9},{5... | collective-permute-start | bytes 3145736 | tf_op jit(solution)/shard_map/ppermute | solution.py:872
  722.1 23.6 %collective-permute-start.45 = (bf16[256,2048]{1,0:T(8,128)(2,1)S(1)}, bf16[256,2048]{1,0:T(8,128)(2,1)S(1)}, u32[]{:S(2)}, u32[]{:S(2)}) collective-permute-start(bf16[256,2048]{1,0:T(8,128)(2,1)S(1)} %pad_maximum_fusion.10), channel_id=1, source_target_pairs={{0,16},{4,20},{8,24},{12,28},{16,0},{20,4},{24,8},{28,12},{1,17},{... | collective-permute-start | bytes 3145736 | tf_op jit(solution)/shard_map/ppermute | solution.py:872
  727.7 24.0 %collective-permute-start.43 = (bf16[256,2048]{1,0:T(8,128)(2,1)S(1)}, bf16[256,2048]{1,0:T(8,128)(2,1)S(1)}, u32[]{:S(2)}, u32[]{:S(2)}) collective-permute-start(bf16[256,2048]{1,0:T(8,128)(2,1)S(1)} %get-tuple-element.372), channel_id=1, source_target_pairs={{0,1},{1,0},{2,3},{3,2},{4,5},{5,4},{6,7},{7,6},{8,9},{9,8},{10,11... | collective-permute-start | bytes 3145736 | tf_op jit(solution)/shard_map/ppermute | solution.py:1200
  728.0 25.6 %collective-permute-start.44 = (bf16[256,2048]{1,0:T(8,128)(2,1)S(1)}, bf16[256,2048]{1,0:T(8,128)(2,1)S(1)}, u32[]{:S(2)}, u32[]{:S(2)}) collective-permute-start(bf16[256,2048]{1,0:T(8,128)(2,1)S(1)} %get-tuple-element.372), channel_id=1, source_target_pairs={{1,2},{2,1},{0,0},{3,3},{5,6},{6,5},{4,4},{7,7},{9,10},{10,9},{8,8... | collective-permute-start | bytes 3145736 | tf_op jit(solution)/shard_map/ppermute | solution.py:1201
  730.6 31.8 %collective-permute-start.50 = (bf16[256,1664]{1,0:T(8,128)(2,1)S(1)}, bf16[256,1664]{1,0:T(8,128)(2,1)S(1)}, u32[]{:S(2)}, u32[]{:S(2)}) collective-permute-start(bf16[256,1664]{1,0:T(8,128)(2,1)S(1)} %pad_maximum_fusion.13), channel_id=1, source_target_pairs={{0,8},{4,12},{8,0},{12,4},{16,24},{20,28},{24,16},{28,20},{1,9},{5... | collective-permute-start | bytes 2555912 | tf_op jit(solution)/shard_map/ppermute | solution.py:872
  754.6 22.9 %collective-permute-start.47 = (bf16[256,2048]{1,0:T(8,128)(2,1)S(1)}, bf16[256,2048]{1,0:T(8,128)(2,1)}, u32[]{:S(2)}, u32[]{:S(2)}) collective-permute-start(bf16[256,2048]{1,0:T(8,128)(2,1)S(1)} %get-tuple-element.408), channel_id=1, source_target_pairs={{0,1},{1,0},{2,3},{3,2},{4,5},{5,4},{6,7},{7,6},{8,9},{9,8},{10,11... | collective-permute-start | bytes 3145736 | tf_op jit(solution)/shard_map/ppermute | solution.py:1200
  754.6 24.8 %collective-permute-start.48 = (bf16[256,2048]{1,0:T(8,128)(2,1)S(1)}, bf16[256,2048]{1,0:T(8,128)(2,1)}, u32[]{:S(2)}, u32[]{:S(2)}) collective-permute-start(bf16[256,2048]{1,0:T(8,128)(2,1)S(1)} %get-tuple-element.407), channel_id=1, source_target_pairs={{1,2},{2,1},{0,0},{3,3},{5,6},{6,5},{4,4},{7,7},{9,10},{10,9},{8,8... | collective-permute-start | bytes 3145736 | tf_op jit(solution)/shard_map/ppermute | solution.py:1201
  757.2 18.6 %collective-permute-start.49 = (bf16[256,1664]{1,0:T(8,128)(2,1)S(1)}, bf16[256,1664]{1,0:T(8,128)(2,1)S(1)}, u32[]{:S(2)}, u32[]{:S(2)}) collective-permute-start(bf16[256,1664]{1,0:T(8,128)(2,1)S(1)} %pad_maximum_fusion.12), channel_id=1, source_target_pairs={{0,16},{4,20},{8,24},{12,28},{16,0},{20,4},{24,8},{28,12},{1,17},{... | collective-permute-start | bytes 2555912 | tf_op jit(solution)/shard_map/ppermute | solution.py:872
  784.8 20.9 %collective-permute-start.53 = (bf16[256,640]{1,0:T(8,128)(2,1)}, bf16[256,640]{1,0:T(8,128)(2,1)}, u32[]{:S(2)}, u32[]{:S(2)}) collective-permute-start(bf16[256,640]{1,0:T(8,128)(2,1)} %get-tuple-element.431), channel_id=1, source_target_pairs={{0,1},{1,0},{2,3},{3,2},{4,5},{5,4},{6,7},{7,6},{8,9},{9,8},{10,11... | collective-permute-start | bytes 983048 | tf_op jit(solution)/shard_map/ppermute | solution.py:1178
  784.8 23.0 %collective-permute-start.54 = (bf16[256,640]{1,0:T(8,128)(2,1)}, bf16[256,640]{1,0:T(8,128)(2,1)}, u32[]{:S(2)}, u32[]{:S(2)}) collective-permute-start(bf16[256,640]{1,0:T(8,128)(2,1)} %get-tuple-element.432), channel_id=1, source_target_pairs={{0,2},{1,3},{2,0},{3,1},{4,6},{5,7},{6,4},{7,5},{8,10},{9,11},{10,... | collective-permute-start | bytes 983048 | tf_op jit(solution)/shard_map/ppermute | solution.py:1178
  787.1 30.2 %collective-permute-start.55 = (bf16[256,640]{1,0:T(8,128)(2,1)S(1)}, bf16[256,640]{1,0:T(8,128)(2,1)}, u32[]{:S(2)}, u32[]{:S(2)}) collective-permute-start(bf16[256,640]{1,0:T(8,128)(2,1)S(1)} %get-tuple-element.433), channel_id=1, source_target_pairs={{0,3},{1,2},{2,1},{3,0},{4,7},{5,6},{6,5},{7,4},{8,11},{9,10},{10,... | collective-permute-start | bytes 983048 | tf_op jit(solution)/shard_map/ppermute | solution.py:1178
  791.4 44.8 %collective-permute-start.51 = (bf16[256,2048]{1,0:T(8,128)(2,1)}, bf16[256,2048]{1,0:T(8,128)(2,1)S(1)}, u32[]{:S(2)}, u32[]{:S(2)}) collective-permute-start(bf16[256,2048]{1,0:T(8,128)(2,1)} %get-tuple-element.406), channel_id=1, source_target_pairs={{1,2},{2,1},{0,0},{3,3},{5,6},{6,5},{4,4},{7,7},{9,10},{10,9},{8,8... | collective-permute-start | bytes 3145736 | tf_op jit(solution)/shard_map/ppermute | solution.py:1201
  794.3 42.0 %collective-permute-start.52 = (bf16[256,2048]{1,0:T(8,128)(2,1)}, bf16[256,2048]{1,0:T(8,128)(2,1)}, u32[]{:S(2)}, u32[]{:S(2)}) collective-permute-start(bf16[256,2048]{1,0:T(8,128)(2,1)} %get-tuple-element.405), channel_id=1, source_target_pairs={{0,1},{1,0},{2,3},{3,2},{4,5},{5,4},{6,7},{7,6},{8,9},{9,8},{10,11... | collective-permute-start | bytes 3145736 | tf_op jit(solution)/shard_map/ppermute | solution.py:1200
  (84 other events, 675.6 us)
Sparse Core Ops, SparseCore 0:
  16.9 123.5 all-gather.6
  142.4 122.5 all-gather.4
  359.6 44.5 reduce-scatter.4
  412.3 45.4 reduce-scatter.6
  508.1 80.7 reduce-scatter.8
  592.2 131.5 reduce-scatter.10

commit v3 on v2

--- a/solution.py
+++ b/solution.py
@@ -391,10 +391,11 @@
 VMEM_BYTES = 62 * 2**20
 COLUMN_TILE = 512
 ROW_TILE = 512
-QUERY_TILE = 256
-EXPERT_STEP = 2
+QUERY_TILE = 512
+BACK_TILE = 128
 HIDDEN_TILE = 256
 LANES = 128
+LOG2_E = 1.4426950408889634
 
 
 def mul(left, right, dims=NN):
@@ -409,14 +410,17 @@
     return pl.BlockSpec(shape, lambda i: (0,) * len(shape), pipeline_mode=pl.Buffered(1))
 
 
-def softmax_block(queries, keys, seg_rows, seg_columns, start, scale):
-    scores = mul(queries, keys, NT) * scale
-    rows = start + lax.broadcasted_iota(jnp.int32, scores.shape, 0)
-    columns = lax.broadcasted_iota(jnp.int32, scores.shape, 1)
-    allowed = (seg_rows == seg_columns) & (columns <= rows)
-    scores = jnp.where(allowed, scores, NEG)
-    raised = jnp.exp(scores - jnp.max(scores, axis=-1, keepdims=True))
-    return raised * (1.0 / jnp.sum(raised, axis=-1, keepdims=True))
+def fill_bias(bias, row_ref, col_ref):
+    @pl.when(pl.program_id(0) == 0)
+    def _():
+        rows = lax.broadcasted_iota(jnp.int32, bias.shape, 0)
+        columns = lax.broadcasted_iota(jnp.int32, bias.shape, 1)
+        allowed = (row_ref[...] == col_ref[...]) & (columns <= rows)
+        bias[...] = jnp.where(allowed, 0.0, NEG)
+
+
+def score_block(queries, keys, bias):
+    return mul(queries, keys, NT) * (HEAD_DIM**-0.5 * LOG2_E) + bias
 
 
 ANYWHERE = pl.BlockSpec(memory_space=pl.ANY)
@@ -462,41 +466,45 @@
 
 def attention_kernel(
     q_ref, k_ref, v_ref, qi_ref, ki_ref, qg_ref, kg_ref, cos_ref, sin_ref, row_ref, col_ref,
-    qh_ref, kh_ref, ctx_ref,
+    qh_ref, kh_ref, ctx_ref, lse_ref, bias,
 ):
     rows, size = q_ref.shape
     tile = min(QUERY_TILE, rows)
+    fill_bias(bias, row_ref, col_ref)
     for raw, inverse, gain, low in ((q_ref, qi_ref, qg_ref, qh_ref), (k_ref, ki_ref, kg_ref, kh_ref)):
         normed = raw[...] * inverse[...] * gain[...]
         turned = normed * cos_ref[...] + pltpu.roll(normed, size // 2, 1) * sin_ref[...]
         low[...] = turned.astype(BF)
     for start in range(0, rows, tile):
         end = start + tile
-        weights = softmax_block(
-            qh_ref[start:end], kh_ref[:end], row_ref[start:end], col_ref[:, :end], start, size**-0.5
-        )
-        ctx_ref[start:end] = mul(weights.astype(BF), v_ref[:end]).astype(BF)
+        scores = score_block(qh_ref[start:end], kh_ref[:end], bias[start:end, :end])
+        top = jnp.max(scores, axis=-1, keepdims=True)
+        raised = jnp.exp2(scores - top)
+        total = jnp.sum(raised, axis=-1, keepdims=True)
+        weights = (raised * (1.0 / total)).astype(BF)
+        ctx_ref[start:end] = mul(weights, v_ref[:end]).astype(BF)
+        lse_ref[0, start:end] = top + jnp.log2(total)
 
 
 def attention_back_kernel(
     q_ref, k_ref, v_ref, qi_ref, ki_ref, qg_ref, kg_ref, cos_ref, sin_ref, row_ref, col_ref,
-    qh_ref, kh_ref, dctx_ref, *rest,
+    qh_ref, kh_ref, ctx_ref, lse_ref, dctx_ref, *rest,
 ):
-    dq_ref, dk_ref, dv_ref, inner_ref, dqg_ref, dkg_ref, dq_total, dk_total, dv_total = rest[-9:]
+    dq_ref, dk_ref, dv_ref, inner_ref, dqg_ref, dkg_ref, dq_total, dk_total, dv_total, bias = rest[-10:]
     rows, size = q_ref.shape
     scale = size**-0.5
-    tile = min(QUERY_TILE, rows)
+    tile = min(BACK_TILE, rows)
+    fill_bias(bias, row_ref, col_ref)
     dk_total[...] = jnp.zeros_like(dk_total)
     dv_total[...] = jnp.zeros_like(dv_total)
+    inner = jnp.sum(dctx_ref[...].astype(F32) * ctx_ref[...].astype(F32), axis=1, keepdims=True)
     for start in range(0, rows, tile):
         end = start + tile
         keys = kh_ref[:end]
-        weights = softmax_block(
-            qh_ref[start:end], keys, row_ref[start:end], col_ref[:, :end], start, scale
-        )
+        scores = score_block(qh_ref[start:end], keys, bias[start:end, :end])
+        weights = jnp.exp2(scores - lse_ref[0, start:end])
         grad_weights = mul(dctx_ref[start:end], v_ref[:end], NT)
-        inner = jnp.sum(weights * grad_weights, axis=-1, keepdims=True)
-        grad_scores = (weights * (grad_weights - inner)).astype(BF)
+        grad_scores = (weights * (grad_weights - inner[start:end])).astype(BF)
         dq_total[start:end] = mul(grad_scores, keys) * scale
         dk_total[:end] += mul(grad_scores, qh_ref[start:end], TN) * scale
         dv_total[:end] += mul(weights.astype(BF), dctx_ref[start:end], TN)
@@ -521,18 +529,21 @@
     gain = pl.BlockSpec((1, HEAD_DIM), lambda h: (0, h))
     column = whole((rows, 1))
     table = whole((rows, HEAD_DIM))
-    return head, gain, [head, head, head, column, column, gain, gain, table, table, column, whole((1, rows))]
+    own_column = pl.BlockSpec((1, rows, 1), lambda h: (h, 0, 0))
+    specs = [head, head, head, column, column, gain, gain, table, table, column, whole((1, rows))]
+    return head, gain, own_column, specs
 
 
 def attention_call(operands, rows, local):
-    head, gain, specs = head_specs(rows)
+    head, gain, own_column, specs = head_specs(rows)
     heads = local // HEAD_DIM
     return pl.pallas_call(
         attention_kernel,
         grid=(heads,),
         in_specs=specs,
-        out_specs=[head] * 3,
-        out_shape=[jax.ShapeDtypeStruct((rows, local), BF)] * 3,
+        out_specs=[head] * 3 + [own_column],
+        out_shape=[jax.ShapeDtypeStruct((rows, local), BF)] * 3 + [jax.ShapeDtypeStruct((heads, rows, 1), F32)],
+        scratch_shapes=[pltpu.VMEM((rows, rows), F32)],
         compiler_params=kernel_params(),
         cost_estimate=pl.CostEstimate(
             flops=2 * rows * rows * local, bytes_accessed=12 * rows * local, transcendentals=rows * rows * heads // 2
@@ -542,17 +553,17 @@
 
 
 def attention_back_call(operands, rows, local, waits=()):
-    head, gain, specs = head_specs(rows)
+    head, gain, own_column, specs = head_specs(rows)
     heads = local // HEAD_DIM
     return pl.pallas_call(
         attention_back_kernel,
         grid=(heads,),
-        in_specs=specs + [head] * 3 + [ANYWHERE] * len(waits),
+        in_specs=specs + [head] * 3 + [own_column, head] + [ANYWHERE] * len(waits),
         out_specs=[head] * 3 + [pl.BlockSpec((1, rows, 2), lambda h: (h, 0, 0)), gain, gain],
         out_shape=[jax.ShapeDtypeStruct((rows, local), F32)] * 2
         + [jax.ShapeDtypeStruct((rows, local), BF), jax.ShapeDtypeStruct((heads, rows, 2), F32)]
         + [jax.ShapeDtypeStruct((1, local), F32)] * 2,
-        scratch_shapes=[pltpu.VMEM((rows, HEAD_DIM), F32)] * 3,
+        scratch_shapes=[pltpu.VMEM((rows, HEAD_DIM), F32)] * 3 + [pltpu.VMEM((rows, rows), F32)],
         compiler_params=kernel_params(),
         cost_estimate=pl.CostEstimate(
             flops=8 * rows * rows * local, bytes_accessed=24 * rows * local, transcendentals=rows * rows * heads // 2
@@ -562,213 +573,209 @@
 
 
 def hidden_kernel(pieces, core_ref, tokens_ref, gain_ref, *refs):
-    ctx_refs, w_ref = refs[:pieces], refs[pieces]
-    hidden_ref, low_ref, inverse_ref = refs[pieces + 1 :]
+    ctx_refs, w_refs = refs[:pieces], refs[pieces : pieces + 3]
+    hidden_ref, low_ref, inverse_ref, heads = refs[pieces + 3 :]
     local = ctx_refs[0].shape[1]
     half = local // 2
     near = pl.ds(pl.multiple_of(core_ref[0] * half, half), half)
     far = pl.ds(pl.multiple_of((1 - core_ref[0]) * half, half), half)
-    total = tokens_ref[...].astype(F32) + mul(ctx_refs[0][...], w_ref[:local])
+    heads[:, :local] = ctx_refs[0][...]
     for number in range(1, pieces):
         mine = local + (number - 1) * half
         other = mine + (pieces - 1) * half
-        total = total + mul(ctx_refs[number][:, near], w_ref[mine : mine + half])
-        total = total + mul(ctx_refs[number][:, far], w_ref[other : other + half])
+        heads[:, mine : mine + half] = ctx_refs[number][:, near]
+        heads[:, other : other + half] = ctx_refs[number][:, far]
+    total = tokens_ref[...].astype(F32)
+    begin = 0
+    for w_ref in w_refs:
+        end = begin + w_ref.shape[0]
+        total = total + mul(heads[:, begin:end], w_ref[...])
+        begin = end
     inverse = lax.rsqrt(jnp.mean(total * total, axis=1, keepdims=True) + EPS)
-    hidden_ref[...] = total
     low_ref[...] = (total * inverse * gain_ref[...]).astype(BF)
-    inverse_ref[...] = inverse
-
-
-def hidden_call(core, tokens, gain, context, weights):
+
+    @pl.when(pl.program_id(0) == core_ref[1])
+    def _():
+        hidden_ref[...] = total
+        inverse_ref[...] = inverse
+
+
+def hidden_call(places, tokens, gain, context, weights):
     rows, width = tokens.shape
-    tile = min(HIDDEN_TILE, rows)
+    tile = rows // len(context)
     row = lambda c: pl.BlockSpec((tile, c), lambda i: (i, 0))
     return pl.pallas_call(
         functools.partial(hidden_kernel, len(context)),
         grid=(rows // tile,),
         in_specs=[pl.BlockSpec(memory_space=pltpu.SMEM), row(width), whole((1, width))]
         + [row(context[0].shape[1])] * len(context)
-        + [whole(weights.shape)],
-        out_specs=[row(width), row(width), row(1)],
+        + [whole(array.shape) for array in weights],
+        out_specs=[whole((tile, width)), row(width), whole((tile, 1))],
         out_shape=[
-            jax.ShapeDtypeStruct((rows, width), F32),
+            jax.ShapeDtypeStruct((tile, width), F32),
             jax.ShapeDtypeStruct((rows, width), BF),
-            jax.ShapeDtypeStruct((rows, 1), F32),
+            jax.ShapeDtypeStruct((tile, 1), F32),
         ],
+        scratch_shapes=[pltpu.VMEM((tile, width), BF)],
         compiler_params=kernel_params(),
         cost_estimate=pl.CostEstimate(
             flops=2 * rows * width * width, bytes_accessed=10 * rows * width + 2 * width * width, transcendentals=0
         ),
         name="hidden_rows",
-    )(core, tokens, gain, *context, weights)
-
-
-def rows_kernel(arrays, first_number, each_device, added, waits, *refs):
-    parts = 2
+    )(places, tokens, gain, *context, *weights)
+
+
+def rows_kernel(place, number_here, each_device, added, waits, *refs):
     core_ref, router_ref = refs[:2]
-    x_refs, dy_refs, carried_refs = refs[2:4], refs[4:6], refs[6:8]
-    w_refs = refs[8 : 8 + arrays]
-    rest = refs[8 + arrays :]
+    x_refs, dy_refs, carried_refs, w_ref = refs[2:4], refs[4:6], refs[6:8], refs[8]
+    rest = refs[9:]
     if added:
         before, rest = rest[:4], rest[4:]
     rest = rest[waits:]
-    moe_refs, dx_refs = rest[:2], rest[2:4]
-    kept_ref, share_ref, held, moe, dx, gates, dots, sems, before_sems = rest[4:]
-    step = pl.program_id(0)
-    slot = lax.rem(step, 2)
+    moe_refs, dx_refs, kept_ref, share_ref = rest[:2], rest[2:4], rest[4], rest[5]
+    x, dy, down, both_w, kept, moe, dx, gates, dots, in_sems, w_sems, before_sems, out_sems = rest[6:]
     blocks, _, own, width = x_refs[0].shape
     rows = blocks * own
-    experts = held.shape[1]
-
-    def take(ref, first, count):
-        part = ref[first // own : (first + count) // own, 0]
-        return part.reshape(count, part.shape[-1])
-
-    hid = held.shape[2] // 3
-    tile = min(ROW_TILE, rows)
-    each = w_refs[0].shape[0] // experts
-    sets = each * arrays
-
-    def source(number):
-        return w_refs[number // each].at[pl.ds(number % each * experts, experts)]
-
-    def fetch(index, place):
-        for number in range(sets):
-
-            @pl.when(index == number)
-            def _():
-                pltpu.make_async_copy(source(number), held.at[place], sems.at[place]).start()
-
-    @pl.when(step == 0)
-    def _():
-        fetch(0, 0)
-        earlier = []
-        if added:
-            for number, place in enumerate((*moe_refs, *dx_refs)):
-                earlier.append(pltpu.make_async_copy(before[number], place, before_sems.at[number]))
-                earlier[-1].start()
-        for number in range(parts):
-            here = slice(number * rows, (number + 1) * rows)
-            logits = mul(take(x_refs[number], 0, rows), router_ref[...])
-            raised = jnp.exp(logits - jnp.max(logits, axis=1, keepdims=True))
-            shares = raised / jnp.sum(raised, axis=1, keepdims=True)
-            if number == 0:
-                share_ref[...] = shares
-            gates[here] = shares * take(carried_refs[number], 0, rows).astype(F32)
-        for copy in earlier:
-            copy.wait()
-        if added:
-            for number in range(parts):
-                here = slice(number * rows, (number + 1) * rows)
-                moe[here] = moe_refs[number][...].astype(F32)
-                dx[here] = dx_refs[number][:, :width].astype(F32)
-                dots[here] = dx_refs[number][:, width:].astype(F32)
-        else:
-            moe[...] = jnp.zeros_like(moe)
-            dx[...] = jnp.zeros_like(dx)
-            dots[...] = jnp.zeros_like(dots)
-
-    @pl.when(step + 1 < sets)
-    def _():
-        fetch(step + 1, 1 - slot)
-
-    pltpu.make_async_copy(source(0), held.at[slot], sems.at[slot]).wait()
-    for one in range(experts):
-        base = one * 3 * hid
-        chip = lax.rem(step, each) * experts + one
-        index = (chip * 2 + core_ref[0]) * each_device + first_number + step // each
-        for first in range(0, parts * rows, tile):
-            here = slice(first, first + tile)
-            both = mul(take(x_refs[first // rows], first % rows, tile), held[slot, one, hid:], NT)
-            back = mul(take(dy_refs[first // rows], first % rows, tile), held[slot, one, :hid], NT)
+    total = 2 * rows
+    experts = w_ref.shape[0]
+    hid = w_ref.shape[1] // 3
+
+    def fetch_rows(refs, held, first):
+        copies = []
+        for side in range(2):
+            for block in range(blocks):
+                to = held.at[pl.ds(side * rows + block * own, own)]
+                copies.append(pltpu.make_async_copy(refs[side].at[block, place], to, in_sems.at[first + side * blocks + block]))
+        return copies
+
+    x_copies = fetch_rows(x_refs, x, 0)
+    dy_copies = fetch_rows(dy_refs, dy, 2 * blocks)
+    w_copies = [
+        (
+            pltpu.make_async_copy(w_ref.at[e, pl.ds(hid, 2 * hid)], both_w.at[pl.ds(2 * e * hid, 2 * hid)], w_sems.at[2 * e]),
+            pltpu.make_async_copy(w_ref.at[e, pl.ds(0, hid)], down.at[pl.ds(e * hid, hid)], w_sems.at[2 * e + 1]),
+        )
+        for e in range(experts)
+    ]
+    for copy in x_copies + [w_copies[0][0]] + dy_copies + [w_copies[0][1]]:
+        copy.start()
+    for pair in w_copies[1:]:
+        for copy in pair:
+            copy.start()
+    earlier = []
+    if added:
+        for side in range(2):
+            here = pl.ds(side * rows, rows)
+            earlier.append(pltpu.make_async_copy(before[side], moe.at[here], before_sems.at[side]))
+            earlier.append(pltpu.make_async_copy(before[2 + side], dx.at[here], before_sems.at[2 + side]))
+    for copy in earlier:
+        copy.start()
+    for copy in x_copies:
+        copy.wait()
+    for side in range(2):
+        here = slice(side * rows, (side + 1) * rows)
+        logits = mul(x[here], router_ref[...])
+        raised = jnp.exp(logits - jnp.max(logits, axis=1, keepdims=True))
+        shares = raised / jnp.sum(raised, axis=1, keepdims=True)
+        if side == 0:
+            share_ref[...] = shares
+        gates[here] = shares * carried_refs[side][:, 0].reshape(rows, -1).astype(F32)
+    dots[...] = jnp.zeros_like(dots)
+    w_copies[0][0].wait()
+    for copy in dy_copies:
+        copy.wait()
+    out_copies = []
+    for e in range(experts):
+        if e:
+            w_copies[e][0].wait()
+        w_copies[e][1].wait()
+        index = (e * 2 + core_ref[0]) * each_device + number_here
+        gh = slice(e * hid, (e + 1) * hid)
+        wide = experts * hid + 2 * e * hid
+        for first in range(0, total, ROW_TILE):
+            here = slice(first, first + ROW_TILE)
+            both = mul(x[here], both_w[2 * e * hid : 2 * (e + 1) * hid], NT)
+            back = mul(dy[here], down[gh], NT)
             pre, up = both[:, :hid], both[:, hid:]
             sigma = 0.5 * jnp.tanh(0.5 * pre) + 0.5
             active = pre * sigma
-            chosen = lax.broadcasted_iota(jnp.int32, (tile, gates.shape[1]), 1) == index
+            chosen = lax.broadcasted_iota(jnp.int32, (ROW_TILE, gates.shape[1]), 1) == index
             gate = jnp.sum(jnp.where(chosen, gates[here], 0.0), axis=1, keepdims=True)
-            column = lax.broadcasted_iota(jnp.int32, (tile, LANES), 1) == index
+            column = lax.broadcasted_iota(jnp.int32, (ROW_TILE, LANES), 1) == index
             hidden = active * up
-            dot = jnp.sum(hidden * back, axis=1, keepdims=True)
-            dots[here] += jnp.where(column, dot, 0.0)
+            dots[here] += jnp.where(column, jnp.sum(hidden * back, axis=1, keepdims=True), 0.0)
             back = back * gate
-            kept_ref[here, base : base + hid] = (hidden * gate).astype(BF)
-            kept_ref[here, base + hid : base + 2 * hid] = (
-                back * up * sigma * (1.0 + pre * (1.0 - sigma))
-            ).astype(BF)
-            kept_ref[here, base + 2 * hid : base + 3 * hid] = (back * active).astype(BF)
-    for first in range(0, width, COLUMN_TILE):
+            kept[here, gh] = (hidden * gate).astype(BF)
+            kept[here, wide : wide + hid] = (back * up * sigma * (1.0 + pre * (1.0 - sigma))).astype(BF)
+            kept[here, wide + hid : wide + 2 * hid] = (back * active).astype(BF)
+    copy = pltpu.make_async_copy(kept, kept_ref, out_sems.at[0])
+    copy.start()
+    out_copies.append(copy)
+    for copy in earlier:
+        copy.wait()
+    for number, first in enumerate(range(0, width, COLUMN_TILE)):
         here = slice(first, first + COLUMN_TILE)
-        total = moe[:, here]
-        for one in range(experts):
-            base = one * 3 * hid
-            total = total + mul(kept_ref[:, base : base + hid], held[slot, one, :hid, here])
-        moe[:, here] = total
-        total = dx[:, here]
-        for one in range(experts):
-            base = one * 3 * hid
-            total = total + mul(kept_ref[:, base + hid : base + 3 * hid], held[slot, one, hid:, here])
-        dx[:, here] = total
-
-    @pl.when(step == sets - 1)
-    def _():
-        for number in range(parts):
-            here = slice(number * rows, (number + 1) * rows)
-            moe_refs[number][...] = moe[here].astype(BF)
-            dx_refs[number][:, :width] = dx[here].astype(BF)
-            dx_refs[number][:, width:] = dots[here].astype(BF)
-
-
-def rows_call(core, router, moe_in, cotangent, carried, place, weights, first_number, each_device, before=None, waits=()):
+        for what, (held, w_held, begin, end) in enumerate((
+            (moe, down, 0, experts * hid), (dx, both_w, experts * hid, 3 * experts * hid)
+        )):
+            value = mul(kept[:, begin:end], w_held[:, here])
+            if added:
+                value = value + held[:, here].astype(F32)
+            held[:, here] = value.astype(BF)
+            for side in range(2):
+                ref = (moe_refs, dx_refs)[what][side]
+                copy = pltpu.make_async_copy(
+                    held.at[pl.ds(side * rows, rows), pl.ds(first, COLUMN_TILE)],
+                    ref.at[:, pl.ds(first, COLUMN_TILE)], out_sems.at[1 + 4 * number + 2 * what + side])
+                copy.start()
+                out_copies.append(copy)
+    value = dots[...]
+    if added:
+        value = value + dx[:, width:].astype(F32)
+    dx[:, width:] = value.astype(BF)
+    last = 1 + 4 * (width // COLUMN_TILE)
+    for side in range(2):
+        copy = pltpu.make_async_copy(
+            dx.at[pl.ds(side * rows, rows), pl.ds(width, LANES)], dx_refs[side].at[:, pl.ds(width, LANES)],
+            out_sems.at[last + side])
+        copy.start()
+        out_copies.append(copy)
+    for copy in out_copies:
+        copy.wait()
+
+def rows_call(core, router, moe_in, cotangent, carried, place, weights, number_here, each_device, before=None, waits=()):
     blocks, _, own, width = moe_in[0].shape
     rows = blocks * own
-    parts = 2
-    chips, depth, _ = weights[0].shape
-    experts = EXPERT_STEP
-    sets = len(weights) * chips // experts
+    experts, depth, _ = weights.shape
     number = router.shape[1]
-    full = whole((rows, width))
-    wide = experts * depth
-    wider = whole((rows, width + LANES))
-    operands = [core, router, *moe_in, *cotangent, *carried, *weights]
-
-    def half(columns):
-        return pl.BlockSpec((blocks, 1, own, columns), lambda i: (0, place, 0, 0), pipeline_mode=pl.Buffered(1))
-
-    specs = [pl.BlockSpec(memory_space=pltpu.SMEM), whole(router.shape)] + [half(width)] * 4 + [half(number)] * 2
-    specs += [pl.BlockSpec(memory_space=pl.ANY)] * len(weights)
+    total = 2 * rows
+    small = pl.BlockSpec((blocks, 1, own, number), lambda i: (0, place, 0, 0), pipeline_mode=pl.Buffered(1))
+    operands = [core, router, *moe_in, *cotangent, *carried, weights]
+    specs = [pl.BlockSpec(memory_space=pltpu.SMEM), whole(router.shape)] + [ANYWHERE] * 4 + [small] * 2 + [ANYWHERE]
     if before is not None:
         operands += before
         specs += [ANYWHERE] * 4
     operands += waits
     specs += [ANYWHERE] * len(waits)
     return pl.pallas_call(
-        functools.partial(rows_kernel, len(weights), first_number, each_device, before is not None, len(waits)),
-        grid=(sets,),
+        functools.partial(rows_kernel, place, number_here, each_device, before is not None, len(waits)),
+        grid=(1,),
         in_specs=specs,
-        out_specs=[full] * 2
-        + [wider] * 2
-        + [pl.BlockSpec((parts * rows, wide), lambda i: (0, i)), whole((rows, number))],
+        out_specs=[ANYWHERE] * 5 + [whole((rows, number))],
         out_shape=[jax.ShapeDtypeStruct((rows, width), BF)] * 2
         + [jax.ShapeDtypeStruct((rows, width + LANES), BF)] * 2
-        + [
-            jax.ShapeDtypeStruct((parts * rows, sets * wide), BF),
-            jax.ShapeDtypeStruct((rows, number), F32),
-        ],
+        + [jax.ShapeDtypeStruct((total, experts * depth), BF), jax.ShapeDtypeStruct((rows, number), F32)],
         scratch_shapes=[
-            pltpu.VMEM((2, experts, depth, width), BF),
-            pltpu.VMEM((parts * rows, width), F32),
-            pltpu.VMEM((parts * rows, width), F32),
-            pltpu.VMEM((parts * rows, number), F32),
-            pltpu.VMEM((parts * rows, LANES), F32),
-            pltpu.SemaphoreType.DMA((2,)),
-            pltpu.SemaphoreType.DMA((4,)),
+            pltpu.VMEM((total, width), BF), pltpu.VMEM((total, width), BF),
+            pltpu.VMEM((experts * depth // 3, width), BF), pltpu.VMEM((2 * experts * depth // 3, width), BF),
+            pltpu.VMEM((total, experts * depth), BF), pltpu.VMEM((total, width), BF), pltpu.VMEM((total, width + LANES), BF),
+            pltpu.VMEM((total, number), F32), pltpu.VMEM((total, LANES), F32),
+            pltpu.SemaphoreType.DMA((4 * blocks,)), pltpu.SemaphoreType.DMA((2 * experts,)), pltpu.SemaphoreType.DMA((4,)),
+            pltpu.SemaphoreType.DMA((3 + 4 * (width // COLUMN_TILE),)),
         ],
         compiler_params=kernel_params(),
         cost_estimate=pl.CostEstimate(
-            flops=4 * parts * rows * width * wide * sets,
-            bytes_accessed=8 * parts * rows * width + 2 * sets * wide * (parts * rows + width),
-            transcendentals=parts * rows * wide * sets // 3,
+            flops=4 * total * width * experts * depth, bytes_accessed=8 * total * width, transcendentals=0
         ),
         name="expert_rows",
     )(*operands)
@@ -777,9 +784,9 @@
 def weight_grads_kernel(sides, halves, outs, added, skipped, order_ref, *refs):
     parts = sides * halves
     x_refs, dy_refs = refs[:parts], refs[parts : 2 * parts]
-    kept_refs = refs[2 * parts : 2 * parts + 2 * halves]
-    add_refs = refs[2 * parts + 2 * halves : 2 * parts + 2 * halves + added]
-    out_refs, turned = refs[2 * parts + 2 * halves + added + skipped : -1], refs[-1]
+    kept_refs = refs[2 * parts : 2 * parts + 4 * halves]
+    add_refs = refs[2 * parts + 4 * halves : 2 * parts + 4 * halves + added]
+    out_refs, turned = refs[2 * parts + 4 * halves + added + skipped : -1], refs[-1]
     hid = turned.shape[0] // 6
     span = kept_refs[0].shape[0]
     rows = span // sides
@@ -789,10 +796,10 @@
         for h in range(halves):
             there = slice(h * span, (h + 1) * span)
             for one in range(2):
-                kept_ref = kept_refs[2 * h + one]
-                turned[one * hid : (one + 1) * hid, there] = kept_ref[:, :hid].T
+                units, grads = kept_refs[4 * h + 2 * one : 4 * h + 2 * one + 2]
+                turned[one * hid : (one + 1) * hid, there] = units[...].T
                 place = 2 * hid + one * 2 * hid
-                turned[place : place + 2 * hid, there] = kept_ref[:, hid:].T
+                turned[place : place + 2 * hid, there] = grads[...].T
 
     def total(first, last, refs):
         return sum(
@@ -826,12 +833,18 @@
     def column(h):
         return pl.BlockSpec((blocks, 1, own, tile), lambda i, order: (0, h, 0, i))
 
+    hid = depth // 3
+    experts = kept[0].shape[1] // depth
+
     def expert(one):
-        return pl.BlockSpec((span, depth), lambda i, order: (0, order[one]), pipeline_mode=pl.Buffered(1))
+        return [
+            pl.BlockSpec((span, hid), lambda i, order: (0, order[one]), pipeline_mode=pl.Buffered(1)),
+            pl.BlockSpec((span, 2 * hid), lambda i, order: (0, experts // 2 + order[one]), pipeline_mode=pl.Buffered(1)),
+        ]
 
     operands = [moe_in[side] for _, side in parts] + [cotangent[side] for _, side in parts]
-    operands += [kept[h] for h in range(halves) for _ in range(2)]
-    specs = [column(h) for h, _ in parts] * 2 + [expert(one) for _ in range(halves) for one in range(2)]
+    operands += [kept[h] for h in range(halves) for _ in range(4)]
+    specs = [column(h) for h, _ in parts] * 2 + [spec for _ in range(halves) for one in range(2) for spec in expert(one)]
     operands += addends
     specs += [pl.BlockSpec((addend.shape[0], tile), lambda i, order: (0, i)) for addend in addends]
     aliases = {}
@@ -965,19 +978,23 @@
         query_raw, key_raw, values, query_inverse, key_inverse, query_gain[None], key_gain[None],
         cos_table, sin_table, segment[:, None], segment[None],
     ]
-    queries, keys, context = attention_call(operands, rows, local)
+    queries, keys, context, lse = attention_call(operands, rows, local)
+    context_here = context
     far_context = swap_tensor(context, 2)
     near_context = swap_tensor(context, 1)
-    packed[1], w_mine[2], context = join(packed[1], w_mine[2], context)
-    weights.append(spread(packed[1]))
+    w_mine[2], context = join(w_mine[2], context)
     near_context, far_context, *w_mine = join(near_context, far_context, *w_mine)
     contexts = [context, near_context, far_context, swap_tensor(far_context, 1)]
     w_mine = jnp.concatenate(w_mine, axis=0)
-    w_all = jnp.concatenate([w_output, w_mine, swap(w_mine, 1)], axis=0)
+    w_other, packed[1], contexts[3] = join(swap(w_mine, 1), packed[1], contexts[3])
+    w_all = [w_output, w_mine, w_other]
+    weights.append(spread(packed[1]))
     carried_later, cotangent_later, contexts[0] = lax.optimization_barrier((carried, cotangent, contexts[0]))
     carried_sides = [view(carried), view(swap(carried_later, 1))]
     cotangent_sides = [view(cotangent), view(swap(cotangent_later, 1))]
-    hidden, moe_low, inverse_moe = hidden_call(core[None], tokens, moe_gain[None], contexts, w_all)
+    hidden_own, moe_low, inverse_own = hidden_call(
+        jnp.stack([core, layer]).astype(jnp.int32), tokens, moe_gain[None], contexts, w_all
+    )
     sides = [view(moe_low), view(swap(moe_low, 1))]
     router_wide = router.astype(F32)
     calls, kept, shares = [None, None], [{}, {}], [None, None]
@@ -985,7 +1002,7 @@
     def run(h, j, *waits):
         before = None if calls[h] is None else calls[h][:4]
         calls[h] = rows_call(
-            core[None], router, sides, cotangent_sides, carried_sides, h, [weights[j]], j, experts_here, before, waits
+            core[None], router, sides, cotangent_sides, carried_sides, h, weights[j], j, experts_here, before, waits
         )
         kept[h][j] = calls[h][4]
         shares[h] = calls[h][5]
@@ -1028,7 +1045,6 @@
     share = jnp.concatenate(
         [lax.dynamic_slice_in_dim(item, layer * (own_rows // HALVES), own_rows // HALVES, 0) for item in shares], axis=0
     )
-    hidden_own, inverse_own = own(hidden), own(inverse_moe)
     moe_in = hidden_own * inverse_own * moe_gain
     dlogits = share * (dshares - jnp.sum(share * dshares, axis=-1, keepdims=True))
     router_back = jnp.einsum("te,de->td", dlogits, router_wide, precision=lax.Precision.HIGHEST)
@@ -1038,17 +1054,15 @@
     grad_hidden = own(cotangent).astype(F32) + grad_norm_moe
     grad_low = grad_hidden.astype(BF)
 
-    by_head = mul(grad_low, w_all, NT).astype(BF)
+    by_head, by_mine, by_other = (mul(grad_low, weight, NT).astype(BF) for weight in w_all)
     core_columns = local // 2
     grad_context = jnp.zeros((rows, local), BF)
     for bits in range(n_tensor):
         if bits == 0:
-            came = by_head[:, :local]
+            came = by_head
         else:
-            begin = local + (bits - 1) * core_columns
-            mine = by_head[:, begin : begin + core_columns]
-            begin += (n_tensor - 1) * core_columns
-            other = by_head[:, begin : begin + core_columns]
+            columns = slice((bits - 1) * core_columns, bits * core_columns)
+            mine, other = by_mine[:, columns], by_other[:, columns]
             lower = jnp.where(core == 0, mine, other)
             upper = jnp.where(core == 0, other, mine)
             came = swap_tensor(jnp.concatenate([lower, upper], axis=1), bits)
@@ -1057,13 +1071,14 @@
     output_grads = mul(relative_columns(grad_low), heads_own, TN).astype(BF)
     output_grads = [output_grads[: width // 2], output_grads[width // 2 :]]
     attn_relative = relative_columns(attn_in)
-    grad_context, moe_terms, attn_relative, *output_grads = join(
-        grad_context, moe_terms, attn_relative, *output_grads
+    router_part = jnp.einsum("td,te->de", moe_in, dlogits, precision=lax.Precision.HIGHEST)
+    grad_context, moe_terms, attn_relative, router_part, *output_grads = join(
+        grad_context, moe_terms, attn_relative, router_part, *output_grads
     )
     moe = scatter_tensor(moe_terms)
     came = swap(output_grads[1], 1)
     back = attention_back_call(
-        operands + [queries, keys, grad_context], rows, local, [output_grads[1]]
+        operands + [queries, keys, context_here, lse, grad_context], rows, local, [output_grads[1]]
     )
     *back, came, near_low[0], near_low[1] = join(*back, came, *near_low)
     near_high = send(near[1::2], (4, 2))
@@ -1096,7 +1111,8 @@
         for mine, near in ((mine_low, near_low), (mine_high, near_high))], axis=0)
     outputs_zero = list(expert_outputs(outputs_zero))
     output_near = send(beside(output_grads, output_via), (4, 2))
-    *came, terms_in, lows = join(*came, terms_in, lows)
+    grad_attn_gain = jnp.sum(terms_in.astype(F32) * tokens.astype(F32) * inverse_in, axis=0)
+    *came, terms_in, lows, grad_attn_gain = join(*came, terms_in, lows, grad_attn_gain)
     out_above, out_below = [from_above(came)], [from_below(came)]
     chunk = lambda place: lax.dynamic_slice_in_dim(terms_in, jnp.clip(place, 0, n_tensor - 1) * own_rows, own_rows, 0)
     sum_above = sum_below = jnp.zeros((), BF)
@@ -1108,8 +1124,6 @@
             jnp.where(layer < step, plus(chunk(layer + n_tensor - step), sum_below), out_below[-1]),
         )
         if step == 1:
-            grad_attn_gain = jnp.sum(terms_in.astype(F32) * tokens.astype(F32) * inverse_in, axis=0)
-            router_part = jnp.einsum("td,te->de", moe_in, dlogits, precision=lax.Precision.HIGHEST)
             own_width, span = width // groups, local // groups
             spread_gain = lambda gain: jnp.pad(
                 gain.reshape(groups, span), ((0, 0), (0, own_width - span))

time: 861 us -> 852 us (0.990)
  Pallas kernels: 340 us -> 311 us
  waiting for transfers between devices: 235 us -> 258 us
  other arithmetic: 91.8 us -> 81.2 us
    pallas_call x4, Pallas kernels: 175 us -> 158 us  [rows_call(): pl.pallas_call(functools.partial(rows_kernel, place, number_here, each_de...]
    ppermute x24, waiting for transfers between devices: 64.8 us -> 78.4 us  [swap(): return lax.ppermute(values, EXPERT, [(i, i ^ bit) for i in range(size)])]
    pallas_call x1, Pallas kernels: 30.9 us -> 18.6 us  [attention_back_call(): pl.pallas_call(attention_back_kernel, grid=(heads,), in_specs=specs + [he...]
    ppermute x12, waiting for transfers between devices: 82.2 us -> 90.9 us  [swap_tensor(): return lax.ppermute(values, TENSOR, [(i, i ^ bit) for i in range(size)])]
    dot_general x4 -> x6, matrix products: 24.3 us -> 25 us  [mul(): return lax.dot_general(left, right, dims, preferred_element_type=F32)]
  transfers between devices with their start and end apart: 62 -> 62, of which waited for: 35 -> 33; matrix products, arithmetic and copies ran while one was open for 15% -> 14% of each run, Pallas kernels for 40% -> 37%
where the time goes in v3:
time: 852 us; the launch traced here: 837 us
  Pallas kernels  311 us (37%)
  waiting for transfers between devices  258 us (30%)
  other arithmetic  81.2 us (10%)
  local copies, waits for them, and re-layouts  74.4 us (9%)
  starting transfers between devices  66.7 us (8%)
  matrix products  29.7 us (3%)
  between operations  16.1 us (2%)
    pallas_call x4, Pallas kernels, rows_call(): pl.pallas_call(functools.partial(rows_kernel, place, number_here, each_de...  158 us
    ppermute x12, waiting for transfers between devices, swap_tensor(): return lax.ppermute(values, TENSOR, [(i, i ^ bit) for i in range(size)])  90.9 us
    pallas_call x4, Pallas kernels, weight_grads_call(): pl.pallas_call(functools.partial(weight_grads_kernel, sides, halves, outs...  88.3 us
    ppermute x24, waiting for transfers between devices, swap(): return lax.ppermute(values, EXPERT, [(i, i ^ bit) for i in range(size)])  78.4 us
    ppermute x7, waiting for transfers between devices, exchange(): lax.ppermute(jnp.where(even, to_above, to_below), TENSOR, [(0, 1), (1, 0)...  41 us
    unnamed x211, local copies, waits for them, and re-layouts  35.7 us
    dot_general x6, matrix products, mul(): return lax.dot_general(left, right, dims, preferred_element_type=F32)  25 us
    ppermute x7, waiting for transfers between devices, exchange(): lax.ppermute(jnp.where(even, to_below, to_above), TENSOR, [(1, 2), (2, 1)...  24.7 us
  transfers between devices with their start and end apart: 62, of which 33 were waited for; matrix products, arithmetic and copies ran while one was open for 14% of the time, Pallas kernels for 37%

profile of v3, /device:TPU:20, one launch (start us, length us, event | category | flops | bytes accessed | tf_op | source)
XLA Modules:
  0.0 837.0 jit_solution(7861843380667672847)
XLA Ops:
  9.6 2.6 fusion.57
  14.5 2.8 slice_bitcast_fusion.4
  30.9 13.3 %front_rows.1 = (bf16[1024,2048]{1,0:T(8,128)(2,1)}, f32[1024,1]{1,0:T(8,128)}, f32[1024,512]{1,0:T(8,128)}, f32[1024,512]{1,0:T(8,128)}, bf16[1024,512]{1,0:T(8,128)(2,1)}, /*index=5*/f32[1024,2]{1,0:T(8,128)}) custom-call(bf16[1024,2048]{1,0:T(8,128)(2,1)} %tokens_ref.3, f32[1,2048]{1,0:T(1,128)} %bitcast.170, bf16[2048,512]{1,0:T(8,128)(2,1)} %wq_ref.1, ...), custom_call_target="tpu_custom_call" | custom-call | flops 6442450944 | bytes 14680064 | tf_op jit(solution)/shard_map/front_rows/pallas_call | solution.py:451
  45.9 2.4 collective-permute-start.1
  52.4 18.5 %collective-permute-done = f32[16,128]{1,0:T(8,128)S(1)} collective-permute-done((f32[16,128]{1,0:T(8,128)S(1)}, f32[16,128]{1,0:T(8,128)S(1)}, u32[]{:S(2)}, u32[]{:S(2)}) %collective-permute-start) | collective-permute-done | bytes 8224 | tf_op jit(solution)/shard_map/ppermute | solution.py:1288
  74.6 15.4 %attention_rows.1 = (bf16[1024,512]{1,0:T(8,128)(2,1)}, bf16[1024,512]{1,0:T(8,128)(2,1)}, bf16[1024,512]{1,0:T(8,128)(2,1)}, f32[4,1024,1]{2,1,0:T(8,128)}) custom-call(f32[1024,512]{1,0:T(8,128)} %get-tuple-element.151.q_ref, f32[1024,512]{1,0:T(8,128)} %get-tuple-element.152.k_ref, bf16[1024,512]{1,0:T(8,128)(2,1)} %get-tuple-element.153.v_ref, ...), custom_call_target="tpu_custom_call" | custom-call | flops 1073741824 | bytes 6291456 | tf_op jit(solution)/shard_map/attention_rows/pallas_call | solution.py:540
  92.0 29.0 %collective-permute-done.5 = bf16[256,2048]{1,0:T(8,128)(2,1)S(1)} collective-permute-done((bf16[256,2048]{1,0:T(8,128)(2,1)}, bf16[256,2048]{1,0:T(8,128)(2,1)S(1)}, u32[]{:S(2)}, u32[]{:S(2)}) %collective-permute-start.5) | collective-permute-done | bytes 1048608 | tf_op jit(solution)/shard_map/ppermute | solution.py:1192
  121.0 20.3 %collective-permute-done.6.refs_1_ = bf16[1024,512]{1,0:T(8,128)(2,1)S(1)} collective-permute-done((bf16[1024,512]{1,0:T(8,128)(2,1)}, bf16[1024,512]{1,0:T(8,128)(2,1)S(1)}, u32[]{:S(2)}, u32[]{:S(2)}) %collective-permute-start.6) | collective-permute-done | bytes 1048608 | tf_op jit(solution)/shard_map/ppermute | solution.py:1192
  149.4 24.1 %collective-permute-done.9.refs_3_ = bf16[1024,512]{1,0:T(8,128)(2,1)S(1)} collective-permute-done((bf16[1024,512]{1,0:T(8,128)(2,1)S(1)}, bf16[1024,512]{1,0:T(8,128)(2,1)S(1)}, u32[]{:S(2)}, u32[]{:S(2)}) %collective-permute-start.9) | collective-permute-done | bytes 1048608 | tf_op jit(solution)/shard_map/ppermute | solution.py:1192
  174.6 17.0 %hidden_rows.1 = (f32[256,2048]{1,0:T(8,128)}, bf16[1024,2048]{1,0:T(8,128)(2,1)}, f32[256,1]{1,0:T(8,128)}) custom-call(s32[2]{0:T(128)} %pad_add_fusion.core_ref, bf16[1024,2048]{1,0:T(8,128)(2,1)} %tokens_ref.3, f32[1,2048]{1,0:T(1,128)} %bitcast.161, bf16[1024,512]{1,0:T(8,128)(2,1)} %get-tuple-element.157.refs_0_.ctx_ref, bf16[1024,512]{1,0:T(8,128)(2,1)} %copy-done.74, ...), custom_call_target="tpu_custom_call" | custom-call | flops 8589934592 | bytes 29360128 | tf_op jit(solution)/shard_map/hidden_rows/pallas_call | solution.py:607
  194.7 2.7 collective-permute-done.12
  199.4 38.0 %expert_rows.4 = (bf16[512,2048]{1,0:T(8,128)(2,1)}, bf16[512,2048]{1,0:T(8,128)(2,1)}, bf16[512,2176]{1,0:T(8,128)(2,1)}, bf16[512,2176]{1,0:T(8,128)(2,1)}, bf...) custom-call(s32[1]{0:T(128)} %bitcast.refs_0_, bf16[2048,16]{1,0:T(8,128)(2,1)} %copy.180.refs_1_, ...), custom_call_target="tpu_custom_call" | custom-call | flops 25769803776 | bytes 16777216 | tf_op jit(solution)/shard_map/expert_rows/pallas_call | solution.py:760
  237.4 38.4 %expert_rows.5 = (bf16[512,2048]{1,0:T(8,128)(2,1)}, bf16[512,2048]{1,0:T(8,128)(2,1)}, bf16[512,2176]{1,0:T(8,128)(2,1)}, bf16[512,2176]{1,0:T(8,128)(2,1)}, bf...) custom-call(s32[1]{0:T(128)} %bitcast.refs_0_, bf16[2048,16]{1,0:T(8,128)(2,1)} %copy.180.refs_1_, ...), custom_call_target="tpu_custom_call" | custom-call | flops 25769803776 | bytes 16777216 | tf_op jit(solution)/shard_map/expert_rows/pallas_call | solution.py:760
  275.8 21.9 %expert_weight_grads.4 = (bf16[384,2048]{1,0:T(8,128)(2,1)}, bf16[384,2048]{1,0:T(8,128)(2,1)}, bf16[384,2048]{1,0:T(8,128)(2,1)}, bf16[384,2048]{1,0:T(8,128)(2,1)}) custom-call(s32[2]{0:T(128)} %pad_add_fusion.1.order_ref, bf16[4,2,128,2048]{3,2,1,0:T(8,128)(2,1)} %bitcast.128, bf16[4,2,128,2048]{3,2,1,0:T(8,128)(2,1)} %bitcast.26.refs_3_.refs_1_, ...), custom_call_target="tpu_custom_call" | custom-call | flops 12884901888 | bytes 29360128 | tf_op jit(solution)/shard_map/expert_weight_grads/pallas_call | solution.py:862
  299.8 40.7 %expert_rows.6 = (bf16[512,2048]{1,0:T(8,128)(2,1)}, bf16[512,2048]{1,0:T(8,128)(2,1)}, bf16[512,2176]{1,0:T(8,128)(2,1)}, bf16[512,2176]{1,0:T(8,128)(2,1)}, bf...) custom-call(s32[1]{0:T(128)} %bitcast.refs_0_, bf16[2048,16]{1,0:T(8,128)(2,1)} %copy.180.refs_1_, ...), custom_call_target="tpu_custom_call" | custom-call | flops 25769803776 | bytes 16777216 | tf_op jit(solution)/shard_map/expert_rows/pallas_call | solution.py:760
  340.6 4.5 collective-permute-done.15
  345.2 3.6 add_convert_fusion.3.refs_13_
  349.0 40.6 %expert_rows.7 = (bf16[512,2048]{1,0:T(8,128)(2,1)}, bf16[512,2048]{1,0:T(8,128)(2,1)}, bf16[512,2176]{1,0:T(8,128)(2,1)}, bf16[512,2176]{1,0:T(8,128)(2,1)}, bf...) custom-call(s32[1]{0:T(128)} %bitcast.refs_0_, bf16[2048,16]{1,0:T(8,128)(2,1)} %copy.180.refs_1_, ...), custom_call_target="tpu_custom_call" | custom-call | flops 25769803776 | bytes 16777216 | tf_op jit(solution)/shard_map/expert_rows/pallas_call | solution.py:760
  389.6 4.7 reduce-scatter.5.cloned.1.call-done
  394.3 4.6 collective-permute-done.16
  398.9 3.5 add_convert_fusion.2.refs_18_
  409.2 22.0 %expert_weight_grads.5 = (bf16[384,2048]{1,0:T(8,128)(2,1)}, bf16[384,2048]{1,0:T(8,128)(2,1)}, bf16[384,2048]{1,0:T(8,128)(2,1)}, bf16[384,2048]{1,0:T(8,128)(2,1)}) custom-call(s32[2]{0:T(128)} %pad_add_fusion.2.order_ref, bf16[4,2,128,2048]{3,2,1,0:T(8,128)(2,1)} %bitcast.132, bf16[4,2,128,2048]{3,2,1,0:T(8,128)(2,1)} %bitcast.26.refs_3_.refs_1_, ...), custom_call_target="tpu_custom_call" | custom-call | flops 12884901888 | bytes 29360128 | tf_op jit(solution)/shard_map/expert_weight_grads/pallas_call | solution.py:862
  431.7 22.2 %expert_weight_grads.6.refs_16_ = bf16[4,768,2048]{2,1,0:T(8,128)(2,1)} custom-call(s32[2]{0:T(128)} %iota.29.order_ref, bf16[4,2,128,2048]{3,2,1,0:T(8,128)(2,1)} %bitcast.134, bf16[4,2,128,2048]{3,2,1,0:T(8,128)(2,1)} %bitcast.26.refs_3_.refs_1_, bf16[4,2,128,2048]{3,2,1,0:T(8,128)(2,1)} %bitcast.135, bf16[4,2,128,2048]{3,2,1,0:T(8,128)(2,1)} %bitcast.26.refs_3_.refs_1_, ...), custom_call_target="tpu_custom_call" | custom-call | flops 12884901888 | bytes 29360128 | tf_op jit(solution)/shard_map/expert_weight_grads/pallas_call | solution.py:862
  455.2 3.3 multiply_reduce_fusion.1
  459.9 3.5 fusion.52
  464.5 3.1 convolution_convert_fusion.2
  470.0 2.9 collective-permute-start.18
  476.8 2.4 convolution_convert_fusion.1
  479.2 4.0 fusion.53
  486.0 4.2 collective-permute-done.17
  490.2 2.8 collective-permute-done.18
  495.7 2.4 pad_maximum_fusion
  502.4 18.6 %attention_rows_back.1 = (f32[1024,512]{1,0:T(8,128)}, f32[1024,512]{1,0:T(8,128)}, bf16[1024,512]{1,0:T(8,128)(2,1)}, f32[4,1024,2]{2,1,0:T(8,128)}, f32[1,512]{1,0:T(1,128)}, /*index=5*/f32[1,512]{1,0:T(1,128)}) custom-call(f32[1024,512]{1,0:T(8,128)} %get-tuple-element.151.q_ref, f32[1024,512]{1,0:T(8,128)} %get-tuple-element.152.k_ref, ...), custom_call_target="tpu_custom_call" | custom-call | flops 4294967296 | bytes 12582912 | tf_op jit(solution)/shard_map/attention_rows_back/pallas_call | solution.py:558
  521.0 14.7 %collective-permute-done.23 = bf16[384,2048]{1,0:T(8,128)(2,1)S(1)} collective-permute-done((bf16[384,2048]{1,0:T(8,128)(2,1)}, bf16[384,2048]{1,0:T(8,128)(2,1)S(1)}, u32[]{:S(2)}, u32[]{:S(2)}) %collective-permute-start.23) | collective-permute-done | bytes 1572896 | tf_op jit(solution)/shard_map/ppermute | solution.py:885
  538.4 3.7 collective-permute-start.25
  542.1 2.6 collective-permute-start.27
  544.8 5.4 add_convert_fusion
  557.2 22.2 %expert_weight_grads.7 = bf16[4,768,2048]{2,1,0:T(8,128)(2,1)} custom-call(s32[2]{0:T(128)} %constant.101.clone.1.order_ref, bf16[4,2,128,2048]{3,2,1,0:T(8,128)(2,1)} %bitcast.136, bf16[4,2,128,2048]{3,2,1,0:T(8,128)(2,1)} %bitcast.26.refs_3_.refs_1_, bf16[4,2,128,2048]{3,2,1,0:T(8,128)(2,1)} %bitcast.137, ...), custom_call_target="tpu_custom_call", output_to_operand_aliasing={{}: (17, {})} | custom-call | flops 12884901888 | bytes 29360128 | tf_op jit(solution)/shard_map/expert_weight_grads/pallas_call | solution.py:862
  584.6 3.7 collective-permute-start.32
  595.7 10.2 %multiply_reduce_fusion = (bf16[2048]{0:T(1024)(128)(2,1)S(1)}, bf16[1024,2048]{1,0:T(8,128)(2,1)}) fusion(bf16[1024,2048]{1,0:T(8,128)(2,1)S(1)} %copy-done.42, f32[1024]{0:T(1024)S(1)} %reduce.2, bf16[2048,512]{1,0:T(8,128)(2,1)} %wv_ref.1, bf16[2048,512]{1,0:T(8,128)(2,1)} %wk_ref.1, bf16[2048,512]{1,0:T(8,128)(2,1)} %wq_ref.1, ...), kind=kOutput, calls=%fused_computation | convolution fusion | flops 6483343360 | bytes 17833984 | tf_op jit(solution)/shard_map/dot_general | solution.py:402
  607.7 3.3 collective-permute-done.32
  611.0 3.3 collective-permute-done.33
  614.7 2.8 broadcast_select_fusion.16
  617.7 2.5 collective-permute-start.35
  620.3 7.6 convolution_convert_fusion
  628.7 12.1 %collective-permute-done.34 = bf16[256,2048]{1,0:T(8,128)(2,1)S(1)} collective-permute-done((bf16[256,2048]{1,0:T(8,128)(2,1)S(1)}, bf16[256,2048]{1,0:T(8,128)(2,1)S(1)}, u32[]{:S(2)}, u32[]{:S(2)}) %collective-permute-start.34) | collective-permute-done | bytes 1048608 | tf_op jit(solution)/shard_map/ppermute | solution.py:1214
  645.3 2.8 add_convert_fusion.6
  649.7 2.5 collective-permute-start.37
  655.3 20.4 %collective-permute-done.36 = bf16[256,2048]{1,0:T(8,128)(2,1)S(1)} collective-permute-done((bf16[256,2048]{1,0:T(8,128)(2,1)S(1)}, bf16[256,2048]{1,0:T(8,128)(2,1)S(1)}, u32[]{:S(2)}, u32[]{:S(2)}) %collective-permute-start.36) | collective-permute-done | bytes 1048608 | tf_op jit(solution)/shard_map/ppermute | solution.py:1214
  681.8 2.5 collective-permute-start.40
  689.4 17.9 %collective-permute-done.41 = bf16[128,1664]{1,0:T(8,128)(2,1)S(1)} collective-permute-done((bf16[128,1664]{1,0:T(8,128)(2,1)S(1)}, bf16[128,1664]{1,0:T(8,128)(2,1)S(1)}, u32[]{:S(2)}, u32[]{:S(2)}) %collective-permute-start.41) | collective-permute-done | bytes 426016 | tf_op jit(solution)/shard_map/ppermute | solution.py:885
  713.6 3.1 collective-permute-start.44
  718.5 16.2 %collective-permute-done.46 = bf16[256,2048]{1,0:T(8,128)(2,1)S(1)} collective-permute-done((bf16[256,2048]{1,0:T(8,128)(2,1)S(1)}, bf16[256,2048]{1,0:T(8,128)(2,1)S(1)}, u32[]{:S(2)}, u32[]{:S(2)}) %collective-permute-start.46) | collective-permute-done | bytes 1048608 | tf_op jit(solution)/shard_map/ppermute | solution.py:885
  734.7 3.0 collective-permute-done.43
  745.9 6.6 collective-permute-done.50
  752.6 8.5 %collective-permute-done.49 = bf16[256,1664]{1,0:T(8,128)(2,1)S(1)} collective-permute-done((bf16[256,1664]{1,0:T(8,128)(2,1)S(1)}, bf16[256,1664]{1,0:T(8,128)(2,1)S(1)}, u32[]{:S(2)}, u32[]{:S(2)}) %collective-permute-start.49) | collective-permute-done | bytes 852000 | tf_op jit(solution)/shard_map/ppermute | solution.py:885
  765.2 3.4 slice_bitcast_fusion.1
  774.1 3.0 broadcast_select_fusion
  783.3 2.5 copy.192
  785.8 4.1 copy.191
  795.1 7.9 collective-permute-done.55
  809.1 13.4 %collective-permute-done.51 = bf16[256,2048]{1,0:T(8,128)(2,1)S(1)} collective-permute-done((bf16[256,2048]{1,0:T(8,128)(2,1)}, bf16[256,2048]{1,0:T(8,128)(2,1)S(1)}, u32[]{:S(2)}, u32[]{:S(2)}) %collective-permute-start.51) | collective-permute-done | bytes 1048608 | tf_op jit(solution)/shard_map/ppermute | solution.py:1215
  824.1 3.0 select_dynamic-update-slice_fusion.1
  827.1 2.9 select_dynamic-update-slice_fusion
  (427 shorter events, 163.0 us)
Async XLA Ops:
  7.2 192.2 %all-gather.7.cloned.1.call-start = ((), (), s32[]{:S(2)}) async-start(), calls=%async_computation.9 | async-start | bytes 15728640 | tf_op jit(solution)/shard_map/all_gather | solution.py:957
  19.1 280.7 %all-gather.5.cloned.1.call-start = ((), (), s32[]{:S(2)}) async-start(), calls=%async_computation.8 | async-start | bytes 15728640 | tf_op jit(solution)/shard_map/all_gather | solution.py:957
  21.5 49.5 %collective-permute-start.3 = (bf16[256,2048]{1,0:T(8,128)(2,1)}, bf16[256,2048]{1,0:T(8,128)(2,1)}, u32[]{:S(2)}, u32[]{:S(2)}) collective-permute-start(bf16[256,2048]{1,0:T(8,128)(2,1)} %constant_dynamic-slice_fusion.6), channel_id=1, source_target_pairs={{0,1},{1,0},{2,3},{3,2},{4,5},{5,4},{6,7},{7,6},{8,9},{9,8},{10,11... | collective-permute-start | bytes 3145736 | tf_op jit(solution)/shard_map/ppermute | solution.py:1192
  23.1 47.9 %collective-permute-start.4 = (bf16[256,2048]{1,0:T(8,128)(2,1)}, bf16[256,2048]{1,0:T(8,128)(2,1)}, u32[]{:S(2)}, u32[]{:S(2)}) collective-permute-start(bf16[256,2048]{1,0:T(8,128)(2,1)} %constant_dynamic-slice_fusion.6), channel_id=1, source_target_pairs={{0,2},{1,3},{2,0},{3,1},{4,6},{5,7},{6,4},{7,5},{8,10},{9,11},{10,... | collective-permute-start | bytes 3145736 | tf_op jit(solution)/shard_map/ppermute | solution.py:1192
  45.5 25.4 %collective-permute-start = (f32[16,128]{1,0:T(8,128)S(1)}, f32[16,128]{1,0:T(8,128)S(1)}, u32[]{:S(2)}, u32[]{:S(2)}) collective-permute-start(f32[16,128]{1,0:T(8,128)S(1)} %reshape.249), channel_id=1, source_target_pairs={{0,1},{1,2},{2,3},{3,0},{4,5},{5,6},{6,7},{7,4},{8,9},{9,10},{10,1... | collective-permute-start | bytes 24584 | tf_op jit(solution)/shard_map/ppermute | solution.py:1288
  45.9 25.0 %collective-permute-start.1 = (f32[16,128]{1,0:T(8,128)S(1)}, f32[16,128]{1,0:T(8,128)S(1)}, u32[]{:S(2)}, u32[]{:S(2)}) collective-permute-start(f32[16,128]{1,0:T(8,128)S(1)} %reshape.249), channel_id=1, source_target_pairs={{0,2},{1,3},{2,0},{3,1},{4,6},{5,7},{6,4},{7,5},{8,10},{9,11},{10,... | collective-permute-start | bytes 24584 | tf_op jit(solution)/shard_map/ppermute | solution.py:1288
  48.3 22.6 %collective-permute-start.2 = (f32[16,128]{1,0:T(8,128)S(1)}, f32[16,128]{1,0:T(8,128)S(1)}, u32[]{:S(2)}, u32[]{:S(2)}) collective-permute-start(f32[16,128]{1,0:T(8,128)S(1)} %reshape.249), channel_id=1, source_target_pairs={{0,3},{1,0},{2,1},{3,2},{4,7},{5,4},{6,5},{7,6},{8,11},{9,8},{10,9... | collective-permute-start | bytes 24584 | tf_op jit(solution)/shard_map/ppermute | solution.py:1288
  73.1 47.9 %collective-permute-start.5 = (bf16[256,2048]{1,0:T(8,128)(2,1)}, bf16[256,2048]{1,0:T(8,128)(2,1)S(1)}, u32[]{:S(2)}, u32[]{:S(2)}) collective-permute-start(bf16[256,2048]{1,0:T(8,128)(2,1)} %collective-permute-done.4), channel_id=1, source_target_pairs={{0,1},{1,0},{2,3},{3,2},{4,5},{5,4},{6,7},{7,6},{8,9},{9,8},{10,11... | collective-permute-start | bytes 3145736 | tf_op jit(solution)/shard_map/ppermute | solution.py:1192
  90.0 51.3 %collective-permute-start.6 = (bf16[1024,512]{1,0:T(8,128)(2,1)}, bf16[1024,512]{1,0:T(8,128)(2,1)S(1)}, u32[]{:S(2)}, u32[]{:S(2)}) collective-permute-start(bf16[1024,512]{1,0:T(8,128)(2,1)} %get-tuple-element.157.refs_0_.ctx_ref), channel_id=1, source_target_pairs={{0,1},{1,0},{2,3},{3,2},{4,5},{5,4},{6,7},{7,6},{8,9},{9,8},{10,11... | collective-permute-start | bytes 3145736 | tf_op jit(solution)/shard_map/ppermute | solution.py:1192
  90.9 52.4 %collective-permute-start.7 = (bf16[1024,512]{1,0:T(8,128)(2,1)}, bf16[1024,512]{1,0:T(8,128)(2,1)S(1)}, u32[]{:S(2)}, u32[]{:S(2)}) collective-permute-start(bf16[1024,512]{1,0:T(8,128)(2,1)} %get-tuple-element.157.refs_0_.ctx_ref), channel_id=1, source_target_pairs={{0,2},{1,3},{2,0},{3,1},{4,6},{5,7},{6,4},{7,5},{8,10},{9,11},{10,... | collective-permute-start | bytes 3145736 | tf_op jit(solution)/shard_map/ppermute | solution.py:1192
  146.3 28.1 %copy-start.81 = (s32[1024,8]{0,1:T(8,128)S(1)}, s32[1024,8]{0,1:T(8,128)}, u32[]{:S(2)}) copy-start(s32[1024,8]{0,1:T(8,128)} %param.21) | copy-start | bytes 98308
  146.3 28.1 %copy-start.82 = (s32[1024,8]{0,1:T(8,128)S(1)}, s32[1024,8]{0,1:T(8,128)}, u32[]{:S(2)}) copy-start(s32[1024,8]{0,1:T(8,128)} %param.20) | copy-start | bytes 98308
  148.0 25.6 %collective-permute-start.8 = (bf16[768,2048]{1,0:T(8,128)(2,1)S(1)}, bf16[768,2048]{1,0:T(8,128)(2,1)}, u32[]{:S(2)}, u32[]{:S(2)}) collective-permute-start(bf16[768,2048]{1,0:T(8,128)(2,1)S(1)} %constant_dynamic-update-slice_fusion.refs_5_), channel_id=1, source_target_pairs={{0,4},{4,0},{8,12},{12,8},{16,20},{20,16},{24,28},{28,24},{1,5},{5... | collective-permute-start | bytes 9437192 | tf_op jit(solution)/shard_map/ppermute | solution.py:885
  148.0 25.6 %collective-permute-start.9 = (bf16[1024,512]{1,0:T(8,128)(2,1)S(1)}, bf16[1024,512]{1,0:T(8,128)(2,1)S(1)}, u32[]{:S(2)}, u32[]{:S(2)}) collective-permute-start(bf16[1024,512]{1,0:T(8,128)(2,1)S(1)} %collective-permute-done.7.refs_2_), channel_id=1, source_target_pairs={{0,1},{1,0},{2,3},{3,2},{4,5},{5,4},{6,7},{7,6},{8,9},{9,8},{10,11... | collective-permute-start | bytes 3145736 | tf_op jit(solution)/shard_map/ppermute | solution.py:1192
  173.6 220.7 %reduce-scatter.5.cloned.1.call-start = ((), (), s32[]{:S(2)}) async-start(), calls=%async_computation.4 | async-start | bytes 2785280 | tf_op jit(solution)/shard_map/reduce_scatter | solution.py:922
  174.5 23.7 %collective-permute-start.11 = (bf16[1024,2048]{1,0:T(8,128)(2,1)}, bf16[1024,2048]{1,0:T(8,128)(2,1)}, u32[]{:S(2)}, u32[]{:S(2)}) collective-permute-start(bf16[1024,2048]{1,0:T(8,128)(2,1)} %param.18), channel_id=1, source_target_pairs={{0,4},{4,0},{8,12},{12,8},{16,20},{20,16},{24,28},{28,24},{1,5},{5... | collective-permute-start | bytes 12582920 | tf_op jit(solution)/shard_map/ppermute | solution.py:885
  191.7 7.7 collective-permute-start.10
  192.2 5.2 collective-permute-start.12
  297.7 42.8 %collective-permute-start.13 = (bf16[384,2048]{1,0:T(8,128)(2,1)}, bf16[384,2048]{1,0:T(8,128)(2,1)S(1)}, u32[]{:S(2)}, u32[]{:S(2)}) collective-permute-start(bf16[384,2048]{1,0:T(8,128)(2,1)} %get-tuple-element.186.refs_13_), channel_id=1, source_target_pairs={{0,8},{4,12},{8,0},{12,4},{16,24},{20,28},{24,16},{28,20},{1,9},{5... | collective-permute-start | bytes 4718600 | tf_op jit(solution)/shard_map/ppermute | solution.py:885
  299.3 41.3 %collective-permute-start.14 = (bf16[384,2048]{1,0:T(8,128)(2,1)}, bf16[384,2048]{1,0:T(8,128)(2,1)}, u32[]{:S(2)}, u32[]{:S(2)}) collective-permute-start(bf16[384,2048]{1,0:T(8,128)(2,1)} %get-tuple-element.187.refs_14_), channel_id=1, source_target_pairs={{0,16},{4,20},{8,24},{12,28},{16,0},{20,4},{24,8},{28,12},{1,17},{... | collective-permute-start | bytes 4718600 | tf_op jit(solution)/shard_map/ppermute | solution.py:885
  340.6 4.6 collective-permute-start.15
  348.8 105.1 %reduce-scatter.7.cloned.1.call-start = ((), (), s32[]{:S(2)}) async-start(), calls=%async_computation.5 | async-start | bytes 2785280 | tf_op jit(solution)/shard_map/reduce_scatter | solution.py:922
  394.3 4.6 collective-permute-start.16
  402.4 178.1 %reduce-scatter.9.cloned.1.call-start = ((), (), s32[]{:S(2)}) async-start(), calls=%async_computation.6 | async-start | bytes 5242880 | tf_op jit(solution)/shard_map/reduce_scatter | solution.py:922
  469.3 23.7 %collective-permute-start.20 = (bf16[512,2048]{1,0:T(8,128)(2,1)S(1)}, bf16[512,2048]{1,0:T(8,128)(2,1)S(1)}, u32[]{:S(2)}, u32[]{:S(2)}) collective-permute-start(bf16[512,2048]{1,0:T(8,128)(2,1)S(1)} %copy-done.85), channel_id=1, source_target_pairs={{0,4},{4,0},{8,12},{12,8},{16,20},{20,16},{24,28},{28,24},{1,5},{5... | collective-permute-start | bytes 6291464 | tf_op jit(solution)/shard_map/ppermute | solution.py:885
  469.4 24.6 %collective-permute-start.21 = (bf16[512,2048]{1,0:T(8,128)(2,1)}, bf16[512,2048]{1,0:T(8,128)(2,1)S(1)}, u32[]{:S(2)}, u32[]{:S(2)}) collective-permute-start(bf16[512,2048]{1,0:T(8,128)(2,1)} %get-tuple-element.219), channel_id=1, source_target_pairs={{0,4},{4,0},{8,12},{12,8},{16,20},{20,16},{24,28},{28,24},{1,5},{5... | collective-permute-start | bytes 6291464 | tf_op jit(solution)/shard_map/ppermute | solution.py:885
  469.9 23.1 %collective-permute-start.19 = (bf16[256,512]{1,0:T(8,128)(2,1)S(1)}, bf16[256,512]{1,0:T(8,128)(2,1)S(1)}, u32[]{:S(2)}, u32[]{:S(2)}) collective-permute-start(bf16[256,512]{1,0:T(8,128)(2,1)S(1)} %pad_maximum_fusion.20), channel_id=1, source_target_pairs={{0,3},{1,2},{2,1},{3,0},{4,7},{5,6},{6,5},{7,4},{8,11},{9,10},{10,... | collective-permute-start | bytes 786440 | tf_op jit(solution)/shard_map/ppermute | solution.py:1192
  470.0 22.9 %collective-permute-start.18 = (bf16[256,512]{1,0:T(8,128)(2,1)S(1)}, bf16[256,512]{1,0:T(8,128)(2,1)S(1)}, u32[]{:S(2)}, u32[]{:S(2)}) collective-permute-start(bf16[256,512]{1,0:T(8,128)(2,1)S(1)} %pad_maximum_fusion.19), channel_id=1, source_target_pairs={{0,2},{1,3},{2,0},{3,1},{4,6},{5,7},{6,4},{7,5},{8,10},{9,11},{10,... | collective-permute-start | bytes 786440 | tf_op jit(solution)/shard_map/ppermute | solution.py:1192
  472.9 17.2 %collective-permute-start.17 = (bf16[256,512]{1,0:T(8,128)(2,1)S(1)}, bf16[256,512]{1,0:T(8,128)(2,1)S(1)}, u32[]{:S(2)}, u32[]{:S(2)}) collective-permute-start(bf16[256,512]{1,0:T(8,128)(2,1)S(1)} %pad_maximum_fusion.18), channel_id=1, source_target_pairs={{0,1},{1,0},{2,3},{3,2},{4,5},{5,4},{6,7},{7,6},{8,9},{9,8},{10,11... | collective-permute-start | bytes 786440 | tf_op jit(solution)/shard_map/ppermute | solution.py:1192
  498.1 267.0 %reduce-scatter.11.cloned.1.call-start = ((), (), s32[]{:S(2)}) async-start(), calls=%async_computation.7 | async-start | bytes 15728640 | tf_op jit(solution)/shard_map/reduce_scatter | solution.py:1092
  498.2 38.2 %collective-permute-start.22 = (bf16[1024,2048]{1,0:T(8,128)(2,1)}, bf16[1024,2048]{1,0:T(8,128)(2,1)}, u32[]{:S(2)}, u32[]{:S(2)}) collective-permute-start(bf16[1024,2048]{1,0:T(8,128)(2,1)} %get-tuple-element.222.rest_0_), channel_id=1, source_target_pairs={{0,4},{4,0},{8,12},{12,8},{16,20},{20,16},{24,28},{28,24},{1,5},{5... | collective-permute-start | bytes 12582920 | tf_op jit(solution)/shard_map/ppermute | solution.py:885
  498.3 37.5 %collective-permute-start.23 = (bf16[384,2048]{1,0:T(8,128)(2,1)}, bf16[384,2048]{1,0:T(8,128)(2,1)S(1)}, u32[]{:S(2)}, u32[]{:S(2)}) collective-permute-start(bf16[384,2048]{1,0:T(8,128)(2,1)} %get-tuple-element.209.refs_16_), channel_id=1, source_target_pairs={{0,16},{4,20},{8,24},{12,28},{16,0},{20,4},{24,8},{28,12},{1,17},{... | collective-permute-start | bytes 4718600 | tf_op jit(solution)/shard_map/ppermute | solution.py:885
  498.9 37.6 %collective-permute-start.24 = (bf16[384,2048]{1,0:T(8,128)(2,1)}, bf16[384,2048]{1,0:T(8,128)(2,1)}, u32[]{:S(2)}, u32[]{:S(2)}) collective-permute-start(bf16[384,2048]{1,0:T(8,128)(2,1)} %get-tuple-element.229), channel_id=1, source_target_pairs={{0,8},{4,12},{8,0},{12,4},{16,24},{20,28},{24,16},{28,20},{1,9},{5... | collective-permute-start | bytes 4718600 | tf_op jit(solution)/shard_map/ppermute | solution.py:885
  500.3 79.1 %collective-permute-start.30 = (bf16[384,2048]{1,0:T(8,128)(2,1)}, bf16[384,2048]{1,0:T(8,128)(2,1)}, u32[]{:S(2)}, u32[]{:S(2)}) collective-permute-start(bf16[384,2048]{1,0:T(8,128)(2,1)} %get-tuple-element.235), channel_id=1, source_target_pairs={{0,16},{4,20},{8,24},{12,28},{16,0},{20,4},{24,8},{28,12},{1,17},{... | collective-permute-start | bytes 4718600 | tf_op jit(solution)/shard_map/ppermute | solution.py:885
  501.8 77.7 %collective-permute-start.31 = (bf16[384,2048]{1,0:T(8,128)(2,1)}, bf16[384,2048]{1,0:T(8,128)(2,1)}, u32[]{:S(2)}, u32[]{:S(2)}) collective-permute-start(bf16[384,2048]{1,0:T(8,128)(2,1)} %get-tuple-element.236), channel_id=1, source_target_pairs={{0,8},{4,12},{8,0},{12,4},{16,24},{20,28},{24,16},{28,20},{1,9},{5... | collective-permute-start | bytes 4718600 | tf_op jit(solution)/shard_map/ppermute | solution.py:885
  538.4 15.1 %collective-permute-start.25 = (f32[16,128]{1,0:T(8,128)S(1)}, f32[16,128]{1,0:T(8,128)S(1)}, u32[]{:S(2)}, u32[]{:S(2)}) collective-permute-start(f32[16,128]{1,0:T(8,128)S(1)} %reshape.258), channel_id=1, source_target_pairs={{0,1},{1,2},{2,3},{3,0},{4,5},{5,6},{6,7},{7,4},{8,9},{9,10},{10,1... | collective-permute-start | bytes 24584 | tf_op jit(solution)/shard_map/ppermute | solution.py:1288
  542.1 12.9 %collective-permute-start.26 = (f32[16,128]{1,0:T(8,128)S(1)}, f32[16,128]{1,0:T(8,128)S(1)}, u32[]{:S(2)}, u32[]{:S(2)}) collective-permute-start(f32[16,128]{1,0:T(8,128)S(1)} %reshape.258), channel_id=1, source_target_pairs={{0,2},{1,3},{2,0},{3,1},{4,6},{5,7},{6,4},{7,5},{8,10},{9,11},{10,... | collective-permute-start | bytes 24584 | tf_op jit(solution)/shard_map/ppermute | solution.py:1288
  542.1 14.5 %collective-permute-start.27 = (f32[16,128]{1,0:T(8,128)S(1)}, f32[16,128]{1,0:T(8,128)S(1)}, u32[]{:S(2)}, u32[]{:S(2)}) collective-permute-start(f32[16,128]{1,0:T(8,128)S(1)} %reshape.258), channel_id=1, source_target_pairs={{0,3},{1,0},{2,1},{3,2},{4,7},{5,4},{6,5},{7,6},{8,11},{9,8},{10,9... | collective-permute-start | bytes 24584 | tf_op jit(solution)/shard_map/ppermute | solution.py:1288
  553.6 26.9 %collective-permute-start.28 = (bf16[128,2048]{1,0:T(8,128)(2,1)}, bf16[128,2048]{1,0:T(8,128)(2,1)S(1)}, u32[]{:S(2)}, u32[]{:S(2)}) collective-permute-start(bf16[128,2048]{1,0:T(8,128)(2,1)} %get-tuple-element.403), channel_id=1, source_target_pairs={{0,8},{4,12},{8,0},{12,4},{16,24},{20,28},{24,16},{28,20},{1,9},{5... | collective-permute-start | bytes 1572872 | tf_op jit(solution)/shard_map/ppermute | solution.py:885
  555.1 25.4 %collective-permute-start.29 = (bf16[128,2048]{1,0:T(8,128)(2,1)}, bf16[128,2048]{1,0:T(8,128)(2,1)S(1)}, u32[]{:S(2)}, u32[]{:S(2)}) collective-permute-start(bf16[128,2048]{1,0:T(8,128)(2,1)} %get-tuple-element.402), channel_id=1, source_target_pairs={{0,16},{4,20},{8,24},{12,28},{16,0},{20,4},{24,8},{28,12},{1,17},{... | collective-permute-start | bytes 1572872 | tf_op jit(solution)/shard_map/ppermute | solution.py:885
  584.6 26.4 %collective-permute-start.32 = (bf16[256,2048]{1,0:T(8,128)(2,1)S(1)}, bf16[256,2048]{1,0:T(8,128)(2,1)S(1)}, u32[]{:S(2)}, u32[]{:S(2)}) collective-permute-start(bf16[256,2048]{1,0:T(8,128)(2,1)S(1)} %get-tuple-element.393), channel_id=1, source_target_pairs={{0,1},{1,0},{2,3},{3,2},{4,5},{5,4},{6,7},{7,6},{8,9},{9,8},{10,11... | collective-permute-start | bytes 3145736 | tf_op jit(solution)/shard_map/ppermute | solution.py:1214
  588.3 26.0 %collective-permute-start.33 = (bf16[256,2048]{1,0:T(8,128)(2,1)S(1)}, bf16[256,2048]{1,0:T(8,128)(2,1)S(1)}, u32[]{:S(2)}, u32[]{:S(2)}) collective-permute-start(bf16[256,2048]{1,0:T(8,128)(2,1)S(1)} %get-tuple-element.393), channel_id=1, source_target_pairs={{1,2},{2,1},{0,0},{3,3},{5,6},{6,5},{4,4},{7,7},{9,10},{10,9},{8,8... | collective-permute-start | bytes 3145736 | tf_op jit(solution)/shard_map/ppermute | solution.py:1215
  617.6 23.2 %collective-permute-start.34 = (bf16[256,2048]{1,0:T(8,128)(2,1)S(1)}, bf16[256,2048]{1,0:T(8,128)(2,1)S(1)}, u32[]{:S(2)}, u32[]{:S(2)}) collective-permute-start(bf16[256,2048]{1,0:T(8,128)(2,1)S(1)} %broadcast_select_fusion.17), channel_id=1, source_target_pairs={{0,1},{1,0},{2,3},{3,2},{4,5},{5,4},{6,7},{7,6},{8,9},{9,8},{10,11... | collective-permute-start | bytes 3145736 | tf_op jit(solution)/shard_map/ppermute | solution.py:1214
  617.7 25.1 %collective-permute-start.35 = (bf16[256,2048]{1,0:T(8,128)(2,1)S(1)}, bf16[256,2048]{1,0:T(8,128)(2,1)S(1)}, u32[]{:S(2)}, u32[]{:S(2)}) collective-permute-start(bf16[256,2048]{1,0:T(8,128)(2,1)S(1)} %get-tuple-element.389), channel_id=1, source_target_pairs={{1,2},{2,1},{0,0},{3,3},{5,6},{6,5},{4,4},{7,7},{9,10},{10,9},{8,8... | collective-permute-start | bytes 3145736 | tf_op jit(solution)/shard_map/ppermute | solution.py:1215
  642.9 34.9 %collective-permute-start.38 = (bf16[1024,1664]{1,0:T(8,128)(2,1)S(1)}, bf16[1024,1664]{1,0:T(8,128)(2,1)S(1)}, u32[]{:S(2)}, u32[]{:S(2)}) collective-permute-start(bf16[1024,1664]{1,0:T(8,128)(2,1)S(1)} %get-tuple-element.254), channel_id=1, source_target_pairs={{0,4},{4,0},{8,12},{12,8},{16,20},{20,16},{24,28},{28,24},{1,5},{5... | collective-permute-start | bytes 10223624 | tf_op jit(solution)/shard_map/ppermute | solution.py:885
  649.7 26.0 %collective-permute-start.36 = (bf16[256,2048]{1,0:T(8,128)(2,1)S(1)}, bf16[256,2048]{1,0:T(8,128)(2,1)S(1)}, u32[]{:S(2)}, u32[]{:S(2)}) collective-permute-start(bf16[256,2048]{1,0:T(8,128)(2,1)S(1)} %broadcast_select_fusion.13), channel_id=1, source_target_pairs={{0,1},{1,0},{2,3},{3,2},{4,5},{5,4},{6,7},{7,6},{8,9},{9,8},{10,11... | collective-permute-start | bytes 3145736 | tf_op jit(solution)/shard_map/ppermute | solution.py:1214
  649.7 28.0 %collective-permute-start.37 = (bf16[256,2048]{1,0:T(8,128)(2,1)S(1)}, bf16[256,2048]{1,0:T(8,128)(2,1)S(1)}, u32[]{:S(2)}, u32[]{:S(2)}) collective-permute-start(bf16[256,2048]{1,0:T(8,128)(2,1)S(1)} %get-tuple-element.386), channel_id=1, source_target_pairs={{1,2},{2,1},{0,0},{3,3},{5,6},{6,5},{4,4},{7,7},{9,10},{10,9},{8,8... | collective-permute-start | bytes 3145736 | tf_op jit(solution)/shard_map/ppermute | solution.py:1215
  681.8 27.0 %collective-permute-start.39 = (bf16[256,2048]{1,0:T(8,128)(2,1)}, bf16[256,2048]{1,0:T(8,128)(2,1)S(1)}, u32[]{:S(2)}, u32[]{:S(2)}) collective-permute-start(bf16[256,2048]{1,0:T(8,128)(2,1)} %broadcast_select_fusion.9), channel_id=1, source_target_pairs={{0,1},{1,0},{2,3},{3,2},{4,5},{5,4},{6,7},{7,6},{8,9},{9,8},{10,11... | collective-permute-start | bytes 3145736 | tf_op jit(solution)/shard_map/ppermute | solution.py:1214
  681.8 27.1 %collective-permute-start.40 = (bf16[256,2048]{1,0:T(8,128)(2,1)S(1)}, bf16[256,2048]{1,0:T(8,128)(2,1)S(1)}, u32[]{:S(2)}, u32[]{:S(2)}) collective-permute-start(bf16[256,2048]{1,0:T(8,128)(2,1)S(1)} %get-tuple-element.383), channel_id=1, source_target_pairs={{1,2},{2,1},{0,0},{3,3},{5,6},{6,5},{4,4},{7,7},{9,10},{10,9},{8,8... | collective-permute-start | bytes 3145736 | tf_op jit(solution)/shard_map/ppermute | solution.py:1215
  685.4 21.8 %collective-permute-start.41 = (bf16[128,1664]{1,0:T(8,128)(2,1)S(1)}, bf16[128,1664]{1,0:T(8,128)(2,1)S(1)}, u32[]{:S(2)}, u32[]{:S(2)}) collective-permute-start(bf16[128,1664]{1,0:T(8,128)(2,1)S(1)} %get-tuple-element.409), channel_id=1, source_target_pairs={{0,8},{4,12},{8,0},{12,4},{16,24},{20,28},{24,16},{28,20},{1,9},{5... | collective-permute-start | bytes 1277960 | tf_op jit(solution)/shard_map/ppermute | solution.py:885
  687.1 21.8 %collective-permute-start.42 = (bf16[128,1664]{1,0:T(8,128)(2,1)S(1)}, bf16[128,1664]{1,0:T(8,128)(2,1)S(1)}, u32[]{:S(2)}, u32[]{:S(2)}) collective-permute-start(bf16[128,1664]{1,0:T(8,128)(2,1)S(1)} %get-tuple-element.408), channel_id=1, source_target_pairs={{0,16},{4,20},{8,24},{12,28},{16,0},{20,4},{24,8},{28,12},{1,17},{... | collective-permute-start | bytes 1277960 | tf_op jit(solution)/shard_map/ppermute | solution.py:885
  688.7 46.0 %collective-permute-start.46 = (bf16[256,2048]{1,0:T(8,128)(2,1)S(1)}, bf16[256,2048]{1,0:T(8,128)(2,1)S(1)}, u32[]{:S(2)}, u32[]{:S(2)}) collective-permute-start(bf16[256,2048]{1,0:T(8,128)(2,1)S(1)} %pad_maximum_fusion.10), channel_id=1, source_target_pairs={{0,8},{4,12},{8,0},{12,4},{16,24},{20,28},{24,16},{28,20},{1,9},{5... | collective-permute-start | bytes 3145736 | tf_op jit(solution)/shard_map/ppermute | solution.py:885
  707.3 27.4 %collective-permute-start.45 = (bf16[256,2048]{1,0:T(8,128)(2,1)S(1)}, bf16[256,2048]{1,0:T(8,128)(2,1)S(1)}, u32[]{:S(2)}, u32[]{:S(2)}) collective-permute-start(bf16[256,2048]{1,0:T(8,128)(2,1)S(1)} %pad_maximum_fusion.9), channel_id=1, source_target_pairs={{0,16},{4,20},{8,24},{12,28},{16,0},{20,4},{24,8},{28,12},{1,17},{... | collective-permute-start | bytes 3145736 | tf_op jit(solution)/shard_map/ppermute | solution.py:885
  713.2 24.5 %collective-permute-start.43 = (bf16[256,2048]{1,0:T(8,128)(2,1)S(1)}, bf16[256,2048]{1,0:T(8,128)(2,1)S(1)}, u32[]{:S(2)}, u32[]{:S(2)}) collective-permute-start(bf16[256,2048]{1,0:T(8,128)(2,1)S(1)} %get-tuple-element.382), channel_id=1, source_target_pairs={{0,1},{1,0},{2,3},{3,2},{4,5},{5,4},{6,7},{7,6},{8,9},{9,8},{10,11... | collective-permute-start | bytes 3145736 | tf_op jit(solution)/shard_map/ppermute | solution.py:1214
  713.6 26.1 %collective-permute-start.44 = (bf16[256,2048]{1,0:T(8,128)(2,1)S(1)}, bf16[256,2048]{1,0:T(8,128)(2,1)S(1)}, u32[]{:S(2)}, u32[]{:S(2)}) collective-permute-start(bf16[256,2048]{1,0:T(8,128)(2,1)S(1)} %get-tuple-element.382), channel_id=1, source_target_pairs={{1,2},{2,1},{0,0},{3,3},{5,6},{6,5},{4,4},{7,7},{9,10},{10,9},{8,8... | collective-permute-start | bytes 3145736 | tf_op jit(solution)/shard_map/ppermute | solution.py:1215
  717.0 35.6 %collective-permute-start.50 = (bf16[256,1664]{1,0:T(8,128)(2,1)S(1)}, bf16[256,1664]{1,0:T(8,128)(2,1)S(1)}, u32[]{:S(2)}, u32[]{:S(2)}) collective-permute-start(bf16[256,1664]{1,0:T(8,128)(2,1)S(1)} %pad_maximum_fusion.12), channel_id=1, source_target_pairs={{0,8},{4,12},{8,0},{12,4},{16,24},{20,28},{24,16},{28,20},{1,9},{5... | collective-permute-start | bytes 2555912 | tf_op jit(solution)/shard_map/ppermute | solution.py:885
  739.8 23.4 %collective-permute-start.47 = (bf16[256,2048]{1,0:T(8,128)(2,1)S(1)}, bf16[256,2048]{1,0:T(8,128)(2,1)}, u32[]{:S(2)}, u32[]{:S(2)}) collective-permute-start(bf16[256,2048]{1,0:T(8,128)(2,1)S(1)} %get-tuple-element.418), channel_id=1, source_target_pairs={{0,1},{1,0},{2,3},{3,2},{4,5},{5,4},{6,7},{7,6},{8,9},{9,8},{10,11... | collective-permute-start | bytes 3145736 | tf_op jit(solution)/shard_map/ppermute | solution.py:1214
  739.9 25.3 %collective-permute-start.48 = (bf16[256,2048]{1,0:T(8,128)(2,1)S(1)}, bf16[256,2048]{1,0:T(8,128)(2,1)}, u32[]{:S(2)}, u32[]{:S(2)}) collective-permute-start(bf16[256,2048]{1,0:T(8,128)(2,1)S(1)} %get-tuple-element.417), channel_id=1, source_target_pairs={{1,2},{2,1},{0,0},{3,3},{5,6},{6,5},{4,4},{7,7},{9,10},{10,9},{8,8... | collective-permute-start | bytes 3145736 | tf_op jit(solution)/shard_map/ppermute | solution.py:1215
  742.2 18.8 %collective-permute-start.49 = (bf16[256,1664]{1,0:T(8,128)(2,1)S(1)}, bf16[256,1664]{1,0:T(8,128)(2,1)S(1)}, u32[]{:S(2)}, u32[]{:S(2)}) collective-permute-start(bf16[256,1664]{1,0:T(8,128)(2,1)S(1)} %pad_maximum_fusion.11), channel_id=1, source_target_pairs={{0,16},{4,20},{8,24},{12,28},{16,0},{20,4},{24,8},{28,12},{1,17},{... | collective-permute-start | bytes 2555912 | tf_op jit(solution)/shard_map/ppermute | solution.py:885
  770.6 20.8 %collective-permute-start.53 = (bf16[256,640]{1,0:T(8,128)(2,1)}, bf16[256,640]{1,0:T(8,128)(2,1)}, u32[]{:S(2)}, u32[]{:S(2)}) collective-permute-start(bf16[256,640]{1,0:T(8,128)(2,1)} %get-tuple-element.441), channel_id=1, source_target_pairs={{0,1},{1,0},{2,3},{3,2},{4,5},{5,4},{6,7},{7,6},{8,9},{9,8},{10,11... | collective-permute-start | bytes 983048 | tf_op jit(solution)/shard_map/ppermute | solution.py:1192
  770.6 23.4 %collective-permute-start.54 = (bf16[256,640]{1,0:T(8,128)(2,1)}, bf16[256,640]{1,0:T(8,128)(2,1)}, u32[]{:S(2)}, u32[]{:S(2)}) collective-permute-start(bf16[256,640]{1,0:T(8,128)(2,1)} %get-tuple-element.442), channel_id=1, source_target_pairs={{0,2},{1,3},{2,0},{3,1},{4,6},{5,7},{6,4},{7,5},{8,10},{9,11},{10,... | collective-permute-start | bytes 983048 | tf_op jit(solution)/shard_map/ppermute | solution.py:1192
  772.3 30.6 %collective-permute-start.55 = (bf16[256,640]{1,0:T(8,128)(2,1)S(1)}, bf16[256,640]{1,0:T(8,128)(2,1)}, u32[]{:S(2)}, u32[]{:S(2)}) collective-permute-start(bf16[256,640]{1,0:T(8,128)(2,1)S(1)} %get-tuple-element.443), channel_id=1, source_target_pairs={{0,3},{1,2},{2,1},{3,0},{4,7},{5,6},{6,5},{7,4},{8,11},{9,10},{10,... | collective-permute-start | bytes 983048 | tf_op jit(solution)/shard_map/ppermute | solution.py:1192
  777.1 45.3 %collective-permute-start.51 = (bf16[256,2048]{1,0:T(8,128)(2,1)}, bf16[256,2048]{1,0:T(8,128)(2,1)S(1)}, u32[]{:S(2)}, u32[]{:S(2)}) collective-permute-start(bf16[256,2048]{1,0:T(8,128)(2,1)} %get-tuple-element.416), channel_id=1, source_target_pairs={{1,2},{2,1},{0,0},{3,3},{5,6},{6,5},{4,4},{7,7},{9,10},{10,9},{8,8... | collective-permute-start | bytes 3145736 | tf_op jit(solution)/shard_map/ppermute | solution.py:1215
  779.4 43.0 %collective-permute-start.52 = (bf16[256,2048]{1,0:T(8,128)(2,1)}, bf16[256,2048]{1,0:T(8,128)(2,1)}, u32[]{:S(2)}, u32[]{:S(2)}) collective-permute-start(bf16[256,2048]{1,0:T(8,128)(2,1)} %get-tuple-element.415), channel_id=1, source_target_pairs={{0,1},{1,0},{2,3},{3,2},{4,5},{5,4},{6,7},{7,6},{8,9},{9,8},{10,11... | collective-permute-start | bytes 3145736 | tf_op jit(solution)/shard_map/ppermute | solution.py:1214
  (85 other events, 548.9 us)
Sparse Core Ops, SparseCore 0:
  19.2 123.5 all-gather.6
  173.7 123.3 all-gather.4
  348.9 45.4 reduce-scatter.4
  402.6 45.3 reduce-scatter.6
  498.3 80.8 reduce-scatter.8
  582.4 136.6 reduce-scatter.10

commit v4 on v3

--- a/solution.py
+++ b/solution.py
@@ -1086,9 +1086,10 @@
     inner = jnp.sum(inner, axis=0).T
     inner = sum_small(inner.reshape(-1, LANES)).reshape(inner.shape)
     output_grads = block_terms(plus(output_grads[0], came))
-    output_via = send(output_grads[0], (2, 4))
     second = part(1, 0 * chip + 2, 0 * chip + 3, (), [inner], pair=1, into=second)
-    inner, moe, second, *output_via, near_high[0], near_high[1] = join(inner, moe, second, *output_via, *near_high)
+    across = output_grads[0]
+    inner, moe, second, near_high[0], near_high[1], *across = join(inner, moe, second, *near_high, *across)
+    output_via = send(across, (2, 4))
     grads_one = lax.psum_scatter(
         second.reshape(-1, width), EXPERT, scatter_dimension=0, axis_index_groups=sides_of, tiled=True
     )
@@ -1110,9 +1111,11 @@
         (mine.astype(F32) + near[0].astype(F32) + near[1].astype(F32)).astype(BF)
         for mine, near in ((mine_low, near_low), (mine_high, near_high))], axis=0)
     outputs_zero = list(expert_outputs(outputs_zero))
+    grad_attn_gain = jnp.sum(terms_in.astype(F32) * tokens.astype(F32) * inverse_in, axis=0)
+    *came, terms_in, lows, grad_attn_gain, output_via[0], output_via[1] = join(
+        *came, terms_in, lows, grad_attn_gain, *output_via
+    )
     output_near = send(beside(output_grads, output_via), (4, 2))
-    grad_attn_gain = jnp.sum(terms_in.astype(F32) * tokens.astype(F32) * inverse_in, axis=0)
-    *came, terms_in, lows, grad_attn_gain = join(*came, terms_in, lows, grad_attn_gain)
     out_above, out_below = [from_above(came)], [from_below(came)]
     chunk = lambda place: lax.dynamic_slice_in_dim(terms_in, jnp.clip(place, 0, n_tensor - 1) * own_rows, own_rows, 0)
     sum_above = sum_below = jnp.zeros((), BF)
@@ -1231,9 +1234,15 @@
     everything = jnp.zeros((rows * size,) + values.shape[1:], values.dtype)
     everything = lax.dynamic_update_slice_in_dim(everything, values, place * rows, 0)
     for ahead in range(1, size):
-        piece = jnp.where(place + ahead < size, above[ahead - 1], below[size - ahead - 1])
+        whole_line = size - ahead - 1 == size - 2
+        after_end = below[0] if whole_line else below[size - ahead - 1]
+        before_end = above[0] if ahead == size - 1 else above[ahead - 1]
+        piece = jnp.where(place + ahead < size, before_end, after_end)
         everything = lax.dynamic_update_slice_in_dim(everything, piece, lax.rem(place + ahead, size) * rows, 0)
-    return everything
+    first, last = place == 0, place == size - 1
+    piece = jnp.where(first, above[-1], jnp.where(last, below[-1], values))
+    position = jnp.where(first, size - 1, jnp.where(last, 0, place))
+    return lax.dynamic_update_slice_in_dim(everything, piece, position * rows, 0)
 
 
 def exchange_doubling(values):

time: 852 us -> 854 us (level)
    ppermute x24, waiting for transfers between devices: 78.4 us -> 89.5 us  [swap(): return lax.ppermute(values, EXPERT, [(i, i ^ bit) for i in range(size)])]
    ppermute x7, waiting for transfers between devices: 24.7 us -> 15.8 us  [exchange(): lax.ppermute(jnp.where(even, to_below, to_above), TENSOR, [(1, 2), (2, 1)...]
    unnamed x211 -> x209, local copies, waits for them, and re-layouts: 35.7 us -> 40.4 us
  transfers between devices with their start and end apart: 62 -> 62, of which waited for: 33 -> 31; matrix products, arithmetic and copies ran while one was open for 14% -> 15% of each run, Pallas kernels for 37% -> 37%
where the time goes in v4:
time: 854 us; the launch traced here: 838 us
  Pallas kernels  310 us (36%)
  waiting for transfers between devices  257 us (30%)
  other arithmetic  81 us (9%)
  local copies, waits for them, and re-layouts  79 us (9%)
  starting transfers between devices  65 us (8%)
  matrix products  29.7 us (3%)
  between operations  16.1 us (2%)
    pallas_call x4, Pallas kernels, rows_call(): pl.pallas_call(functools.partial(rows_kernel, place, number_here, each_de...  157 us
    ppermute x24, waiting for transfers between devices, swap(): return lax.ppermute(values, EXPERT, [(i, i ^ bit) for i in range(size)])  89.5 us
    ppermute x12, waiting for transfers between devices, swap_tensor(): return lax.ppermute(values, TENSOR, [(i, i ^ bit) for i in range(size)])  88.9 us
    pallas_call x4, Pallas kernels, weight_grads_call(): pl.pallas_call(functools.partial(weight_grads_kernel, sides, halves, outs...  88.2 us
    unnamed x209, local copies, waits for them, and re-layouts  40.4 us
    ppermute x7, waiting for transfers between devices, exchange(): lax.ppermute(jnp.where(even, to_above, to_below), TENSOR, [(0, 1), (1, 0)...  37.1 us
    dot_general x6, matrix products, mul(): return lax.dot_general(left, right, dims, preferred_element_type=F32)  25 us
    ppermute x7, starting transfers between devices, exchange(): lax.ppermute(jnp.where(even, to_below, to_above), TENSOR, [(1, 2), (2, 1)...  20.2 us
  transfers between devices with their start and end apart: 62, of which 31 were waited for; matrix products, arithmetic and copies ran while one was open for 15% of the time, Pallas kernels for 37%

profile of v4, /device:TPU:20, one launch (start us, length us, event | category | flops | bytes accessed | tf_op | source)
XLA Modules:
  0.0 838.4 jit_solution(12681874164418614432)
XLA Ops:
  9.6 2.6 fusion.57
  14.5 2.8 slice_bitcast_fusion.4
  30.9 13.3 %front_rows.1 = (bf16[1024,2048]{1,0:T(8,128)(2,1)}, f32[1024,1]{1,0:T(8,128)}, f32[1024,512]{1,0:T(8,128)}, f32[1024,512]{1,0:T(8,128)}, bf16[1024,512]{1,0:T(8,128)(2,1)}, /*index=5*/f32[1024,2]{1,0:T(8,128)}) custom-call(bf16[1024,2048]{1,0:T(8,128)(2,1)} %tokens_ref.3, f32[1,2048]{1,0:T(1,128)} %bitcast.170, bf16[2048,512]{1,0:T(8,128)(2,1)} %wq_ref.1, ...), custom_call_target="tpu_custom_call" | custom-call | flops 6442450944 | bytes 14680064 | tf_op jit(solution)/shard_map/front_rows/pallas_call | solution.py:451
  52.4 18.6 %collective-permute-done = f32[16,128]{1,0:T(8,128)S(1)} collective-permute-done((f32[16,128]{1,0:T(8,128)S(1)}, f32[16,128]{1,0:T(8,128)S(1)}, u32[]{:S(2)}, u32[]{:S(2)}) %collective-permute-start) | collective-permute-done | bytes 8224 | tf_op jit(solution)/shard_map/ppermute | solution.py:1297
  74.7 15.4 %attention_rows.1 = (bf16[1024,512]{1,0:T(8,128)(2,1)}, bf16[1024,512]{1,0:T(8,128)(2,1)}, bf16[1024,512]{1,0:T(8,128)(2,1)}, f32[4,1024,1]{2,1,0:T(8,128)}) custom-call(f32[1024,512]{1,0:T(8,128)} %get-tuple-element.153.q_ref, f32[1024,512]{1,0:T(8,128)} %get-tuple-element.154.k_ref, bf16[1024,512]{1,0:T(8,128)(2,1)} %get-tuple-element.155.v_ref, ...), custom_call_target="tpu_custom_call" | custom-call | flops 1073741824 | bytes 6291456 | tf_op jit(solution)/shard_map/attention_rows/pallas_call | solution.py:540
  92.1 29.0 %collective-permute-done.5 = bf16[256,2048]{1,0:T(8,128)(2,1)S(1)} collective-permute-done((bf16[256,2048]{1,0:T(8,128)(2,1)}, bf16[256,2048]{1,0:T(8,128)(2,1)S(1)}, u32[]{:S(2)}, u32[]{:S(2)}) %collective-permute-start.5) | collective-permute-done | bytes 1048608 | tf_op jit(solution)/shard_map/ppermute | solution.py:1195
  121.2 20.3 %collective-permute-done.6.refs_1_ = bf16[1024,512]{1,0:T(8,128)(2,1)S(1)} collective-permute-done((bf16[1024,512]{1,0:T(8,128)(2,1)}, bf16[1024,512]{1,0:T(8,128)(2,1)S(1)}, u32[]{:S(2)}, u32[]{:S(2)}) %collective-permute-start.6) | collective-permute-done | bytes 1048608 | tf_op jit(solution)/shard_map/ppermute | solution.py:1195
  149.5 24.2 %collective-permute-done.9.refs_3_ = bf16[1024,512]{1,0:T(8,128)(2,1)S(1)} collective-permute-done((bf16[1024,512]{1,0:T(8,128)(2,1)S(1)}, bf16[1024,512]{1,0:T(8,128)(2,1)S(1)}, u32[]{:S(2)}, u32[]{:S(2)}) %collective-permute-start.9) | collective-permute-done | bytes 1048608 | tf_op jit(solution)/shard_map/ppermute | solution.py:1195
  174.8 17.0 %hidden_rows.1 = (f32[256,2048]{1,0:T(8,128)}, bf16[1024,2048]{1,0:T(8,128)(2,1)}, f32[256,1]{1,0:T(8,128)}) custom-call(s32[2]{0:T(128)} %pad_add_fusion.core_ref, bf16[1024,2048]{1,0:T(8,128)(2,1)} %tokens_ref.3, f32[1,2048]{1,0:T(1,128)} %bitcast.161, bf16[1024,512]{1,0:T(8,128)(2,1)} %get-tuple-element.159.refs_0_.ctx_ref, bf16[1024,512]{1,0:T(8,128)(2,1)} %copy-done.73, ...), custom_call_target="tpu_custom_call" | custom-call | flops 8589934592 | bytes 29360128 | tf_op jit(solution)/shard_map/hidden_rows/pallas_call | solution.py:607
  194.9 2.7 collective-permute-done.12
  199.5 38.0 %expert_rows.4 = (bf16[512,2048]{1,0:T(8,128)(2,1)}, bf16[512,2048]{1,0:T(8,128)(2,1)}, bf16[512,2176]{1,0:T(8,128)(2,1)}, bf16[512,2176]{1,0:T(8,128)(2,1)}, bf...) custom-call(s32[1]{0:T(128)} %bitcast.refs_0_, bf16[2048,16]{1,0:T(8,128)(2,1)} %copy.180.refs_1_, ...), custom_call_target="tpu_custom_call" | custom-call | flops 25769803776 | bytes 16777216 | tf_op jit(solution)/shard_map/expert_rows/pallas_call | solution.py:760
  237.5 38.4 %expert_rows.5 = (bf16[512,2048]{1,0:T(8,128)(2,1)}, bf16[512,2048]{1,0:T(8,128)(2,1)}, bf16[512,2176]{1,0:T(8,128)(2,1)}, bf16[512,2176]{1,0:T(8,128)(2,1)}, bf...) custom-call(s32[1]{0:T(128)} %bitcast.refs_0_, bf16[2048,16]{1,0:T(8,128)(2,1)} %copy.180.refs_1_, ...), custom_call_target="tpu_custom_call" | custom-call | flops 25769803776 | bytes 16777216 | tf_op jit(solution)/shard_map/expert_rows/pallas_call | solution.py:760
  276.0 21.9 %expert_weight_grads.4 = (bf16[384,2048]{1,0:T(8,128)(2,1)}, bf16[384,2048]{1,0:T(8,128)(2,1)}, bf16[384,2048]{1,0:T(8,128)(2,1)}, bf16[384,2048]{1,0:T(8,128)(2,1)}) custom-call(s32[2]{0:T(128)} %pad_add_fusion.1.order_ref, bf16[4,2,128,2048]{3,2,1,0:T(8,128)(2,1)} %bitcast.128, bf16[4,2,128,2048]{3,2,1,0:T(8,128)(2,1)} %bitcast.26.refs_3_.refs_1_, ...), custom_call_target="tpu_custom_call" | custom-call | flops 12884901888 | bytes 29360128 | tf_op jit(solution)/shard_map/expert_weight_grads/pallas_call | solution.py:862
  300.0 40.4 %expert_rows.6 = (bf16[512,2048]{1,0:T(8,128)(2,1)}, bf16[512,2048]{1,0:T(8,128)(2,1)}, bf16[512,2176]{1,0:T(8,128)(2,1)}, bf16[512,2176]{1,0:T(8,128)(2,1)}, bf...) custom-call(s32[1]{0:T(128)} %bitcast.refs_0_, bf16[2048,16]{1,0:T(8,128)(2,1)} %copy.180.refs_1_, ...), custom_call_target="tpu_custom_call" | custom-call | flops 25769803776 | bytes 16777216 | tf_op jit(solution)/shard_map/expert_rows/pallas_call | solution.py:760
  340.5 4.5 collective-permute-done.15
  345.0 3.5 add_convert_fusion.3.refs_13_
  348.8 40.6 %expert_rows.7 = (bf16[512,2048]{1,0:T(8,128)(2,1)}, bf16[512,2048]{1,0:T(8,128)(2,1)}, bf16[512,2176]{1,0:T(8,128)(2,1)}, bf16[512,2176]{1,0:T(8,128)(2,1)}, bf...) custom-call(s32[1]{0:T(128)} %bitcast.refs_0_, bf16[2048,16]{1,0:T(8,128)(2,1)} %copy.180.refs_1_, ...), custom_call_target="tpu_custom_call" | custom-call | flops 25769803776 | bytes 16777216 | tf_op jit(solution)/shard_map/expert_rows/pallas_call | solution.py:760
  389.4 4.7 reduce-scatter.5.cloned.1.call-done
  394.1 4.6 collective-permute-done.16
  398.6 3.5 add_convert_fusion.2.refs_18_
  409.5 22.0 %expert_weight_grads.5 = (bf16[384,2048]{1,0:T(8,128)(2,1)}, bf16[384,2048]{1,0:T(8,128)(2,1)}, bf16[384,2048]{1,0:T(8,128)(2,1)}, bf16[384,2048]{1,0:T(8,128)(2,1)}) custom-call(s32[2]{0:T(128)} %pad_add_fusion.2.order_ref, bf16[4,2,128,2048]{3,2,1,0:T(8,128)(2,1)} %bitcast.132, bf16[4,2,128,2048]{3,2,1,0:T(8,128)(2,1)} %bitcast.26.refs_3_.refs_1_, ...), custom_call_target="tpu_custom_call" | custom-call | flops 12884901888 | bytes 29360128 | tf_op jit(solution)/shard_map/expert_weight_grads/pallas_call | solution.py:862
  432.1 22.1 %expert_weight_grads.6.refs_16_ = bf16[4,768,2048]{2,1,0:T(8,128)(2,1)} custom-call(s32[2]{0:T(128)} %iota.29.order_ref, bf16[4,2,128,2048]{3,2,1,0:T(8,128)(2,1)} %bitcast.134, bf16[4,2,128,2048]{3,2,1,0:T(8,128)(2,1)} %bitcast.26.refs_3_.refs_1_, bf16[4,2,128,2048]{3,2,1,0:T(8,128)(2,1)} %bitcast.135, bf16[4,2,128,2048]{3,2,1,0:T(8,128)(2,1)} %bitcast.26.refs_3_.refs_1_, ...), custom_call_target="tpu_custom_call" | custom-call | flops 12884901888 | bytes 29360128 | tf_op jit(solution)/shard_map/expert_weight_grads/pallas_call | solution.py:862
  455.5 3.3 multiply_reduce_fusion.1
  460.2 3.5 fusion.52
  464.7 3.1 convolution_convert_fusion.2
  470.2 3.0 collective-permute-start.18
  476.9 2.4 convolution_convert_fusion.1
  479.3 4.2 fusion.53
  486.2 4.2 collective-permute-done.17
  490.4 2.8 collective-permute-done.18
  496.0 2.4 pad_maximum_fusion
  502.7 18.7 %attention_rows_back.1 = (f32[1024,512]{1,0:T(8,128)}, f32[1024,512]{1,0:T(8,128)}, bf16[1024,512]{1,0:T(8,128)(2,1)}, f32[4,1024,2]{2,1,0:T(8,128)}, f32[1,512]{1,0:T(1,128)}, /*index=5*/f32[1,512]{1,0:T(1,128)}) custom-call(f32[1024,512]{1,0:T(8,128)} %get-tuple-element.153.q_ref, f32[1024,512]{1,0:T(8,128)} %get-tuple-element.154.k_ref, ...), custom_call_target="tpu_custom_call" | custom-call | flops 4294967296 | bytes 12582912 | tf_op jit(solution)/shard_map/attention_rows_back/pallas_call | solution.py:558
  521.4 14.7 %collective-permute-done.23 = bf16[384,2048]{1,0:T(8,128)(2,1)S(1)} collective-permute-done((bf16[384,2048]{1,0:T(8,128)(2,1)}, bf16[384,2048]{1,0:T(8,128)(2,1)S(1)}, u32[]{:S(2)}, u32[]{:S(2)}) %collective-permute-start.23) | collective-permute-done | bytes 1572896 | tf_op jit(solution)/shard_map/ppermute | solution.py:885
  538.8 3.7 collective-permute-start.25
  542.5 2.6 collective-permute-start.27
  545.1 5.4 add_convert_fusion
  554.5 22.2 %expert_weight_grads.7 = bf16[4,768,2048]{2,1,0:T(8,128)(2,1)} custom-call(s32[2]{0:T(128)} %constant.101.clone.1.order_ref, bf16[4,2,128,2048]{3,2,1,0:T(8,128)(2,1)} %bitcast.136, bf16[4,2,128,2048]{3,2,1,0:T(8,128)(2,1)} %bitcast.26.refs_3_.refs_1_, bf16[4,2,128,2048]{3,2,1,0:T(8,128)(2,1)} %bitcast.137, ...), custom_call_target="tpu_custom_call", output_to_operand_aliasing={{}: (17, {})} | custom-call | flops 12884901888 | bytes 29360128 | tf_op jit(solution)/shard_map/expert_weight_grads/pallas_call | solution.py:862
  576.8 2.7 reduce-scatter.9.cloned.1.call-done
  594.5 10.2 %multiply_reduce_fusion = (bf16[2048]{0:T(1024)(128)(2,1)S(1)}, bf16[1024,2048]{1,0:T(8,128)(2,1)}) fusion(bf16[1024,2048]{1,0:T(8,128)(2,1)S(1)} %copy-done.39, f32[1024]{0:T(1024)S(1)} %reduce.2, bf16[2048,512]{1,0:T(8,128)(2,1)} %wv_ref.1, bf16[2048,512]{1,0:T(8,128)(2,1)} %wk_ref.1, bf16[2048,512]{1,0:T(8,128)(2,1)} %wq_ref.1, ...), kind=kOutput, calls=%fused_computation | convolution fusion | flops 6483343360 | bytes 17833984 | tf_op jit(solution)/shard_map/dot_general | solution.py:402
  606.4 4.3 collective-permute-done.32
  610.7 2.7 collective-permute-done.33
  615.0 3.2 broadcast_select_fusion.16
  620.2 3.9 collective-permute-start.35
  624.2 7.6 convolution_convert_fusion
  632.6 10.9 %collective-permute-done.34 = bf16[256,2048]{1,0:T(8,128)(2,1)S(1)} collective-permute-done((bf16[256,2048]{1,0:T(8,128)(2,1)S(1)}, bf16[256,2048]{1,0:T(8,128)(2,1)S(1)}, u32[]{:S(2)}, u32[]{:S(2)}) %collective-permute-start.34) | collective-permute-done | bytes 1048608 | tf_op jit(solution)/shard_map/ppermute | solution.py:1217
  645.9 2.4 add_convert_fusion.7
  648.2 3.3 add_convert_fusion.6
  653.4 3.7 collective-permute-start.37
  659.7 19.1 %collective-permute-done.36 = bf16[256,2048]{1,0:T(8,128)(2,1)S(1)} collective-permute-done((bf16[256,2048]{1,0:T(8,128)(2,1)S(1)}, bf16[256,2048]{1,0:T(8,128)(2,1)S(1)}, u32[]{:S(2)}, u32[]{:S(2)}) %collective-permute-start.36) | collective-permute-done | bytes 1048608 | tf_op jit(solution)/shard_map/ppermute | solution.py:1217
  684.5 3.5 collective-permute-start.40
  692.5 18.4 %collective-permute-done.41 = bf16[128,1664]{1,0:T(8,128)(2,1)S(1)} collective-permute-done((bf16[128,1664]{1,0:T(8,128)(2,1)S(1)}, bf16[128,1664]{1,0:T(8,128)(2,1)S(1)}, u32[]{:S(2)}, u32[]{:S(2)}) %collective-permute-start.41) | collective-permute-done | bytes 426016 | tf_op jit(solution)/shard_map/ppermute | solution.py:885
  715.9 2.8 constant_dynamic-update-slice_fusion.5
  722.6 20.5 %collective-permute-done.46 = bf16[256,2048]{1,0:T(8,128)(2,1)S(1)} collective-permute-done((bf16[256,2048]{1,0:T(8,128)(2,1)S(1)}, bf16[256,2048]{1,0:T(8,128)(2,1)S(1)}, u32[]{:S(2)}, u32[]{:S(2)}) %collective-permute-start.46) | collective-permute-done | bytes 1048608 | tf_op jit(solution)/shard_map/ppermute | solution.py:885
  751.9 8.9 %collective-permute-done.50 = bf16[256,1664]{1,0:T(8,128)(2,1)S(1)} collective-permute-done((bf16[256,1664]{1,0:T(8,128)(2,1)S(1)}, bf16[256,1664]{1,0:T(8,128)(2,1)S(1)}, u32[]{:S(2)}, u32[]{:S(2)}) %collective-permute-start.50) | collective-permute-done | bytes 852000 | tf_op jit(solution)/shard_map/ppermute | solution.py:885
  760.8 6.4 collective-permute-done.49
  771.3 3.4 slice_bitcast_fusion.1
  779.4 3.6 broadcast_select_fusion.1
  785.3 2.4 collective-permute-start.52
  791.0 2.5 copy.192
  793.5 4.1 copy.191
  801.2 7.4 collective-permute-done.55
  813.9 6.2 collective-permute-done.51
  820.1 8.2 collective-permute-done.52
  828.3 3.1 select_dynamic-update-slice_fusion
  (424 shorter events, 161.0 us)
Async XLA Ops:
  7.2 192.3 %all-gather.7.cloned.1.call-start = ((), (), s32[]{:S(2)}) async-start(), calls=%async_computation.9 | async-start | bytes 15728640 | tf_op jit(solution)/shard_map/all_gather | solution.py:957
  19.2 280.8 %all-gather.5.cloned.1.call-start = ((), (), s32[]{:S(2)}) async-start(), calls=%async_computation.8 | async-start | bytes 15728640 | tf_op jit(solution)/shard_map/all_gather | solution.py:957
  21.6 49.5 %collective-permute-start.3 = (bf16[256,2048]{1,0:T(8,128)(2,1)}, bf16[256,2048]{1,0:T(8,128)(2,1)}, u32[]{:S(2)}, u32[]{:S(2)}) collective-permute-start(bf16[256,2048]{1,0:T(8,128)(2,1)} %constant_dynamic-slice_fusion.6), channel_id=1, source_target_pairs={{0,1},{1,0},{2,3},{3,2},{4,5},{5,4},{6,7},{7,6},{8,9},{9,8},{10,11... | collective-permute-start | bytes 3145736 | tf_op jit(solution)/shard_map/ppermute | solution.py:1195
  23.2 47.9 %collective-permute-start.4 = (bf16[256,2048]{1,0:T(8,128)(2,1)}, bf16[256,2048]{1,0:T(8,128)(2,1)}, u32[]{:S(2)}, u32[]{:S(2)}) collective-permute-start(bf16[256,2048]{1,0:T(8,128)(2,1)} %constant_dynamic-slice_fusion.6), channel_id=1, source_target_pairs={{0,2},{1,3},{2,0},{3,1},{4,6},{5,7},{6,4},{7,5},{8,10},{9,11},{10,... | collective-permute-start | bytes 3145736 | tf_op jit(solution)/shard_map/ppermute | solution.py:1195
  45.5 25.5 %collective-permute-start = (f32[16,128]{1,0:T(8,128)S(1)}, f32[16,128]{1,0:T(8,128)S(1)}, u32[]{:S(2)}, u32[]{:S(2)}) collective-permute-start(f32[16,128]{1,0:T(8,128)S(1)} %reshape.249), channel_id=1, source_target_pairs={{0,1},{1,2},{2,3},{3,0},{4,5},{5,6},{6,7},{7,4},{8,9},{9,10},{10,1... | collective-permute-start | bytes 24584 | tf_op jit(solution)/shard_map/ppermute | solution.py:1297
  46.0 25.0 %collective-permute-start.1 = (f32[16,128]{1,0:T(8,128)S(1)}, f32[16,128]{1,0:T(8,128)S(1)}, u32[]{:S(2)}, u32[]{:S(2)}) collective-permute-start(f32[16,128]{1,0:T(8,128)S(1)} %reshape.249), channel_id=1, source_target_pairs={{0,2},{1,3},{2,0},{3,1},{4,6},{5,7},{6,4},{7,5},{8,10},{9,11},{10,... | collective-permute-start | bytes 24584 | tf_op jit(solution)/shard_map/ppermute | solution.py:1297
  48.4 22.6 %collective-permute-start.2 = (f32[16,128]{1,0:T(8,128)S(1)}, f32[16,128]{1,0:T(8,128)S(1)}, u32[]{:S(2)}, u32[]{:S(2)}) collective-permute-start(f32[16,128]{1,0:T(8,128)S(1)} %reshape.249), channel_id=1, source_target_pairs={{0,3},{1,0},{2,1},{3,2},{4,7},{5,4},{6,5},{7,6},{8,11},{9,8},{10,9... | collective-permute-start | bytes 24584 | tf_op jit(solution)/shard_map/ppermute | solution.py:1297
  73.2 47.9 %collective-permute-start.5 = (bf16[256,2048]{1,0:T(8,128)(2,1)}, bf16[256,2048]{1,0:T(8,128)(2,1)S(1)}, u32[]{:S(2)}, u32[]{:S(2)}) collective-permute-start(bf16[256,2048]{1,0:T(8,128)(2,1)} %collective-permute-done.4), channel_id=1, source_target_pairs={{0,1},{1,0},{2,3},{3,2},{4,5},{5,4},{6,7},{7,6},{8,9},{9,8},{10,11... | collective-permute-start | bytes 3145736 | tf_op jit(solution)/shard_map/ppermute | solution.py:1195
  90.2 51.3 %collective-permute-start.6 = (bf16[1024,512]{1,0:T(8,128)(2,1)}, bf16[1024,512]{1,0:T(8,128)(2,1)S(1)}, u32[]{:S(2)}, u32[]{:S(2)}) collective-permute-start(bf16[1024,512]{1,0:T(8,128)(2,1)} %get-tuple-element.159.refs_0_.ctx_ref), channel_id=1, source_target_pairs={{0,1},{1,0},{2,3},{3,2},{4,5},{5,4},{6,7},{7,6},{8,9},{9,8},{10,11... | collective-permute-start | bytes 3145736 | tf_op jit(solution)/shard_map/ppermute | solution.py:1195
  91.0 52.4 %collective-permute-start.7 = (bf16[1024,512]{1,0:T(8,128)(2,1)}, bf16[1024,512]{1,0:T(8,128)(2,1)S(1)}, u32[]{:S(2)}, u32[]{:S(2)}) collective-permute-start(bf16[1024,512]{1,0:T(8,128)(2,1)} %get-tuple-element.159.refs_0_.ctx_ref), channel_id=1, source_target_pairs={{0,2},{1,3},{2,0},{3,1},{4,6},{5,7},{6,4},{7,5},{8,10},{9,11},{10,... | collective-permute-start | bytes 3145736 | tf_op jit(solution)/shard_map/ppermute | solution.py:1195
  146.4 28.1 %copy-start.80 = (s32[1024,8]{0,1:T(8,128)S(1)}, s32[1024,8]{0,1:T(8,128)}, u32[]{:S(2)}) copy-start(s32[1024,8]{0,1:T(8,128)} %param.21) | copy-start | bytes 98308
  146.4 28.1 %copy-start.81 = (s32[1024,8]{0,1:T(8,128)S(1)}, s32[1024,8]{0,1:T(8,128)}, u32[]{:S(2)}) copy-start(s32[1024,8]{0,1:T(8,128)} %param.20) | copy-start | bytes 98308
  148.1 25.6 %collective-permute-start.8 = (bf16[768,2048]{1,0:T(8,128)(2,1)S(1)}, bf16[768,2048]{1,0:T(8,128)(2,1)}, u32[]{:S(2)}, u32[]{:S(2)}) collective-permute-start(bf16[768,2048]{1,0:T(8,128)(2,1)S(1)} %constant_dynamic-update-slice_fusion.refs_5_), channel_id=1, source_target_pairs={{0,4},{4,0},{8,12},{12,8},{16,20},{20,16},{24,28},{28,24},{1,5},{5... | collective-permute-start | bytes 9437192 | tf_op jit(solution)/shard_map/ppermute | solution.py:885
  148.1 25.6 %collective-permute-start.9 = (bf16[1024,512]{1,0:T(8,128)(2,1)S(1)}, bf16[1024,512]{1,0:T(8,128)(2,1)S(1)}, u32[]{:S(2)}, u32[]{:S(2)}) collective-permute-start(bf16[1024,512]{1,0:T(8,128)(2,1)S(1)} %collective-permute-done.7.refs_2_), channel_id=1, source_target_pairs={{0,1},{1,0},{2,3},{3,2},{4,5},{5,4},{6,7},{7,6},{8,9},{9,8},{10,11... | collective-permute-start | bytes 3145736 | tf_op jit(solution)/shard_map/ppermute | solution.py:1195
  173.7 220.3 %reduce-scatter.5.cloned.1.call-start = ((), (), s32[]{:S(2)}) async-start(), calls=%async_computation.4 | async-start | bytes 2785280 | tf_op jit(solution)/shard_map/reduce_scatter | solution.py:922
  174.7 23.8 %collective-permute-start.11 = (bf16[1024,2048]{1,0:T(8,128)(2,1)}, bf16[1024,2048]{1,0:T(8,128)(2,1)}, u32[]{:S(2)}, u32[]{:S(2)}) collective-permute-start(bf16[1024,2048]{1,0:T(8,128)(2,1)} %param.18), channel_id=1, source_target_pairs={{0,4},{4,0},{8,12},{12,8},{16,20},{20,16},{24,28},{28,24},{1,5},{5... | collective-permute-start | bytes 12582920 | tf_op jit(solution)/shard_map/ppermute | solution.py:885
  191.8 7.7 collective-permute-start.10
  192.3 5.3 collective-permute-start.12
  297.9 42.5 %collective-permute-start.13 = (bf16[384,2048]{1,0:T(8,128)(2,1)}, bf16[384,2048]{1,0:T(8,128)(2,1)S(1)}, u32[]{:S(2)}, u32[]{:S(2)}) collective-permute-start(bf16[384,2048]{1,0:T(8,128)(2,1)} %get-tuple-element.188.refs_13_), channel_id=1, source_target_pairs={{0,8},{4,12},{8,0},{12,4},{16,24},{20,28},{24,16},{28,20},{1,9},{5... | collective-permute-start | bytes 4718600 | tf_op jit(solution)/shard_map/ppermute | solution.py:885
  299.5 41.0 %collective-permute-start.14 = (bf16[384,2048]{1,0:T(8,128)(2,1)}, bf16[384,2048]{1,0:T(8,128)(2,1)}, u32[]{:S(2)}, u32[]{:S(2)}) collective-permute-start(bf16[384,2048]{1,0:T(8,128)(2,1)} %get-tuple-element.189.refs_14_), channel_id=1, source_target_pairs={{0,16},{4,20},{8,24},{12,28},{16,0},{20,4},{24,8},{28,12},{1,17},{... | collective-permute-start | bytes 4718600 | tf_op jit(solution)/shard_map/ppermute | solution.py:885
  340.4 4.6 collective-permute-start.15
  348.6 105.6 %reduce-scatter.7.cloned.1.call-start = ((), (), s32[]{:S(2)}) async-start(), calls=%async_computation.5 | async-start | bytes 2785280 | tf_op jit(solution)/shard_map/reduce_scatter | solution.py:922
  394.1 4.6 collective-permute-start.16
  402.2 177.3 %reduce-scatter.9.cloned.1.call-start = ((), (), s32[]{:S(2)}) async-start(), calls=%async_computation.6 | async-start | bytes 5242880 | tf_op jit(solution)/shard_map/reduce_scatter | solution.py:922
  469.5 23.8 %collective-permute-start.20 = (bf16[512,2048]{1,0:T(8,128)(2,1)S(1)}, bf16[512,2048]{1,0:T(8,128)(2,1)S(1)}, u32[]{:S(2)}, u32[]{:S(2)}) collective-permute-start(bf16[512,2048]{1,0:T(8,128)(2,1)S(1)} %copy-done.84), channel_id=1, source_target_pairs={{0,4},{4,0},{8,12},{12,8},{16,20},{20,16},{24,28},{28,24},{1,5},{5... | collective-permute-start | bytes 6291464 | tf_op jit(solution)/shard_map/ppermute | solution.py:885
  469.7 24.6 %collective-permute-start.21 = (bf16[512,2048]{1,0:T(8,128)(2,1)}, bf16[512,2048]{1,0:T(8,128)(2,1)S(1)}, u32[]{:S(2)}, u32[]{:S(2)}) collective-permute-start(bf16[512,2048]{1,0:T(8,128)(2,1)} %get-tuple-element.221), channel_id=1, source_target_pairs={{0,4},{4,0},{8,12},{12,8},{16,20},{20,16},{24,28},{28,24},{1,5},{5... | collective-permute-start | bytes 6291464 | tf_op jit(solution)/shard_map/ppermute | solution.py:885
  470.1 23.1 %collective-permute-start.19 = (bf16[256,512]{1,0:T(8,128)(2,1)S(1)}, bf16[256,512]{1,0:T(8,128)(2,1)S(1)}, u32[]{:S(2)}, u32[]{:S(2)}) collective-permute-start(bf16[256,512]{1,0:T(8,128)(2,1)S(1)} %pad_maximum_fusion.20), channel_id=1, source_target_pairs={{0,3},{1,2},{2,1},{3,0},{4,7},{5,6},{6,5},{7,4},{8,11},{9,10},{10,... | collective-permute-start | bytes 786440 | tf_op jit(solution)/shard_map/ppermute | solution.py:1195
  470.2 23.0 %collective-permute-start.18 = (bf16[256,512]{1,0:T(8,128)(2,1)S(1)}, bf16[256,512]{1,0:T(8,128)(2,1)S(1)}, u32[]{:S(2)}, u32[]{:S(2)}) collective-permute-start(bf16[256,512]{1,0:T(8,128)(2,1)S(1)} %pad_maximum_fusion.19), channel_id=1, source_target_pairs={{0,2},{1,3},{2,0},{3,1},{4,6},{5,7},{6,4},{7,5},{8,10},{9,11},{10,... | collective-permute-start | bytes 786440 | tf_op jit(solution)/shard_map/ppermute | solution.py:1195
  473.2 17.2 %collective-permute-start.17 = (bf16[256,512]{1,0:T(8,128)(2,1)S(1)}, bf16[256,512]{1,0:T(8,128)(2,1)S(1)}, u32[]{:S(2)}, u32[]{:S(2)}) collective-permute-start(bf16[256,512]{1,0:T(8,128)(2,1)S(1)} %pad_maximum_fusion.18), channel_id=1, source_target_pairs={{0,1},{1,0},{2,3},{3,2},{4,5},{5,4},{6,7},{7,6},{8,9},{9,8},{10,11... | collective-permute-start | bytes 786440 | tf_op jit(solution)/shard_map/ppermute | solution.py:1195
  498.5 272.8 %reduce-scatter.11.cloned.1.call-start = ((), (), s32[]{:S(2)}) async-start(), calls=%async_computation.7 | async-start | bytes 15728640 | tf_op jit(solution)/shard_map/reduce_scatter | solution.py:1093
  498.5 38.3 %collective-permute-start.22 = (bf16[1024,2048]{1,0:T(8,128)(2,1)}, bf16[1024,2048]{1,0:T(8,128)(2,1)}, u32[]{:S(2)}, u32[]{:S(2)}) collective-permute-start(bf16[1024,2048]{1,0:T(8,128)(2,1)} %get-tuple-element.224.rest_0_), channel_id=1, source_target_pairs={{0,4},{4,0},{8,12},{12,8},{16,20},{20,16},{24,28},{28,24},{1,5},{5... | collective-permute-start | bytes 12582920 | tf_op jit(solution)/shard_map/ppermute | solution.py:885
  498.6 37.5 %collective-permute-start.23 = (bf16[384,2048]{1,0:T(8,128)(2,1)}, bf16[384,2048]{1,0:T(8,128)(2,1)S(1)}, u32[]{:S(2)}, u32[]{:S(2)}) collective-permute-start(bf16[384,2048]{1,0:T(8,128)(2,1)} %get-tuple-element.211.refs_16_), channel_id=1, source_target_pairs={{0,16},{4,20},{8,24},{12,28},{16,0},{20,4},{24,8},{28,12},{1,17},{... | collective-permute-start | bytes 4718600 | tf_op jit(solution)/shard_map/ppermute | solution.py:885
  499.2 37.6 %collective-permute-start.24 = (bf16[384,2048]{1,0:T(8,128)(2,1)}, bf16[384,2048]{1,0:T(8,128)(2,1)}, u32[]{:S(2)}, u32[]{:S(2)}) collective-permute-start(bf16[384,2048]{1,0:T(8,128)(2,1)} %get-tuple-element.231), channel_id=1, source_target_pairs={{0,8},{4,12},{8,0},{12,4},{16,24},{20,28},{24,16},{28,20},{1,9},{5... | collective-permute-start | bytes 4718600 | tf_op jit(solution)/shard_map/ppermute | solution.py:885
  500.7 76.1 %collective-permute-start.28 = (bf16[384,2048]{1,0:T(8,128)(2,1)}, bf16[384,2048]{1,0:T(8,128)(2,1)}, u32[]{:S(2)}, u32[]{:S(2)}) collective-permute-start(bf16[384,2048]{1,0:T(8,128)(2,1)} %get-tuple-element.235), channel_id=1, source_target_pairs={{0,16},{4,20},{8,24},{12,28},{16,0},{20,4},{24,8},{28,12},{1,17},{... | collective-permute-start | bytes 4718600 | tf_op jit(solution)/shard_map/ppermute | solution.py:885
  502.2 74.6 %collective-permute-start.29 = (bf16[384,2048]{1,0:T(8,128)(2,1)}, bf16[384,2048]{1,0:T(8,128)(2,1)}, u32[]{:S(2)}, u32[]{:S(2)}) collective-permute-start(bf16[384,2048]{1,0:T(8,128)(2,1)} %get-tuple-element.236), channel_id=1, source_target_pairs={{0,8},{4,12},{8,0},{12,4},{16,24},{20,28},{24,16},{28,20},{1,9},{5... | collective-permute-start | bytes 4718600 | tf_op jit(solution)/shard_map/ppermute | solution.py:885
  538.8 15.1 %collective-permute-start.25 = (f32[16,128]{1,0:T(8,128)S(1)}, f32[16,128]{1,0:T(8,128)S(1)}, u32[]{:S(2)}, u32[]{:S(2)}) collective-permute-start(f32[16,128]{1,0:T(8,128)S(1)} %reshape.258), channel_id=1, source_target_pairs={{0,1},{1,2},{2,3},{3,0},{4,5},{5,6},{6,7},{7,4},{8,9},{9,10},{10,1... | collective-permute-start | bytes 24584 | tf_op jit(solution)/shard_map/ppermute | solution.py:1297
  542.5 11.4 %collective-permute-start.26 = (f32[16,128]{1,0:T(8,128)S(1)}, f32[16,128]{1,0:T(8,128)S(1)}, u32[]{:S(2)}, u32[]{:S(2)}) collective-permute-start(f32[16,128]{1,0:T(8,128)S(1)} %reshape.258), channel_id=1, source_target_pairs={{0,2},{1,3},{2,0},{3,1},{4,6},{5,7},{6,4},{7,5},{8,10},{9,11},{10,... | collective-permute-start | bytes 24584 | tf_op jit(solution)/shard_map/ppermute | solution.py:1297
  542.5 11.4 %collective-permute-start.27 = (f32[16,128]{1,0:T(8,128)S(1)}, f32[16,128]{1,0:T(8,128)S(1)}, u32[]{:S(2)}, u32[]{:S(2)}) collective-permute-start(f32[16,128]{1,0:T(8,128)S(1)} %reshape.258), channel_id=1, source_target_pairs={{0,3},{1,0},{2,1},{3,2},{4,7},{5,4},{6,5},{7,6},{8,11},{9,8},{10,9... | collective-permute-start | bytes 24584 | tf_op jit(solution)/shard_map/ppermute | solution.py:1297
  584.1 29.4 %collective-permute-start.30 = (bf16[256,2048]{1,0:T(8,128)(2,1)S(1)}, bf16[256,2048]{1,0:T(8,128)(2,1)S(1)}, u32[]{:S(2)}, u32[]{:S(2)}) collective-permute-start(bf16[256,2048]{1,0:T(8,128)(2,1)S(1)} %get-tuple-element.400), channel_id=1, source_target_pairs={{0,1},{1,0},{2,3},{3,2},{4,5},{5,4},{6,7},{7,6},{8,9},{9,8},{10,11... | collective-permute-start | bytes 3145736 | tf_op jit(solution)/shard_map/ppermute | solution.py:1217
  584.6 28.9 %collective-permute-start.31 = (bf16[256,2048]{1,0:T(8,128)(2,1)S(1)}, bf16[256,2048]{1,0:T(8,128)(2,1)S(1)}, u32[]{:S(2)}, u32[]{:S(2)}) collective-permute-start(bf16[256,2048]{1,0:T(8,128)(2,1)S(1)} %get-tuple-element.400), channel_id=1, source_target_pairs={{1,2},{2,1},{0,0},{3,3},{5,6},{6,5},{4,4},{7,7},{9,10},{10,9},{8,8... | collective-permute-start | bytes 3145736 | tf_op jit(solution)/shard_map/ppermute | solution.py:1218
  586.6 24.1 %collective-permute-start.32 = (bf16[128,2048]{1,0:T(8,128)(2,1)}, bf16[128,2048]{1,0:T(8,128)(2,1)S(1)}, u32[]{:S(2)}, u32[]{:S(2)}) collective-permute-start(bf16[128,2048]{1,0:T(8,128)(2,1)} %get-tuple-element.245), channel_id=1, source_target_pairs={{0,8},{4,12},{8,0},{12,4},{16,24},{20,28},{24,16},{28,20},{1,9},{5... | collective-permute-start | bytes 1572872 | tf_op jit(solution)/shard_map/ppermute | solution.py:885
  588.2 25.3 %collective-permute-start.33 = (bf16[128,2048]{1,0:T(8,128)(2,1)}, bf16[128,2048]{1,0:T(8,128)(2,1)S(1)}, u32[]{:S(2)}, u32[]{:S(2)}) collective-permute-start(bf16[128,2048]{1,0:T(8,128)(2,1)} %get-tuple-element.246), channel_id=1, source_target_pairs={{0,16},{4,20},{8,24},{12,28},{16,0},{20,4},{24,8},{28,12},{1,17},{... | collective-permute-start | bytes 1572872 | tf_op jit(solution)/shard_map/ppermute | solution.py:885
  620.2 23.3 %collective-permute-start.34 = (bf16[256,2048]{1,0:T(8,128)(2,1)S(1)}, bf16[256,2048]{1,0:T(8,128)(2,1)S(1)}, u32[]{:S(2)}, u32[]{:S(2)}) collective-permute-start(bf16[256,2048]{1,0:T(8,128)(2,1)S(1)} %get-tuple-element.429), channel_id=1, source_target_pairs={{0,1},{1,0},{2,3},{3,2},{4,5},{5,4},{6,7},{7,6},{8,9},{9,8},{10,11... | collective-permute-start | bytes 3145736 | tf_op jit(solution)/shard_map/ppermute | solution.py:1217
  620.2 25.6 %collective-permute-start.35 = (bf16[256,2048]{1,0:T(8,128)(2,1)S(1)}, bf16[256,2048]{1,0:T(8,128)(2,1)S(1)}, u32[]{:S(2)}, u32[]{:S(2)}) collective-permute-start(bf16[256,2048]{1,0:T(8,128)(2,1)S(1)} %get-tuple-element.396), channel_id=1, source_target_pairs={{1,2},{2,1},{0,0},{3,3},{5,6},{6,5},{4,4},{7,7},{9,10},{10,9},{8,8... | collective-permute-start | bytes 3145736 | tf_op jit(solution)/shard_map/ppermute | solution.py:1218
  645.8 35.2 %collective-permute-start.38 = (bf16[1024,1664]{1,0:T(8,128)(2,1)S(1)}, bf16[1024,1664]{1,0:T(8,128)(2,1)S(1)}, u32[]{:S(2)}, u32[]{:S(2)}) collective-permute-start(bf16[1024,1664]{1,0:T(8,128)(2,1)S(1)} %get-tuple-element.258), channel_id=1, source_target_pairs={{0,4},{4,0},{8,12},{12,8},{16,20},{20,16},{24,28},{28,24},{1,5},{5... | collective-permute-start | bytes 10223624 | tf_op jit(solution)/shard_map/ppermute | solution.py:885
  653.3 25.6 %collective-permute-start.36 = (bf16[256,2048]{1,0:T(8,128)(2,1)S(1)}, bf16[256,2048]{1,0:T(8,128)(2,1)S(1)}, u32[]{:S(2)}, u32[]{:S(2)}) collective-permute-start(bf16[256,2048]{1,0:T(8,128)(2,1)S(1)} %broadcast_select_fusion.13), channel_id=1, source_target_pairs={{0,1},{1,0},{2,3},{3,2},{4,5},{5,4},{6,7},{7,6},{8,9},{9,8},{10,11... | collective-permute-start | bytes 3145736 | tf_op jit(solution)/shard_map/ppermute | solution.py:1217
  653.4 27.6 %collective-permute-start.37 = (bf16[256,2048]{1,0:T(8,128)(2,1)S(1)}, bf16[256,2048]{1,0:T(8,128)(2,1)S(1)}, u32[]{:S(2)}, u32[]{:S(2)}) collective-permute-start(bf16[256,2048]{1,0:T(8,128)(2,1)S(1)} %get-tuple-element.393), channel_id=1, source_target_pairs={{1,2},{2,1},{0,0},{3,3},{5,6},{6,5},{4,4},{7,7},{9,10},{10,9},{8,8... | collective-permute-start | bytes 3145736 | tf_op jit(solution)/shard_map/ppermute | solution.py:1218
  682.6 29.4 %collective-permute-start.39 = (bf16[256,2048]{1,0:T(8,128)(2,1)S(1)}, bf16[256,2048]{1,0:T(8,128)(2,1)S(1)}, u32[]{:S(2)}, u32[]{:S(2)}) collective-permute-start(bf16[256,2048]{1,0:T(8,128)(2,1)S(1)} %broadcast_select_fusion.9), channel_id=1, source_target_pairs={{0,1},{1,0},{2,3},{3,2},{4,5},{5,4},{6,7},{7,6},{8,9},{9,8},{10,11... | collective-permute-start | bytes 3145736 | tf_op jit(solution)/shard_map/ppermute | solution.py:1217
  684.5 27.5 %collective-permute-start.40 = (bf16[256,2048]{1,0:T(8,128)(2,1)S(1)}, bf16[256,2048]{1,0:T(8,128)(2,1)S(1)}, u32[]{:S(2)}, u32[]{:S(2)}) collective-permute-start(bf16[256,2048]{1,0:T(8,128)(2,1)S(1)} %get-tuple-element.390), channel_id=1, source_target_pairs={{1,2},{2,1},{0,0},{3,3},{5,6},{6,5},{4,4},{7,7},{9,10},{10,9},{8,8... | collective-permute-start | bytes 3145736 | tf_op jit(solution)/shard_map/ppermute | solution.py:1218
  689.1 21.9 %collective-permute-start.41 = (bf16[128,1664]{1,0:T(8,128)(2,1)S(1)}, bf16[128,1664]{1,0:T(8,128)(2,1)S(1)}, u32[]{:S(2)}, u32[]{:S(2)}) collective-permute-start(bf16[128,1664]{1,0:T(8,128)(2,1)S(1)} %get-tuple-element.416), channel_id=1, source_target_pairs={{0,8},{4,12},{8,0},{12,4},{16,24},{20,28},{24,16},{28,20},{1,9},{5... | collective-permute-start | bytes 1277960 | tf_op jit(solution)/shard_map/ppermute | solution.py:885
  690.2 21.8 %collective-permute-start.42 = (bf16[128,1664]{1,0:T(8,128)(2,1)S(1)}, bf16[128,1664]{1,0:T(8,128)(2,1)S(1)}, u32[]{:S(2)}, u32[]{:S(2)}) collective-permute-start(bf16[128,1664]{1,0:T(8,128)(2,1)S(1)} %get-tuple-element.415), channel_id=1, source_target_pairs={{0,16},{4,20},{8,24},{12,28},{16,0},{20,4},{24,8},{28,12},{1,17},{... | collective-permute-start | bytes 1277960 | tf_op jit(solution)/shard_map/ppermute | solution.py:885
  690.4 52.6 %collective-permute-start.46 = (bf16[256,2048]{1,0:T(8,128)(2,1)S(1)}, bf16[256,2048]{1,0:T(8,128)(2,1)S(1)}, u32[]{:S(2)}, u32[]{:S(2)}) collective-permute-start(bf16[256,2048]{1,0:T(8,128)(2,1)S(1)} %pad_maximum_fusion.10), channel_id=1, source_target_pairs={{0,8},{4,12},{8,0},{12,4},{16,24},{20,28},{24,16},{28,20},{1,9},{5... | collective-permute-start | bytes 3145736 | tf_op jit(solution)/shard_map/ppermute | solution.py:885
  710.9 32.1 %collective-permute-start.45 = (bf16[256,2048]{1,0:T(8,128)(2,1)S(1)}, bf16[256,2048]{1,0:T(8,128)(2,1)S(1)}, u32[]{:S(2)}, u32[]{:S(2)}) collective-permute-start(bf16[256,2048]{1,0:T(8,128)(2,1)S(1)} %pad_maximum_fusion.9), channel_id=1, source_target_pairs={{0,16},{4,20},{8,24},{12,28},{16,0},{20,4},{24,8},{28,12},{1,17},{... | collective-permute-start | bytes 3145736 | tf_op jit(solution)/shard_map/ppermute | solution.py:885
  718.7 24.3 %collective-permute-start.43 = (bf16[256,2048]{1,0:T(8,128)(2,1)S(1)}, bf16[256,2048]{1,0:T(8,128)(2,1)S(1)}, u32[]{:S(2)}, u32[]{:S(2)}) collective-permute-start(bf16[256,2048]{1,0:T(8,128)(2,1)S(1)} %get-tuple-element.389), channel_id=1, source_target_pairs={{0,1},{1,0},{2,3},{3,2},{4,5},{5,4},{6,7},{7,6},{8,9},{9,8},{10,11... | collective-permute-start | bytes 3145736 | tf_op jit(solution)/shard_map/ppermute | solution.py:1217
  718.8 25.1 %collective-permute-start.44 = (bf16[256,2048]{1,0:T(8,128)(2,1)S(1)}, bf16[256,2048]{1,0:T(8,128)(2,1)S(1)}, u32[]{:S(2)}, u32[]{:S(2)}) collective-permute-start(bf16[256,2048]{1,0:T(8,128)(2,1)S(1)} %get-tuple-element.389), channel_id=1, source_target_pairs={{1,2},{2,1},{0,0},{3,3},{5,6},{6,5},{4,4},{7,7},{9,10},{10,9},{8,8... | collective-permute-start | bytes 3145736 | tf_op jit(solution)/shard_map/ppermute | solution.py:1218
  721.4 39.3 %collective-permute-start.50 = (bf16[256,1664]{1,0:T(8,128)(2,1)S(1)}, bf16[256,1664]{1,0:T(8,128)(2,1)S(1)}, u32[]{:S(2)}, u32[]{:S(2)}) collective-permute-start(bf16[256,1664]{1,0:T(8,128)(2,1)S(1)} %pad_maximum_fusion.12), channel_id=1, source_target_pairs={{0,8},{4,12},{8,0},{12,4},{16,24},{20,28},{24,16},{28,20},{1,9},{5... | collective-permute-start | bytes 2555912 | tf_op jit(solution)/shard_map/ppermute | solution.py:885
  744.7 23.3 %collective-permute-start.47 = (bf16[256,2048]{1,0:T(8,128)(2,1)S(1)}, bf16[256,2048]{1,0:T(8,128)(2,1)S(1)}, u32[]{:S(2)}, u32[]{:S(2)}) collective-permute-start(bf16[256,2048]{1,0:T(8,128)(2,1)S(1)} %get-tuple-element.425), channel_id=1, source_target_pairs={{0,1},{1,0},{2,3},{3,2},{4,5},{5,4},{6,7},{7,6},{8,9},{9,8},{10,11... | collective-permute-start | bytes 3145736 | tf_op jit(solution)/shard_map/ppermute | solution.py:1217
  745.4 25.9 %collective-permute-start.48 = (bf16[256,2048]{1,0:T(8,128)(2,1)S(1)}, bf16[256,2048]{1,0:T(8,128)(2,1)}, u32[]{:S(2)}, u32[]{:S(2)}) collective-permute-start(bf16[256,2048]{1,0:T(8,128)(2,1)S(1)} %get-tuple-element.385), channel_id=1, source_target_pairs={{1,2},{2,1},{0,0},{3,3},{5,6},{6,5},{4,4},{7,7},{9,10},{10,9},{8,8... | collective-permute-start | bytes 3145736 | tf_op jit(solution)/shard_map/ppermute | solution.py:1218
  747.8 19.3 %collective-permute-start.49 = (bf16[256,1664]{1,0:T(8,128)(2,1)S(1)}, bf16[256,1664]{1,0:T(8,128)(2,1)S(1)}, u32[]{:S(2)}, u32[]{:S(2)}) collective-permute-start(bf16[256,1664]{1,0:T(8,128)(2,1)S(1)} %pad_maximum_fusion.11), channel_id=1, source_target_pairs={{0,16},{4,20},{8,24},{12,28},{16,0},{20,4},{24,8},{28,12},{1,17},{... | collective-permute-start | bytes 2555912 | tf_op jit(solution)/shard_map/ppermute | solution.py:885
  775.8 23.3 %collective-permute-start.53 = (bf16[256,640]{1,0:T(8,128)(2,1)S(1)}, bf16[256,640]{1,0:T(8,128)(2,1)}, u32[]{:S(2)}, u32[]{:S(2)}) collective-permute-start(bf16[256,640]{1,0:T(8,128)(2,1)S(1)} %get-tuple-element.452), channel_id=1, source_target_pairs={{0,1},{1,0},{2,3},{3,2},{4,5},{5,4},{6,7},{7,6},{8,9},{9,8},{10,11... | collective-permute-start | bytes 983048 | tf_op jit(solution)/shard_map/ppermute | solution.py:1195
  775.9 24.2 %collective-permute-start.54 = (bf16[256,640]{1,0:T(8,128)(2,1)S(1)}, bf16[256,640]{1,0:T(8,128)(2,1)}, u32[]{:S(2)}, u32[]{:S(2)}) collective-permute-start(bf16[256,640]{1,0:T(8,128)(2,1)S(1)} %get-tuple-element.453), channel_id=1, source_target_pairs={{0,2},{1,3},{2,0},{3,1},{4,6},{5,7},{6,4},{7,5},{8,10},{9,11},{10,... | collective-permute-start | bytes 983048 | tf_op jit(solution)/shard_map/ppermute | solution.py:1195
  777.6 30.9 %collective-permute-start.55 = (bf16[256,640]{1,0:T(8,128)(2,1)S(1)}, bf16[256,640]{1,0:T(8,128)(2,1)}, u32[]{:S(2)}, u32[]{:S(2)}) collective-permute-start(bf16[256,640]{1,0:T(8,128)(2,1)S(1)} %get-tuple-element.454), channel_id=1, source_target_pairs={{0,3},{1,2},{2,1},{3,0},{4,7},{5,6},{6,5},{7,4},{8,11},{9,10},{10,... | collective-permute-start | bytes 983048 | tf_op jit(solution)/shard_map/ppermute | solution.py:1195
  784.3 35.7 %collective-permute-start.51 = (bf16[256,2048]{1,0:T(8,128)(2,1)}, bf16[256,2048]{1,0:T(8,128)(2,1)}, u32[]{:S(2)}, u32[]{:S(2)}) collective-permute-start(bf16[256,2048]{1,0:T(8,128)(2,1)} %get-tuple-element.422), channel_id=1, source_target_pairs={{0,1},{1,0},{2,3},{3,2},{4,5},{5,4},{6,7},{7,6},{8,9},{9,8},{10,11... | collective-permute-start | bytes 3145736 | tf_op jit(solution)/shard_map/ppermute | solution.py:1217
  785.3 43.0 %collective-permute-start.52 = (bf16[256,2048]{1,0:T(8,128)(2,1)}, bf16[256,2048]{1,0:T(8,128)(2,1)}, u32[]{:S(2)}, u32[]{:S(2)}) collective-permute-start(bf16[256,2048]{1,0:T(8,128)(2,1)} %get-tuple-element.424), channel_id=1, source_target_pairs={{1,2},{2,1},{0,0},{3,3},{5,6},{6,5},{4,4},{7,7},{9,10},{10,9},{8,8... | collective-permute-start | bytes 3145736 | tf_op jit(solution)/shard_map/ppermute | solution.py:1218
  (84 other events, 466.6 us)
Sparse Core Ops, SparseCore 0:
  19.3 123.5 all-gather.6
  173.9 123.3 all-gather.4
  348.7 45.3 reduce-scatter.4
  402.3 45.4 reduce-scatter.6
  498.6 80.8 reduce-scatter.8
  582.7 149.3 reduce-scatter.10
